TPU v7x, 128 devices: a whole 4x4x4 slice. The times are simulated.
128 devices in a mesh: wide: 32 (over z, y, core), patch: 4 (over x).
Axes of the slice: x: 4, y: 4, z: 4, core: 2. Of those that a mesh axis runs over, the one named last changes fastest.
Arguments:
- grid_state: bfloat16 [84, 262144], P(None, ('wide', 'patch')), may hold values from -6 to 6
- cotangent: bfloat16 [84, 262144], P(None, ('wide', 'patch')), may hold values from -6 to 6
- encoder_weight: bfloat16 [84, 512], replicated, may hold values from -0.625 to 0.625
- norm_gain: bfloat16 [512], replicated, may hold values from 0.5 to 1.5
- query_weight: bfloat16 [512, 512], replicated
- key_weight: bfloat16 [512, 512], replicated
- value_weight: bfloat16 [512, 512], replicated, may hold values from -0.25 to 0.25
- output_weight: bfloat16 [512, 512], replicated, may hold values from -0.25 to 0.25
- decoder_weight: bfloat16 [512, 84], replicated, may hold values from -0.25 to 0.25
- grid_owner: int32 [262144], P(('wide', 'patch')), may hold values from 0 to 65535, as said below
- decode_node: int32 [262144], P(('wide', 'patch')), may hold values from 0 to 65535, as said below
- tile_pattern: int32 [512, 16], P(('wide', 'patch')), may hold values from 0 to 1, as said below
Outputs:
- denoised: bfloat16 [84, 262144], P(None, ('wide', 'patch'))
- state_grad: float32 [84, 262144], P(None, ('wide', 'patch'))
- encoder_grad: float32 [84, 512], replicated
Inputs may be any that keep to these rules, and one draw needn't show every extreme that they name: `grid_owner`: the node of every grid point lies on a device with the same patch index. At most 128 grid points of one device belong to the nodes of one device, and on every device one such pair holds exactly 128. `decode_node`: the node of every grid point lies on a device with the same patch index. At most 128 grid points of one device read the nodes of one device, and on every device one such pair holds exactly 128. `tile_pattern`: every query tile attends to its own tile: entry (t, ((t * 128 // 512) % 4) * 4 + t % 4) is 1.
All inputs are finite; a program needn't handle non-finite values.
Results may differ from a plain program's by a relative error of at most 0.008.
Values may be sent and summed in bfloat16 or wider, within the bound.
No kernel may reach another device: no remote copies, remote signals or barrier semaphores. Data moves between devices by JAX's collectives and lax.ppermute only.
A program may use at most 192 MiB of HBM per device.

v0:
```python
import math

import jax
import jax.numpy as jnp
from jax import lax
from jax.sharding import PartitionSpec as P

HEADS = 4
HEAD = 128
TILE = 128


HIGHEST = lax.Precision.HIGHEST


def route_slots(owners, peer_count, group_size, node_count, capacity):
    target = owners // (node_count * group_size)
    local = owners % node_count
    onehot = (target[:, None] == jnp.arange(peer_count, dtype=jnp.int32)[None, :]).astype(jnp.int32)
    before = jnp.cumsum(onehot, axis=0) - onehot
    within = jnp.sum(before * onehot, axis=1)
    return (target * capacity + within, local)


def pack_columns(columns, position, slot_total):
    empty = jnp.zeros((columns.shape[0], slot_total), columns.dtype)
    return empty.at[:, position].set(columns)


def pack_index(local, position, slot_total, filler):
    return jnp.full((slot_total,), filler, jnp.int32).at[position].set(local)


def node_sums(received, slots, node_count):
    selector = (jnp.arange(node_count, dtype=jnp.int32)[:, None] == slots[None, :]).astype(
        received.dtype
    )
    return lax.dot_general(
        selector, received, (((1,), (1,)), ((), ())), preferred_element_type=jnp.float32
    )


def attend(queries, keys, values, allowed, mixed_grad):
    query_rows = queries.shape[0]
    key_rows = keys.shape[0]
    scale = 1.0 / math.sqrt(HEAD)
    query_heads = queries.reshape(query_rows, HEADS, HEAD)
    key_heads = keys.reshape(key_rows, HEADS, HEAD)
    value_heads = values.reshape(key_rows, HEADS, HEAD)
    grad_heads = mixed_grad.reshape(query_rows, HEADS, HEAD)
    scores = (
        jnp.einsum("qhd,khd->hqk", query_heads, key_heads, preferred_element_type=jnp.float32)
        * scale
    )
    scores = jnp.where(allowed[None, :, :], scores, -1e30)
    highest = jnp.max(scores, axis=2, keepdims=True)
    weights = jnp.exp(scores - highest)
    total = jnp.sum(weights, axis=2, keepdims=True)
    probs = weights / total
    probs_bf = probs.astype(jnp.bfloat16)
    mixed = jnp.einsum("hqk,khd->qhd", probs_bf, value_heads, preferred_element_type=jnp.float32)
    mixed = mixed.astype(jnp.bfloat16).reshape(query_rows, HEADS * HEAD)
    prob_grad = jnp.einsum(
        "qhd,khd->hqk", grad_heads, value_heads, preferred_element_type=jnp.float32
    )
    delta = jnp.sum(probs * prob_grad, axis=2, keepdims=True)
    score_grad = (probs * (prob_grad - delta) * scale).astype(jnp.bfloat16)
    query_grad = jnp.einsum(
        "hqk,khd->qhd", score_grad, key_heads, preferred_element_type=jnp.float32
    )
    query_grad = query_grad.astype(jnp.bfloat16).reshape(query_rows, HEADS * HEAD)
    return (
        mixed,
        query_grad,
        highest[:, :, 0],
        total[:, :, 0],
        delta[:, :, 0],
        score_grad,
        probs_bf,
    )


def key_side(score_grad, probs_bf, queries, mixed_grad, key_rows):
    query_rows = queries.shape[0]
    query_heads = queries.reshape(query_rows, HEADS, HEAD)
    grad_heads = mixed_grad.reshape(query_rows, HEADS, HEAD)
    key_part = jnp.einsum(
        "hqk,qhd->khd", score_grad, query_heads, preferred_element_type=jnp.float32
    ).reshape(key_rows, HEADS * HEAD)
    value_part = jnp.einsum(
        "hqk,qhd->khd", probs_bf, grad_heads, preferred_element_type=jnp.float32
    ).reshape(key_rows, HEADS * HEAD)
    return (key_part, value_part)


def body(
    grid_state,
    cotangent,
    encoder_weight,
    norm_gain,
    query_weight,
    key_weight,
    value_weight,
    output_weight,
    decoder_weight,
    grid_owner,
    decode_node,
    tile_pattern,
):
    peer_count = lax.axis_size("wide")
    group_size = lax.axis_size("patch")
    variables = grid_state.shape[0]
    model_width = query_weight.shape[0]
    grid_count = grid_state.shape[1]
    node_count = tile_pattern.shape[0] * TILE
    capacity = 2 * grid_count // peer_count
    slot_total = peer_count * capacity
    owner_pos, owner_local = route_slots(grid_owner, peer_count, group_size, node_count, capacity)
    decode_pos, decode_local = route_slots(
        decode_node, peer_count, group_size, node_count, capacity
    )
    state_send = pack_columns(grid_state, owner_pos, slot_total).reshape(
        variables, peer_count, capacity
    )
    cot_send = pack_columns(cotangent, decode_pos, slot_total).reshape(
        variables, peer_count, capacity
    )
    index_send = jnp.stack(
        [
            pack_index(owner_local, owner_pos, slot_total, node_count),
            pack_index(decode_local, decode_pos, slot_total, node_count),
        ]
    ).reshape(2, peer_count, capacity)
    state_recv, cot_recv, index_recv = (
        lax.all_to_all(state_send, "wide", split_axis=1, concat_axis=1, tiled=True),
        lax.all_to_all(cot_send, "wide", split_axis=1, concat_axis=1, tiled=True),
        lax.all_to_all(index_send, "wide", split_axis=1, concat_axis=1, tiled=True),
    )
    owner_slots = index_recv[0].reshape(slot_total)
    decode_slots = index_recv[1].reshape(slot_total)
    state_sum = node_sums(state_recv.reshape(variables, slot_total), owner_slots, node_count)
    cot_sum = node_sums(cot_recv.reshape(variables, slot_total), decode_slots, node_count)
    encoder_full = encoder_weight.astype(jnp.float32)
    start_rows = jnp.dot(state_sum, encoder_full, precision=HIGHEST)
    inverse_rms = lax.rsqrt(jnp.mean(start_rows * start_rows, axis=1, keepdims=True) + 1e-05)
    gain_full = norm_gain.astype(jnp.float32)
    normed = (start_rows * inverse_rms * gain_full).astype(jnp.bfloat16)
    queries = jnp.dot(normed, query_weight, preferred_element_type=jnp.float32).astype(jnp.bfloat16)
    keys_local = jnp.dot(normed, key_weight, preferred_element_type=jnp.float32).astype(
        jnp.bfloat16
    )
    values_local = jnp.dot(normed, value_weight, preferred_element_type=jnp.float32).astype(
        jnp.bfloat16
    )
    top_grad = jnp.dot(cot_sum, decoder_weight.astype(jnp.float32).T, precision=HIGHEST)
    top_grad_bf = top_grad.astype(jnp.bfloat16)
    mixed_grad = jnp.dot(top_grad_bf, output_weight.T, preferred_element_type=jnp.float32).astype(
        jnp.bfloat16
    )
    keys_all, values_all = (
        lax.all_gather(keys_local, "patch", axis=0, tiled=True),
        lax.all_gather(values_local, "patch", axis=0, tiled=True),
    )
    allowed = jnp.repeat(jnp.repeat(tile_pattern > 0, TILE, axis=0), TILE, axis=1)
    mixed, query_grad, highest, total, delta, score_grad, probs_bf = attend(
        queries, keys_all, values_all, allowed, mixed_grad
    )
    final_rows = start_rows + jnp.dot(mixed, output_weight, preferred_element_type=jnp.float32)
    final_bf = final_rows.astype(jnp.bfloat16)
    decode_clip = jnp.minimum(decode_slots, node_count - 1)
    owner_clip = jnp.minimum(owner_slots, node_count - 1)
    decoded_send = jnp.take(final_bf, decode_clip, axis=0).reshape(
        peer_count, capacity, model_width
    )
    decoded_back = lax.all_to_all(decoded_send, "wide", split_axis=0, concat_axis=0, tiled=True)
    key_part, value_part = key_side(score_grad, probs_bf, queries, mixed_grad, keys_all.shape[0])
    key_grad, value_grad = (
        lax.psum_scatter(
            key_part.astype(jnp.bfloat16), "patch", scatter_dimension=0, tiled=True
        ).astype(jnp.float32),
        lax.psum_scatter(
            value_part.astype(jnp.bfloat16), "patch", scatter_dimension=0, tiled=True
        ).astype(jnp.float32),
    )
    normed_grad = jnp.dot(query_grad, query_weight.T, preferred_element_type=jnp.float32)
    normed_grad = normed_grad + jnp.dot(
        key_grad.astype(jnp.bfloat16), key_weight.T, preferred_element_type=jnp.float32
    )
    normed_grad = normed_grad + jnp.dot(
        value_grad.astype(jnp.bfloat16), value_weight.T, preferred_element_type=jnp.float32
    )
    scaled_grad = normed_grad * gain_full
    start_grad = (
        top_grad
        + inverse_rms * scaled_grad
        - start_rows * inverse_rms**3 * jnp.mean(start_rows * scaled_grad, axis=1, keepdims=True)
    )
    encoder_grad = lax.psum(jnp.dot(state_sum.T, start_grad, precision=HIGHEST), ("wide", "patch"))
    grad_send = jnp.take(start_grad, owner_clip, axis=0).reshape(peer_count, capacity, model_width)
    grad_back = lax.all_to_all(
        grad_send.astype(jnp.bfloat16), "wide", split_axis=0, concat_axis=0, tiled=True
    ).astype(grad_send.dtype)
    picked = jnp.take(decoded_back.reshape(slot_total, model_width), decode_pos, axis=0)
    denoised = lax.dot_general(
        decoder_weight, picked, (((0,), (1,)), ((), ())), preferred_element_type=jnp.float32
    )
    grad_rows = jnp.take(grad_back.reshape(slot_total, model_width), owner_pos, axis=0)
    state_grad = lax.dot_general(
        encoder_full, grad_rows, (((1,), (1,)), ((), ())), precision=HIGHEST
    )
    return (denoised.astype(jnp.bfloat16), state_grad, encoder_grad)


def solution(mesh):
    in_specs = (
        P(None, ("wide", "patch")),
        P(None, ("wide", "patch")),
        P(),
        P(),
        P(),
        P(),
        P(),
        P(),
        P(),
        P(("wide", "patch")),
        P(("wide", "patch")),
        P(("wide", "patch"), None),
    )
    out_specs = (P(None, ("wide", "patch")), P(None, ("wide", "patch")), P())
    return jax.shard_map(body, mesh=mesh, in_specs=in_specs, out_specs=out_specs, check_vma=False)
```

profile of v0, /device:TPU:1, one launch (start us, length us, event | category | flops | bytes accessed | tf_op | source)
XLA Modules:
  0.0 477.2 jit_solution(5449545339493520804)
XLA Ops:
  7.2 0.8 add_select_fusion.1
  8.0 9.1 %reduce-window.16 = s32[32,16,128]{2,1,0:T(8,128)S(1)} reduce-window(s32[32,16,128]{2,1,0:T(8,128)S(1)} %fusion.69, s32[]{:T(128)} %constant.106.clone.1), window={size=1x1x128 pad=0_0x0_0x127_0}, to_apply=%region_3.4 | reduce-window | flops 8323072 | bytes 524292 | tf_op jit(solution)/shard_map/reduce-window.2
  17.2 0.2 copy.89
  17.9 1.3 compare_and_fusion.2
  19.2 0.7 add_select_fusion
  20.0 9.1 %reduce-window.14 = s32[32,16,128]{2,1,0:T(8,128)S(1)} reduce-window(s32[32,16,128]{2,1,0:T(8,128)S(1)} %fusion.68, s32[]{:T(128)} %constant.106.clone.1), window={size=1x1x128 pad=0_0x0_0x127_0}, to_apply=%region_0.1 | reduce-window | flops 8323072 | bytes 524292 | tf_op jit(solution)/shard_map/reduce-window
  29.2 0.2 copy.88
  29.9 0.6 compare_and_fusion.3
  30.5 8.1 %scatter_custom_fusion.1 = s32[4096]{0:T(1024)S(1)} fusion(s32[2048]{0:T(1024)S(1)} %get-tuple-element.8, s32[2048]{0:T(1024)S(1)} %get-tuple-element.14, s32[]{:T(128)} %constant.113.clone.1), kind=kCustom, calls=%fused_computation.117 | custom fusion | bytes 16388 | tf_op jit(solution)/shard_map/scatter | solution.py:31
  38.6 8.1 %scatter_custom_fusion = s32[4096]{0:T(1024)S(1)} fusion(s32[2048]{0:T(1024)S(1)} %get-tuple-element.4, s32[2048]{0:T(1024)S(1)} %get-tuple-element.11, s32[]{:T(128)} %constant.113.clone.1), kind=kCustom, calls=%fused_computation.119 | custom fusion | bytes 16388 | tf_op jit(solution)/shard_map/scatter | solution.py:31
  46.6 0.6 pad_add_fusion
  47.3 9.6 %all-to-all-start = ((s32[2,32,128]{2,0,1:T(2,128)}), s32[2,32,128]{2,0,1:T(2,128)S(1)}, u32[]{:S(2)}, u32[]{:S(2)}) async-start(s32[2,32,128]{2,0,1:T(2,128)} %pad_add_fusion), calls=%async_computation | async-start | bytes 65536 | tf_op jit(solution)/shard_map/all_to_all | solution.py:137
  56.9 0.3 copy.68
  57.2 6.1 %scatter_custom_fusion.2 = bf16[84,4096]{0,1:T(8,128)(2,1)S(1)} fusion(s32[2048]{0:T(1024)S(1)} %get-tuple-element.4, bf16[2048,84]{1,0:T(8,128)(2,1)S(1)} %copy.68, bf16[]{:T(256)} %constant.115.clone.1), kind=kCustom, calls=%fused_computation.72 | custom fusion | bytes 688130 | tf_op jit(solution)/shard_map/scatter | solution.py:27
  63.3 1.3 copy.69
  64.6 7.4 %all-to-all-start.1 = ((bf16[84,32,128]{2,0,1:T(8,128)(2,1)}), bf16[84,32,128]{2,0,1:T(8,128)(2,1)S(1)}, u32[]{:S(2)}, u32[]{:S(2)}) async-start(bf16[84,32,128]{2,0,1:T(8,128)(2,1)} %copy.69), calls=%async_computation.1 | async-start | bytes 1441792 | tf_op jit(solution)/shard_map/all_to_all | solution.py:135
  72.1 13.5 %all-to-all-done.1 = bf16[84,32,128]{2,0,1:T(8,128)(2,1)S(1)} async-done(((bf16[84,32,128]{2,0,1:T(8,128)(2,1)}), bf16[84,32,128]{2,0,1:T(8,128)(2,1)S(1)}, u32[]{:S(2)}, u32[]{:S(2)}) %all-to-all-start.1) | async-done | bytes 688160 | tf_op jit(solution)/shard_map/all_to_all | solution.py:135
  85.7 0.3 copy.95
  86.0 1.6 fusion.9
  87.7 0.6 multiply_reduce_fusion.2
  88.5 1.2 convolution_convert_fusion.2
  89.9 1.2 convolution_convert_fusion.4
  91.1 1.3 copy.77
  92.4 6.2 %scatter_custom_fusion.3 = bf16[84,4096]{0,1:T(8,128)(2,1)S(1)} fusion(s32[2048]{0:T(1024)S(1)} %get-tuple-element.8, bf16[2048,84]{1,0:T(8,128)(2,1)S(1)} %copy.77, bf16[]{:T(256)} %constant.115.clone.1), kind=kCustom, calls=%fused_computation.70 | custom fusion | bytes 688130 | tf_op jit(solution)/shard_map/scatter | solution.py:27
  98.7 1.3 copy.78
  100.0 4.1 all-to-all-start.3
  104.2 3.5 broadcast_in_dim.86
  107.7 1.6 copy.111
  109.3 8.5 %all-to-all-done.3 = bf16[84,32,128]{2,0,1:T(8,128)(2,1)S(1)} async-done(((bf16[84,32,128]{2,0,1:T(8,128)(2,1)}), bf16[84,32,128]{2,0,1:T(8,128)(2,1)S(1)}, u32[]{:S(2)}, u32[]{:S(2)}) %all-to-all-start.3) | async-done | bytes 688160 | tf_op jit(solution)/shard_map/all_to_all | solution.py:136
  118.0 0.3 copy.97
  118.3 1.6 fusion.10
  120.0 0.6 fusion.90
  120.6 1.3 convolution_convert_fusion.3
  121.9 0.5 convolution_convert_fusion.1
  122.4 4.0 copy.91
  126.4 11.5 %fusion.89 = (f32[4,512]{1,0:T(4,128)S(1)}, f32[4,512,2048]{2,1,0:T(8,128)}) fusion(pred[512,2048]{1,0:T(8,128)(4,1)} %bitcast.161, bf16[512,4,128]{0,2,1:T(8,128)(2,1)} %bitcast.166, bf16[2048,4,128]{0,2,1:T(8,128)(2,1)} %bitcast.157), kind=kOutput, calls=%fused_computation.144 | convolution fusion | flops 1090521088 | bytes 20455424 | tf_op jit(solution)/shard_map/sub | solution.py:57
  137.9 12.9 %all-gather.3.cloned.1.call-done = bf16[2048,512]{1,0:T(8,128)(2,1)} async-done(((bf16[512,512]{1,0:T(8,128)(2,1)}), bf16[2048,512]{1,0:T(8,128)(2,1)}) %all-gather.3.cloned.1.call-update) | async-done | bytes 2097168 | tf_op jit(solution)/shard_map/all_gather | solution.py:162
  150.8 9.7 %fusion.36 = f32[4,512,2048]{2,1,0:T(8,128)} fusion(bf16[512,4,128]{0,2,1:T(8,128)(2,1)S(1)} %bitcast.153, bf16[2048,512]{1,0:T(8,128)(2,1)} %all-gather.3.cloned.1.call-done), kind=kOutput, calls=%fused_computation.44 | convolution fusion | flops 1073741824 | bytes 19398656 | tf_op jit(solution)/shard_map/qhd,khd->hqk/dot_general | solution.py:63
  160.5 24.8 %fusion.25 = bf16[4,128,2048]{2,1,0:T(8,128)(2,1)} fusion(bf16[512,4,128]{0,2,1:T(8,128)(2,1)} %bitcast.167, f32[4,512,2048]{2,1,0:T(8,128)} %fusion.36, f32[4,512,2048]{2,1,0:T(8,128)} %get-tuple-element.22, f32[4,512]{1,0:T(4,128)S(1)} %get-tuple-element.21), kind=kOutput, calls=%fused_computation.38 | convolution fusion | flops 1104154624 | bytes 36184064 | tf_op jit(solution)/shard_map/hqk,qhd->khd/dot_general | solution.py:87
  185.4 8.5 %fusion.28 = bf16[4,128,2048]{2,1,0:T(8,128)(2,1)} fusion(bf16[512,4,128]{0,2,1:T(8,128)(2,1)S(1)} %bitcast.154, f32[4,512,2048]{2,1,0:T(8,128)} %get-tuple-element.22, f32[4,512]{1,0:T(4,128)S(1)} %get-tuple-element.21), kind=kOutput, calls=%fused_computation.39 | convolution fusion | flops 1083179008 | bytes 19406848 | tf_op jit(solution)/shard_map/hqk,qhd->khd/dot_general | solution.py:90
  193.9 9.8 %fusion.47 = bf16[4,128,512]{2,1,0:T(8,128)(2,1)S(1)} fusion(f32[4,512,2048]{2,1,0:T(8,128)} %get-tuple-element.22, f32[4,512]{1,0:T(4,128)S(1)} %get-tuple-element.21, bf16[2048,512]{1,0:T(8,128)(2,1)} %all-gather.3.cloned.1.call-done), kind=kOutput, calls=%fused_computation.57 | convolution fusion | flops 1082392576 | bytes 19406848 | tf_op jit(solution)/shard_map/hqk,khd->qhd/dot_general | solution.py:61
  203.6 1.3 fusion.55
  204.9 1.3 copy.75
  206.2 17.3 %gather_fusion = bf16[4096,512]{1,0:T(8,128)(2,1)} fusion(bf16[512,512]{1,0:T(8,128)(2,1)S(1)} %copy.75, s32[4096]{0:T(1024)S(1)} %broadcast_clamp_fusion.1), kind=kCustom, calls=%fused_computation | custom fusion | bytes 8404992 | tf_op jit(solution)/shard_map/jit(_take)/gather | solution.py:172
  223.5 3.9 broadcast_select_fusion
  227.4 8.1 %all-to-all-start.2 = ((bf16[32,128,512]{2,1,0:T(8,128)(2,1)}), bf16[32,128,512]{2,1,0:T(8,128)(2,1)}, u32[]{:S(2)}, u32[]{:S(2)}) async-start(bf16[32,128,512]{2,1,0:T(8,128)(2,1)} %broadcast_select_fusion), calls=%async_computation.2 | async-start | bytes 8388608 | tf_op jit(solution)/shard_map/all_to_all | solution.py:175
  235.6 1.3 copy.83
  237.0 23.5 %fusion.52 = bf16[4,128,512]{2,1,0:T(8,128)(2,1)S(1)} fusion(bf16[2048,4,128]{0,2,1:T(8,128)(2,1)} %bitcast.158, f32[4,512,2048]{2,1,0:T(8,128)} %fusion.36, f32[4,512,2048]{2,1,0:T(8,128)} %get-tuple-element.22, f32[4,512]{1,0:T(4,128)S(1)} %get-tuple-element.21), kind=kOutput, calls=%fused_computation.58 | convolution fusion | flops 1103368192 | bytes 36184064 | tf_op jit(solution)/shard_map/hqk,khd->qhd/dot_general | solution.py:68
  260.5 1.4 fusion.92
  261.9 1.8 convolution_add_fusion.1
  263.8 1.6 multiply_reduce_fusion.1
  265.4 0.4 multiply_subtract_fusion
  266.0 17.3 %gather_fusion.2 = bf16[4096,512]{1,0:T(8,128)(2,1)} fusion(bf16[512,512]{1,0:T(8,128)(2,1)S(1)} %copy.84, s32[4096]{0:T(1024)S(1)} %broadcast_clamp_fusion), kind=kCustom, calls=%fused_computation.2 | custom fusion | bytes 8404992 | tf_op jit(solution)/shard_map/jit(_take)/gather | solution.py:199
  283.3 4.0 select_convert_fusion
  287.4 7.5 %all-to-all-start.4 = ((bf16[32,128,512]{2,1,0:T(8,128)(2,1)}), bf16[32,128,512]{2,1,0:T(8,128)(2,1)}, u32[]{:S(2)}, u32[]{:S(2)}) async-start(bf16[32,128,512]{2,1,0:T(8,128)(2,1)} %select_convert_fusion), calls=%async_computation.6 | async-start | bytes 8388608 | tf_op jit(solution)/shard_map/all_to_all | solution.py:200
  294.9 12.0 %gather_fusion.1 = bf16[2048,512]{1,0:T(8,128)(2,1)} fusion(bf16[4096,512]{1,0:T(8,128)(2,1)} %bitcast.21, s32[2048]{0:T(1024)S(1)} %broadcast_clamp_fusion.3), kind=kCustom, calls=%fused_computation.1 | custom fusion | bytes 4202496 | tf_op jit(solution)/shard_map/jit(_take)/gather | solution.py:203
  306.9 3.2 fusion.34
  310.1 1.8 fusion.91
  311.9 33.2 %all-to-all-done.4 = bf16[32,128,512]{2,1,0:T(8,128)(2,1)} async-done(((bf16[32,128,512]{2,1,0:T(8,128)(2,1)}), bf16[32,128,512]{2,1,0:T(8,128)(2,1)}, u32[]{:S(2)}, u32[]{:S(2)}) %all-to-all-start.4) | async-done | bytes 4194336 | tf_op jit(solution)/shard_map/all_to_all | solution.py:200
  345.1 6.6 %bitcast_convert_fusion = f32[4096,512]{1,0:T(8,128)} fusion(bf16[32,128,512]{2,1,0:T(8,128)(2,1)} %all-to-all-done.4), kind=kLoop, calls=%fused_computation.27 | loop fusion | flops 2097152 | bytes 12582912 | tf_op jit(solution)/shard_map/reshape | solution.py:207
  351.7 13.0 %gather_fusion.3 = f32[2048,512]{1,0:T(8,128)} fusion(f32[4096,512]{1,0:T(8,128)} %bitcast_convert_fusion, s32[2048]{0:T(1024)S(1)} %broadcast_clamp_fusion.2), kind=kCustom, calls=%fused_computation.3 | custom fusion | bytes 8396800 | tf_op jit(solution)/shard_map/jit(_take)/gather | solution.py:207
  364.7 5.6 %fusion.31 = f32[84,2048]{1,0:T(8,128)} fusion(bf16[84,512]{1,0:T(8,128)(2,1)S(1)} %copy-done.12, f32[2048,512]{1,0:T(8,128)} %gather_fusion.3, pred[2048]{0:T(1024)(128)(4,1)S(1)} %copy-done.15), kind=kOutput, calls=%fused_computation.40 | convolution fusion | flops 1058013184 | bytes 4970496 | tf_op jit(solution)/shard_map/dot_general | solution.py:208
  370.3 98.3 %all-reduce.2.cloned.1.call-done = f32[84,512]{1,0:T(8,128)} async-done(((f32[84,512]{1,0:T(8,128)}), f32[84,512]{1,0:T(8,128)}) %all-reduce.2.cloned.1.call-update) | async-done | bytes 172048 | tf_op jit(solution)/shard_map/psum | solution.py:198
  468.6 1.6 copy.113
  (85 shorter events, 2.5 us)
Async XLA Ops:
  7.2 82.7 %copy-start = (bf16[512,512]{1,0:T(8,128)(2,1)S(1)}, bf16[512,512]{1,0:T(8,128)(2,1)}, u32[]{:S(2)}) copy-start(bf16[512,512]{1,0:T(8,128)(2,1)} %param.18) | copy-start | bytes 1572868
  7.2 22.7 %copy-start.14 = (s32[2048]{0:T(1024)S(1)}, s32[2048]{0:T(1024)}, u32[]{:S(2)}) copy-start(s32[2048]{0:T(1024)} %param.22) | copy-start | bytes 24580
  7.2 49.7 %copy-start.10 = (bf16[84,2048]{1,0:T(8,128)(2,1)S(1)}, bf16[84,2048]{1,0:T(8,128)(2,1)}, u32[]{:S(2)}) copy-start(bf16[84,2048]{1,0:T(8,128)(2,1)} %param.12) | copy-start | bytes 1032196
  17.8 54.2 %copy-start.18 = (bf16[512]{0:T(512)(128)(2,1)S(1)}, bf16[512]{0:T(512)(128)(2,1)}, u32[]{:S(2)}) copy-start(bf16[512]{0:T(512)(128)(2,1)} %param.15) | copy-start | bytes 3076
  47.3 17.3 %all-to-all-start = ((s32[2,32,128]{2,0,1:T(2,128)}), s32[2,32,128]{2,0,1:T(2,128)S(1)}, u32[]{:S(2)}, u32[]{:S(2)}) async-start(s32[2,32,128]{2,0,1:T(2,128)} %pad_add_fusion), calls=%async_computation | async-start | bytes 65536 | tf_op jit(solution)/shard_map/all_to_all | solution.py:137
  64.6 21.0 %all-to-all-start.1 = ((bf16[84,32,128]{2,0,1:T(8,128)(2,1)}), bf16[84,32,128]{2,0,1:T(8,128)(2,1)S(1)}, u32[]{:S(2)}, u32[]{:S(2)}) async-start(bf16[84,32,128]{2,0,1:T(8,128)(2,1)} %copy.69), calls=%async_computation.1 | async-start | bytes 1441792 | tf_op jit(solution)/shard_map/all_to_all | solution.py:135
  72.0 50.4 %all-gather.5.cloned.1.call-start = ((), (), s32[]{:S(2)}) async-start(), calls=%async_computation.8 | async-start | bytes 2621440 | tf_op jit(solution)/shard_map/all_gather | solution.py:161
  85.7 2.0 copy-start.11
  86.0 2.5 copy-start.8
  88.5 2.6 copy-start.2
  89.8 14.4 %copy-start.16 = (s32[4,16]{1,0:T(4,128)S(1)}, s32[4,16]{1,0:T(4,128)}, u32[]{:S(2)}) copy-start(s32[4,16]{1,0:T(4,128)} %param.23) | copy-start | bytes 772
  89.8 61.0 %all-gather.3.cloned.1.call-start = ((), (), s32[]{:S(2)}) async-start(), calls=%async_computation.7 | async-start | bytes 2621440 | tf_op jit(solution)/shard_map/all_gather | solution.py:162
  100.0 17.8 %all-to-all-start.3 = ((bf16[84,32,128]{2,0,1:T(8,128)(2,1)}), bf16[84,32,128]{2,0,1:T(8,128)(2,1)S(1)}, u32[]{:S(2)}, u32[]{:S(2)}) async-start(bf16[84,32,128]{2,0,1:T(8,128)(2,1)} %copy.78), calls=%async_computation.3 | async-start | bytes 1441792 | tf_op jit(solution)/shard_map/all_to_all | solution.py:136
  104.1 157.8 %reduce-scatter.3.cloned.1.call-start = ((), (), s32[]{:S(2)}) async-start(), calls=%async_computation.9 | async-start | bytes 2621440 | tf_op jit(solution)/shard_map/reduce_scatter | solution.py:178
  117.9 2.0 copy-start.13
  118.0 2.6 copy-start.3
  118.0 2.6 copy-start.6
  118.3 3.6 copy-start.4
  185.3 78.5 %reduce-scatter.5.cloned.1.call-start = ((), (), s32[]{:S(2)}) async-start(), calls=%async_computation.10 | async-start | bytes 2621440 | tf_op jit(solution)/shard_map/reduce_scatter | solution.py:181
  193.9 9.8 %copy-start.5 = (bf16[512,512]{1,0:T(8,128)(2,1)S(1)}, bf16[512,512]{1,0:T(8,128)(2,1)}, u32[]{:S(2)}) copy-start(bf16[512,512]{1,0:T(8,128)(2,1)} %param.19) | copy-start | bytes 1572868
  227.4 60.0 %all-to-all-start.2 = ((bf16[32,128,512]{2,1,0:T(8,128)(2,1)}), bf16[32,128,512]{2,1,0:T(8,128)(2,1)}, u32[]{:S(2)}, u32[]{:S(2)}) async-start(bf16[32,128,512]{2,1,0:T(8,128)(2,1)} %broadcast_select_fusion), calls=%async_computation.2 | async-start | bytes 8388608 | tf_op jit(solution)/shard_map/all_to_all | solution.py:175
  237.0 23.5 %copy-start.7 = (bf16[512,512]{1,0:T(8,128)(2,1)S(1)}, bf16[512,512]{1,0:T(8,128)(2,1)}, u32[]{:S(2)}) copy-start(bf16[512,512]{1,0:T(8,128)(2,1)} %param.16) | copy-start | bytes 1572868
  237.0 25.0 %copy-start.9 = (bf16[512,512]{1,0:T(8,128)(2,1)S(1)}, bf16[512,512]{1,0:T(8,128)(2,1)}, u32[]{:S(2)}) copy-start(bf16[512,512]{1,0:T(8,128)(2,1)} %param.17) | copy-start | bytes 1572868
  263.8 1.6 copy-start.1
  287.4 57.7 %all-to-all-start.4 = ((bf16[32,128,512]{2,1,0:T(8,128)(2,1)}), bf16[32,128,512]{2,1,0:T(8,128)(2,1)}, u32[]{:S(2)}, u32[]{:S(2)}) async-start(bf16[32,128,512]{2,1,0:T(8,128)(2,1)} %select_convert_fusion), calls=%async_computation.6 | async-start | bytes 8388608 | tf_op jit(solution)/shard_map/all_to_all | solution.py:200
  294.9 173.7 %all-reduce.2.cloned.1.call-start = ((), (), s32[]{:S(2)}) async-start(), calls=%async_computation.11 | async-start | bytes 360448 | tf_op jit(solution)/shard_map/psum | solution.py:198
  294.9 12.0 %copy-start.17 = (pred[2048]{0:T(1024)(128)(4,1)S(1)}, pred[2048]{0:T(1024)(128)(4,1)}, u32[]{:S(2)}) copy-start(pred[2048]{0:T(1024)(128)(4,1)} %get-tuple-element.7) | copy-start | bytes 6148
  351.7 13.0 %copy-start.12 = (bf16[84,512]{1,0:T(8,128)(2,1)S(1)}, bf16[84,512]{1,0:T(8,128)(2,1)}, u32[]{:S(2)}) copy-start(bf16[84,512]{1,0:T(8,128)(2,1)} %param.14) | copy-start | bytes 258052
  351.7 13.0 %copy-start.15 = (pred[2048]{0:T(1024)(128)(4,1)S(1)}, pred[2048]{0:T(1024)(128)(4,1)}, u32[]{:S(2)}) copy-start(pred[2048]{0:T(1024)(128)(4,1)} %get-tuple-element.3) | copy-start | bytes 6148
Sparse Core Ops, SparseCore 0:
  89.9 28.2 all-gather.4
  119.9 30.8 all-gather.2
  185.4 29.7 reduce-scatter.2
  217.5 29.3 reduce-scatter.4
  312.0 156.5 all-reduce.1
where the time goes:
time: 486 us; the launch traced here: 477 us
  waiting for transfers between devices  166 us (34%)
  matrix products  113 us (23%)
  local copies, waits for them, and re-layouts  107 us (22%)
  other arithmetic  38.3 us (8%)
  starting transfers between devices  36.9 us (8%)
  between operations  14.9 us (3%)
    psum x1, waiting for transfers between devices, body(): lax.psum(jnp.dot(state_sum.T, start_grad, precision=HIGHEST), ('wide', 'p...  98.3 us
    all_to_all x1, waiting for transfers between devices, body(): lax.all_to_all(grad_send.astype(jnp.bfloat16), 'wide', split_axis=0, conc...  33.2 us
    dot_general x1, matrix products, key_side(): jnp.einsum('hqk,qhd->khd', score_grad, query_heads, preferred_element_typ...  24.8 us
    dot_general x1, matrix products, attend(): jnp.einsum('hqk,khd->qhd', score_grad, key_heads, preferred_element_type=...  23.5 us
    another operation x6, other arithmetic  18.8 us
    gather x1, local copies, waits for them, and re-layouts, body(): jnp.take(start_grad, owner_clip, axis=0)  17.3 us
    gather x1, local copies, waits for them, and re-layouts, body(): jnp.take(final_bf, decode_clip, axis=0)  17.3 us
    scatter x2, local copies, waits for them, and re-layouts, pack_index(): return jnp.full((slot_total,), filler, jnp.int32).at[position].set(local)  16.1 us
  transfers between devices with their start and end apart: 10, of which 5 were waited for; matrix products, arithmetic and copies ran while one was open for 37% of the time, Pallas kernels for 0%

commit v1 on v0

v1 whole, which is shorter than its diff:
```python
import functools
import math

import jax
import jax.numpy as jnp
from jax import lax
from jax.experimental import pallas as pl
from jax.experimental.pallas import tpu as pltpu
from jax.sharding import PartitionSpec as P

HEADS = 4
HEAD = 128
TILE = 128
ROWS = 88
F32 = jnp.float32
BF16 = jnp.bfloat16
MIB = 1024 * 1024


def dot(a, b):
    return jnp.dot(a, b, preferred_element_type=F32)


def dot_nt(a, b):
    return lax.dot_general(a, b, (((1,), (1,)), ((), ())), preferred_element_type=F32)


def split(x):
    high = x.astype(BF16)
    return high, (x - high.astype(F32)).astype(BF16)


def call(kernel, outs, scratch, name, flops, *args, smem=()):
    specs = [
        pl.BlockSpec(memory_space=pltpu.SMEM if i in smem else pltpu.VMEM) for i in range(len(args))
    ]
    return pl.pallas_call(
        kernel,
        out_shape=[jax.ShapeDtypeStruct(s, d) for s, d in outs],
        in_specs=specs,
        out_specs=[pl.BlockSpec(memory_space=pltpu.VMEM) for _ in outs],
        scratch_shapes=scratch,
        compiler_params=pltpu.CompilerParams(vmem_limit_bytes=56 * MIB),
        cost_estimate=pl.CostEstimate(flops=flops, bytes_accessed=1 << 20, transcendentals=0),
        name=name,
    )(*args)


def slot_onehot(rank_ref, pair):
    grid_count = rank_ref.shape[1]
    level = lax.broadcasted_iota(jnp.int32, (TILE, grid_count), 0).astype(F32).astype(BF16)
    parts = []
    for k in range(2):
        row = rank_ref[pl.ds(2 * pair + k, 1), :].astype(BF16)
        parts.append(jnp.where(level == row, jnp.ones((), BF16), jnp.zeros((), BF16)))
    return jnp.concatenate(parts, axis=0)


def pack_kernel(
    shift, x_ref, c_ref, own_ref, dec_ref, out_ref, own_rank, dec_rank, wide_s, pay_o, pay_d
):
    variables, grid_count = x_ref.shape
    peers = out_ref.shape[0]
    node_mask = 511
    chunk = 256
    upper = jnp.where(
        lax.broadcasted_iota(jnp.int32, (chunk, chunk), 0)
        < lax.broadcasted_iota(jnp.int32, (chunk, chunk), 1),
        1.0,
        0.0,
    ).astype(BF16)
    for data, index, rank, pay in (
        (x_ref, own_ref, own_rank, pay_o),
        (c_ref, dec_ref, dec_rank, pay_d),
    ):
        carry = jnp.zeros((peers, 1), F32)
        for start in range(0, grid_count, chunk):
            span = pl.ds(start, chunk)
            nodes = index[:, span]
            hit = lax.broadcasted_iota(jnp.int32, (peers, chunk), 0) == (nodes >> shift)
            ones = jnp.where(hit, 1.0, 0.0)
            before = dot(ones.astype(BF16), upper) + carry
            rank[:, span] = jnp.where(hit, before, -1.0)
            carry = carry + jnp.sum(ones, axis=1, keepdims=True)
        local = index[...] & node_mask
        wide_s[0:variables, :] = data[...].astype(F32)
        wide_s[variables : variables + 1, :] = (local >> 1).astype(F32)
        wide_s[variables + 1 : variables + 2, :] = (local & 1).astype(F32)
        wide_s[variables + 2 : ROWS, :] = jnp.zeros((ROWS - variables - 2, grid_count), F32)
        pay[...] = wide_s[...].astype(BF16)

    def step(pair, _):
        for k, rank, pay in ((0, own_rank, pay_o), (1, dec_rank, pay_d)):
            got = dot_nt(pay[...], slot_onehot(rank, pair)).astype(BF16)
            out_ref[2 * pair, pl.ds(k * ROWS, ROWS), :] = got[:, :TILE]
            out_ref[2 * pair + 1, pl.ds(k * ROWS, ROWS), :] = got[:, TILE:]
        return 0

    lax.fori_loop(0, peers // 2, step, 0)


def sums_kernel(variables, recv_ref, state_ref, state_bf_ref, cot_ref, own_ref, dec_ref):
    peers = recv_ref.shape[0]
    node_count = state_ref.shape[1]
    nodes = lax.broadcasted_iota(jnp.int32, (node_count, TILE), 0)
    state_ref[...] = jnp.zeros_like(state_ref)
    cot_ref[...] = jnp.zeros_like(cot_ref)

    def step(pair, _):
        for k, total, index in ((0, state_ref, own_ref), (1, cot_ref, dec_ref)):
            data, picks = [], []
            for one in range(2):
                block = recv_ref[2 * pair + one, pl.ds(k * ROWS, ROWS), :]
                wide = block[80:ROWS].astype(F32)
                at = variables - 80
                slots = (2.0 * wide[at : at + 1] + wide[at + 1 : at + 2]).astype(jnp.int32)
                index[pl.ds(2 * pair + one, 1), :] = slots
                picks.append(jnp.where(nodes == slots, 1.0, 0.0).astype(BF16))
                data.append(block)
            total[...] += dot_nt(jnp.concatenate(data, axis=1), jnp.concatenate(picks, axis=1))
        return 0

    lax.fori_loop(0, peers // 2, step, 0)
    keep = lax.broadcasted_iota(jnp.int32, state_ref.shape, 0) < variables
    state_ref[...] = jnp.where(keep, state_ref[...], 0.0)
    cot_ref[...] = jnp.where(keep, cot_ref[...], 0.0)
    state_bf_ref[...] = state_ref[...].astype(BF16)


def norm_t(start, gain):
    inverse = lax.rsqrt(jnp.mean(start * start, axis=0, keepdims=True) + 1e-05)
    return inverse, (start * inverse * gain).astype(BF16)


def query_kernel(
    state_ref,
    cot_ref,
    encoder_t,
    decoder,
    gain_ref,
    query_t,
    output,
    start_ref,
    inverse_ref,
    top_ref,
    q_ref,
    qt_ref,
    g_ref,
    gt_ref,
):
    high, low = split(state_ref[...])
    start = dot(encoder_t[...], high) + dot(encoder_t[...], low)
    start_ref[...] = start
    inverse, normed = norm_t(start, gain_ref[...])
    inverse_ref[...] = inverse
    queries = dot(query_t[...], normed).astype(BF16)
    qt_ref[...] = queries
    q_ref[...] = queries.T
    high, low = split(cot_ref[...])
    top = dot(decoder[...], high) + dot(decoder[...], low)
    top_ref[...] = top
    grad = dot(output[...], top.astype(BF16)).astype(BF16)
    gt_ref[...] = grad
    g_ref[...] = grad.T


def attend_kernel(
    pattern,
    s0_ref,
    s1_ref,
    s2_ref,
    s3_ref,
    start_ref,
    inverse_ref,
    top_ref,
    q_ref,
    qt_ref,
    g_ref,
    gt_ref,
    encoder,
    encoder_t,
    gain_ref,
    query_w,
    key_w,
    value_w,
    key_t,
    value_t,
    output_t,
    decoder_t,
    decoded_ref,
    own_ref,
    o1_ref,
    o2_ref,
    o3_ref,
    enc_ref,
    start_s,
    inverse_s,
    keys_s,
    values_s,
    weight_s,
    prob_s,
    score_s,
    mixed_s,
    query_s,
    keyg_s,
    valueg_s,
):
    node_count = s0_ref.shape[1]
    pieces = (s0_ref, s1_ref, s2_ref, s3_ref)
    key_count = len(pieces) * node_count
    gain = gain_ref[...]
    scale = 1.0 / math.sqrt(HEAD)
    for r, piece in enumerate(pieces):
        span = pl.ds(r * node_count, node_count)
        start = dot(encoder_t[...], piece[...])
        start_s[:, span] = start
        inverse, normed = norm_t(start, gain)
        inverse_s[:, span] = inverse
        keys_s[:, span] = dot(key_t[...], normed).astype(BF16)
        values_s[:, span] = dot(value_t[...], normed).astype(BF16)

    def head(h, _):
        rows = pl.ds(pl.multiple_of(h * HEAD, HEAD), HEAD)
        q = q_ref[:, rows]
        g = g_ref[:, rows]
        kt = keys_s[rows, :]
        vt = values_s[rows, :]
        scores = dot(q, kt)
        for qt in range(node_count // TILE):
            for kb in range(key_count // TILE):
                bias = jnp.where(pattern[qt, kb] > 0, 0.0, -1e30).astype(F32)
                at = (slice(qt * TILE, (qt + 1) * TILE), slice(kb * TILE, (kb + 1) * TILE))
                weight_s[at] = scores[at] * (scale / math.log(2.0)) + bias
        biased = weight_s[...]
        weights = jnp.exp2(biased - jnp.max(biased, axis=1, keepdims=True))
        probs = weights * (1.0 / jnp.sum(weights, axis=1, keepdims=True))
        weight_s[...] = probs
        prob_s[...] = probs.astype(BF16)
        mixed = dot_nt(prob_s[...], vt)
        mixed_s[rows, :] = mixed.astype(BF16).T
        delta = jnp.sum(mixed * g.astype(F32), axis=1, keepdims=True)
        prob_grad = dot(g, vt)
        score_s[...] = (weight_s[...] * ((prob_grad - delta) * scale)).astype(BF16)
        query_s[rows, :] = dot_nt(score_s[...], kt).astype(BF16).T
        keyg_s[rows, :] = dot(qt_ref[rows, :], score_s[...]).astype(BF16)
        valueg_s[rows, :] = dot(gt_ref[rows, :], prob_s[...]).astype(BF16)
        return 0

    lax.fori_loop(0, HEADS, head, 0)
    final = start_ref[...] + dot(output_t[...], mixed_s[...])
    decoded_ref[...] = dot(decoder_t[...], final.astype(BF16)).astype(BF16)
    enc = jnp.zeros(enc_ref.shape, F32)
    for r, (piece, out) in enumerate(zip(pieces, (own_ref, o1_ref, o2_ref, o3_ref))):
        span = pl.ds(r * node_count, node_count)
        grad = dot(key_w[...], keyg_s[:, span]) + dot(value_w[...], valueg_s[:, span])
        if r == 0:
            grad = grad + dot(query_w[...], query_s[...])
            start, inverse = start_ref[...], inverse_ref[...]
        else:
            start, inverse = start_s[:, span], inverse_s[:, span]
        scaled = grad * gain
        mean = jnp.mean(start * scaled, axis=0, keepdims=True)
        total = inverse * scaled - start * (inverse * inverse * inverse * mean)
        if r == 0:
            total = total + top_ref[...]
        total = total.astype(BF16)
        out[...] = dot(encoder[...], total).astype(out.dtype)
        enc = enc + dot_nt(piece[...], total)
    enc_ref[...] = enc


def slots_kernel(own_idx, dec_idx, decoded_ref, own_ref, i1_ref, i2_ref, i3_ref, out_ref, grad_s):
    peers = out_ref.shape[0]
    node_count = decoded_ref.shape[1]
    total = own_ref[...]
    for piece in (i1_ref, i2_ref, i3_ref):
        total = total + piece[...].astype(F32)
    grad_s[...] = total.astype(BF16)
    nodes = lax.broadcasted_iota(jnp.int32, (node_count, TILE), 0)

    def step(pair, _):
        for k, index, data in ((0, dec_idx, decoded_ref), (1, own_idx, grad_s)):
            picks = [
                jnp.where(nodes == index[pl.ds(2 * pair + one, 1), :], 1.0, 0.0).astype(BF16)
                for one in range(2)
            ]
            got = dot(data[...], jnp.concatenate(picks, axis=1)).astype(BF16)
            out_ref[2 * pair, pl.ds(k * ROWS, ROWS), :] = got[:, :TILE]
            out_ref[2 * pair + 1, pl.ds(k * ROWS, ROWS), :] = got[:, TILE:]
        return 0

    lax.fori_loop(0, peers // 2, step, 0)


def unpack_kernel(back_ref, own_rank, dec_rank, denoised_ref, grad_ref, acc_d, acc_o):
    peers = back_ref.shape[0]
    variables = denoised_ref.shape[0]
    acc_d[...] = jnp.zeros_like(acc_d)
    acc_o[...] = jnp.zeros_like(acc_o)

    def step(pair, _):
        for k, rank, acc in ((0, dec_rank, acc_d), (1, own_rank, acc_o)):
            rows = pl.ds(k * ROWS, ROWS)
            data = jnp.concatenate([back_ref[2 * pair, rows, :], back_ref[2 * pair + 1, rows, :]], axis=1)
            acc[...] += dot(data, slot_onehot(rank, pair))
        return 0

    lax.fori_loop(0, peers // 2, step, 0)
    denoised_ref[...] = acc_d[0:variables, :].astype(BF16)
    grad_ref[...] = acc_o[0:variables, :]


def body(
    grid_state,
    cotangent,
    encoder_weight,
    norm_gain,
    query_weight,
    key_weight,
    value_weight,
    output_weight,
    decoder_weight,
    grid_owner,
    decode_node,
    tile_pattern,
):
    peers = lax.axis_size("wide")
    group = lax.axis_size("patch")
    variables, grid_count = grid_state.shape
    width = query_weight.shape[0]
    nodes = tile_pattern.shape[0] * TILE
    keys = group * nodes
    capacity = 2 * grid_count // peers
    shift = (nodes * group).bit_length() - 1
    vm = pltpu.VMEM

    send, own_rank, dec_rank = call(
        functools.partial(pack_kernel, shift),
        [((peers, 2 * ROWS, capacity), BF16), ((peers, grid_count), F32), ((peers, grid_count), F32)],
        [vm((ROWS, grid_count), F32), vm((ROWS, grid_count), BF16), vm((ROWS, grid_count), BF16)],
        "pack",
        4 * ROWS * grid_count * peers * capacity,
        grid_state,
        cotangent,
        grid_owner.reshape(1, grid_count),
        decode_node.reshape(1, grid_count),
    )
    recv = lax.all_to_all(send, "wide", split_axis=0, concat_axis=0, tiled=True)

    pad = ROWS - variables
    encoder = jnp.pad(encoder_weight, ((0, pad), (0, 0)))
    decoder = jnp.pad(decoder_weight, ((0, 0), (0, pad)))
    gain = norm_gain.astype(F32).reshape(width, 1)
    me = lax.axis_index("patch")
    pattern = jnp.roll(tile_pattern, -me * (nodes // TILE), axis=1)

    state, state_bf, cot, own_idx, dec_idx = call(
        functools.partial(sums_kernel, variables),
        [
            ((ROWS, nodes), F32),
            ((ROWS, nodes), BF16),
            ((ROWS, nodes), F32),
            ((peers, capacity), jnp.int32),
            ((peers, capacity), jnp.int32),
        ],
        [],
        "sums",
        4 * ROWS * nodes * peers * capacity,
        recv,
    )

    def from_ahead(x, r):
        return lax.ppermute(x, "patch", [((i + r) % group, i) for i in range(group)])

    def to_ahead(x, r):
        return lax.ppermute(x, "patch", [(i, (i + r) % group) for i in range(group)])

    pieces = [state_bf] + [from_ahead(state_bf, r) for r in range(1, group)]

    start, inverse, top, q, qt, g, gt = call(
        query_kernel,
        [
            ((width, nodes), F32),
            ((1, nodes), F32),
            ((width, nodes), F32),
            ((nodes, width), BF16),
            ((width, nodes), BF16),
            ((nodes, width), BF16),
            ((width, nodes), BF16),
        ],
        [],
        "query",
        4 * width * width * nodes,
        state,
        cot,
        encoder.T,
        decoder,
        gain,
        query_weight.T,
        output_weight,
    )
    decoded, own, o1, o2, o3, enc = call(
        attend_kernel,
        [((ROWS, nodes), BF16), ((ROWS, nodes), F32)]
        + [((ROWS, nodes), BF16)] * 3
        + [((ROWS, width), F32)],
        [
            vm((width, keys), F32),
            vm((1, keys), F32),
            vm((width, keys), BF16),
            vm((width, keys), BF16),
            vm((nodes, keys), F32),
            vm((nodes, keys), BF16),
            vm((nodes, keys), BF16),
            vm((width, nodes), BF16),
            vm((width, nodes), BF16),
            vm((width, keys), BF16),
            vm((width, keys), BF16),
        ],
        "attend",
        20 * nodes * keys * width,
        pattern,
        *pieces,
        start,
        inverse,
        top,
        q,
        qt,
        g,
        gt,
        encoder,
        encoder.T,
        gain,
        query_weight,
        key_weight,
        value_weight,
        key_weight.T,
        value_weight.T,
        output_weight.T,
        decoder.T,
        smem=(0,),
    )
    back = [to_ahead(o, r) for r, o in ((1, o1), (2, o2), (3, o3))]
    (reply,) = call(
        slots_kernel,
        [((peers, 2 * ROWS, capacity), BF16)],
        [vm((ROWS, nodes), BF16)],
        "slots",
        4 * ROWS * nodes * peers * capacity,
        own_idx,
        dec_idx,
        decoded,
        own,
        *back,
    )
    returned = lax.all_to_all(reply, "wide", split_axis=0, concat_axis=0, tiled=True)

    part = width // group
    turned = jnp.roll(enc, -me * part, axis=1)
    mine = turned[:, :part]
    for r in range(1, group):
        mine = mine + to_ahead(turned[:, r * part : (r + 1) * part], r)
    step = 1
    while step < peers:
        mine = mine + lax.ppermute(mine, "wide", [(i, i ^ step) for i in range(peers)])
        step *= 2
    whole = jnp.concatenate([mine] + [from_ahead(mine, r) for r in range(1, group)], axis=1)
    encoder_grad = jnp.roll(whole, me * part, axis=1)[:variables]

    denoised, state_grad = call(
        unpack_kernel,
        [((variables, grid_count), BF16), ((variables, grid_count), F32)],
        [vm((ROWS, grid_count), F32), vm((ROWS, grid_count), F32)],
        "unpack",
        4 * ROWS * grid_count * peers * capacity,
        returned,
        own_rank,
        dec_rank,
    )
    return (denoised, state_grad, encoder_grad)


def solution(mesh):
    in_specs = (
        P(None, ("wide", "patch")),
        P(None, ("wide", "patch")),
        P(),
        P(),
        P(),
        P(),
        P(),
        P(),
        P(),
        P(("wide", "patch")),
        P(("wide", "patch")),
        P(("wide", "patch"), None),
    )
    out_specs = (P(None, ("wide", "patch")), P(None, ("wide", "patch")), P())
    return jax.shard_map(body, mesh=mesh, in_specs=in_specs, out_specs=out_specs, check_vma=False)
```

time: 486 us -> 176 us (0.36)
  the two profiles are of different devices: /device:TPU:1 before, /device:TPU:0 now
where the time goes in v1:
time: 176 us; the launch traced here: 175 us
  Pallas kernels  72.1 us (41%)
  waiting for transfers between devices  52.1 us (30%)
  starting transfers between devices  37 us (21%)
  local copies, waits for them, and re-layouts  12.1 us (7%)
    pallas_call x6, Pallas kernels, call(): pl.pallas_call(kernel, out_shape=[jax.ShapeDtypeStruct(s, d) for s, d in...  72.1 us
    all_to_all x1, waiting for transfers between devices, body(): recv = lax.all_to_all(send, 'wide', split_axis=0, concat_axis=0, tiled=True)  20.7 us
    ppermute x5, waiting for transfers between devices, body(): lax.ppermute(mine, 'wide', [(i, i ^ step) for i in range(peers)])  17.3 us
    ppermute x5, starting transfers between devices, body(): lax.ppermute(mine, 'wide', [(i, i ^ step) for i in range(peers)])  9.15 us
    ppermute x6, waiting for transfers between devices, to_ahead(): lax.ppermute(x, 'patch', [(i, (i + r) % group) for i in range(group)])  9 us
    all_to_all x1, starting transfers between devices, body(): recv = lax.all_to_all(send, 'wide', split_axis=0, concat_axis=0, tiled=True)  8.56 us
    unnamed x41, local copies, waits for them, and re-layouts  7.97 us
    ppermute x6, starting transfers between devices, to_ahead(): lax.ppermute(x, 'patch', [(i, (i + r) % group) for i in range(group)])  7.67 us
  transfers between devices with their start and end apart: 19, of which 15 were waited for; matrix products, arithmetic and copies ran while one was open for 5% of the time, Pallas kernels for 3%

profile of v1, /device:TPU:0, one launch (start us, length us, event | category | flops | bytes accessed | tf_op | source)
XLA Modules:
  0.0 175.1 jit_solution(10275796398927478725)
XLA Ops:
  0.6 15.4 %pack.1 = (bf16[32,176,128]{2,1,0:T(8,128)(2,1)}, f32[32,2048]{1,0:T(8,128)}, f32[32,2048]{1,0:T(8,128)}) custom-call(bf16[84,2048]{1,0:T(8,128)(2,1)} %x_ref.1, bf16[84,2048]{1,0:T(8,128)(2,1)} %c_ref.1, s32[1,2048]{1,0:T(1,128)} %bitcast.16, s32[1,2048]{1,0:T(1,128)} %bitcast.17), custom_call_target="tpu_custom_call" | custom-call | flops 2952790016 | bytes 1048576 | tf_op jit(solution)/shard_map/pack/pallas_call | solution.py:37
  16.0 8.6 %all-to-all-start = ((bf16[32,176,128]{2,1,0:T(8,128)(2,1)}), bf16[32,176,128]{2,1,0:T(8,128)(2,1)S(1)}, u32[]{:S(2)}, u32[]{:S(2)}) async-start(bf16[32,176,128]{2,1,0:T(8,128)(2,1)} %get-tuple-element.27), calls=%async_computation | async-start | bytes 2883584 | tf_op jit(solution)/shard_map/all_to_all | solution.py:348
  24.6 0.1 copy.22
  24.8 0.1 pad_add_fusion
  24.9 0.6 pad_bitcast_fusion.decoder_t
  25.5 0.7 pad_bitcast_fusion.1.encoder_t
  26.2 20.7 %all-to-all-done.recv_ref = bf16[32,176,128]{2,1,0:T(8,128)(2,1)S(1)} async-done(((bf16[32,176,128]{2,1,0:T(8,128)(2,1)}), bf16[32,176,128]{2,1,0:T(8,128)(2,1)S(1)}, u32[]{:S(2)}, u32[]{:S(2)}) %all-to-all-start) | async-done | bytes 1441824 | tf_op jit(solution)/shard_map/all_to_all | solution.py:348
  46.9 1.1 copy-done.1
  48.0 7.0 %sums.1 = (f32[88,512]{1,0:T(8,128)}, bf16[88,512]{1,0:T(8,128)(2,1)}, f32[88,512]{1,0:T(8,128)}, s32[32,128]{1,0:T(8,128)}, s32[32,128]{1,0:T(8,128)}) custom-call(bf16[32,176,128]{2,1,0:T(8,128)(2,1)} %copy-done.1), custom_call_target="tpu_custom_call" | custom-call | flops 738197504 | bytes 1048576 | tf_op jit(solution)/shard_map/sums/pallas_call | solution.py:37
  55.0 2.8 %collective-permute-start = (bf16[88,512]{1,0:T(8,128)(2,1)}, bf16[88,512]{1,0:T(8,128)(2,1)S(1)}, u32[]{:S(2)}, u32[]{:S(2)}) collective-permute-start(bf16[88,512]{1,0:T(8,128)(2,1)} %get-tuple-element.30.s0_ref), channel_id=1, source_target_pairs={{1,0},{2,1},{3,2},{0,3},{5,4},{6,5},{7,6},{4,7},{9,8},{10,9},{11,1... | collective-permute-start | bytes 270344 | tf_op jit(solution)/shard_map/ppermute | solution.py:373
  57.8 0.8 collective-permute-start.1
  58.6 0.9 collective-permute-start.2
  59.4 0.6 constant_dynamic-slice_fusion.pattern
  60.1 0.1 copy.31
  60.2 0.1 copy.32
  60.4 0.9 copy.25.gain_ref
  61.2 1.0 copy.23
  62.2 0.7 pad.9.clone.decoder
  62.9 0.6 pad.8.clone.encoder
  63.6 1.0 copy.26
  64.6 1.0 copy.27
  65.6 1.0 copy.28
  66.6 4.5 %query.1 = (f32[512,512]{1,0:T(8,128)}, f32[1,512]{1,0:T(1,128)}, f32[512,512]{1,0:T(8,128)}, bf16[512,512]{1,0:T(8,128)(2,1)}, bf16[512,512]{1,0:T(8,128)(2,1)}...) custom-call(f32[88,512]{1,0:T(8,128)} %get-tuple-element.31.state_ref, f32[88,512]{1,0:T(8,128)} %get-tuple-element.32.cot_ref, ...), custom_call_target="tpu_custom_call" | custom-call | flops 536870912 | bytes 1048576 | tf_op jit(solution)/shard_map/query/pallas_call | solution.py:37
  71.1 0.0 collective-permute-done.s1_ref
  71.1 0.0 collective-permute-done.1.s2_ref
  71.2 0.6 copy-done.11
  71.8 0.0 copy-done.12
  71.8 0.0 copy-done.13
  71.8 29.0 %attend.1 = (bf16[88,512]{1,0:T(8,128)(2,1)}, f32[88,512]{1,0:T(8,128)}, bf16[88,512]{1,0:T(8,128)(2,1)}, bf16[88,512]{1,0:T(8,128)(2,1)}, bf16[88,512]{1,0:T(8,128)(2,1)}, /*index=5*/f32[88,512]{1,0:T(8,128)}) custom-call(s32[4,16]{1,0:T(4,128)} %constant_dynamic-slice_fusion.pattern, bf16[88,512]{1,0:T(8,128)(2,1)} %get-tuple-element.30.s0_ref, ...), custom_call_target="tpu_custom_call" | custom-call | flops 10737418240 | bytes 1048576 | tf_op jit(solution)/shard_map/attend/pallas_call | solution.py:37
  100.8 1.9 %collective-permute-start.3 = (bf16[88,512]{1,0:T(8,128)(2,1)}, bf16[88,512]{1,0:T(8,128)(2,1)S(1)}, u32[]{:S(2)}, u32[]{:S(2)}) collective-permute-start(bf16[88,512]{1,0:T(8,128)(2,1)} %get-tuple-element.42), channel_id=1, source_target_pairs={{0,1},{1,2},{2,3},{3,0},{4,5},{5,6},{6,7},{7,4},{8,9},{9,10},{10,1... | collective-permute-start | bytes 270344 | tf_op jit(solution)/shard_map/ppermute | solution.py:376
  102.7 2.0 %collective-permute-start.4 = (bf16[88,512]{1,0:T(8,128)(2,1)}, bf16[88,512]{1,0:T(8,128)(2,1)S(1)}, u32[]{:S(2)}, u32[]{:S(2)}) collective-permute-start(bf16[88,512]{1,0:T(8,128)(2,1)} %get-tuple-element.43), channel_id=1, source_target_pairs={{0,2},{1,3},{2,0},{3,1},{4,6},{5,7},{6,4},{7,5},{8,10},{9,11},{10,... | collective-permute-start | bytes 270344 | tf_op jit(solution)/shard_map/ppermute | solution.py:376
  104.7 0.8 collective-permute-start.5
  105.5 1.4 collective-permute-done.3.i1_ref
  106.8 2.1 %collective-permute-done.4.i2_ref = bf16[88,512]{1,0:T(8,128)(2,1)S(1)} collective-permute-done((bf16[88,512]{1,0:T(8,128)(2,1)}, bf16[88,512]{1,0:T(8,128)(2,1)S(1)}, u32[]{:S(2)}, u32[]{:S(2)}) %collective-permute-start.4) | collective-permute-done | bytes 90144 | tf_op jit(solution)/shard_map/ppermute | solution.py:376
  108.9 0.5 collective-permute-done.5.i3_ref
  109.4 0.1 copy-done.15
  109.6 0.5 copy-done.16
  110.1 5.9 %slots.1 = bf16[32,176,128]{2,1,0:T(8,128)(2,1)} custom-call(s32[32,128]{1,0:T(8,128)} %get-tuple-element.28.own_idx, s32[32,128]{1,0:T(8,128)} %get-tuple-element.29.dec_idx, bf16[88,512]{1,0:T(8,128)(2,1)} %get-tuple-element.40.decoded_ref, f32[88,512]{1,0:T(8,128)} %get-tuple-element.41.own_ref, bf16[88,512]{1,0:T(8,128)(2,1)} %copy-done.14, ...), custom_call_target="tpu_custom_call" | custom-call | flops 738197504 | bytes 1048576 | tf_op jit(solution)/shard_map/slots/pallas_call | solution.py:37
  116.0 4.1 %all-to-all-start.1 = ((bf16[32,176,128]{2,1,0:T(8,128)(2,1)}), bf16[32,176,128]{2,1,0:T(8,128)(2,1)S(1)}, u32[]{:S(2)}, u32[]{:S(2)}) async-start(bf16[32,176,128]{2,1,0:T(8,128)(2,1)} %slots.1), calls=%async_computation.1 | async-start | bytes 2883584 | tf_op jit(solution)/shard_map/all_to_all | solution.py:456
  120.2 2.0 %collective-permute-start.8 = (f32[88,128]{1,0:T(8,128)S(1)}, f32[88,128]{1,0:T(8,128)S(1)}, u32[]{:S(2)}, u32[]{:S(2)}) collective-permute-start(f32[88,128]{1,0:T(8,128)S(1)} %get-tuple-element.52), channel_id=1, source_target_pairs={{0,3},{1,0},{2,1},{3,2},{4,7},{5,4},{6,5},{7,6},{8,11},{9,8},{10,9... | collective-permute-start | bytes 135176 | tf_op jit(solution)/shard_map/ppermute | solution.py:376
  122.2 0.7 collective-permute-start.7
  122.9 0.4 collective-permute-start.6
  123.3 1.5 collective-permute-done.8
  124.7 3.1 %collective-permute-done.7 = f32[88,128]{1,0:T(8,128)S(1)} collective-permute-done((f32[88,128]{1,0:T(8,128)S(1)}, f32[88,128]{1,0:T(8,128)S(1)}, u32[]{:S(2)}, u32[]{:S(2)}) %collective-permute-start.7) | collective-permute-done | bytes 45088 | tf_op jit(solution)/shard_map/ppermute | solution.py:376
  127.8 0.5 collective-permute-done.6
  128.3 0.1 collective-permute-start.9
  128.4 1.2 collective-permute-done.9
  129.6 1.8 %collective-permute-start.10 = (f32[88,128]{1,0:T(8,128)S(1)}, f32[88,128]{1,0:T(8,128)S(1)}, u32[]{:S(2)}, u32[]{:S(2)}) collective-permute-start(f32[88,128]{1,0:T(8,128)S(1)} %add.50), channel_id=1, source_target_pairs={{0,8},{4,12},{8,0},{12,4},{16,24},{20,28},{24,16},{28,20},{32,40},... | collective-permute-start | bytes 135176 | tf_op jit(solution)/shard_map/ppermute | solution.py:465
  131.4 8.0 %collective-permute-done.10 = f32[88,128]{1,0:T(8,128)S(1)} collective-permute-done((f32[88,128]{1,0:T(8,128)S(1)}, f32[88,128]{1,0:T(8,128)S(1)}, u32[]{:S(2)}, u32[]{:S(2)}) %collective-permute-start.10) | collective-permute-done | bytes 45088 | tf_op jit(solution)/shard_map/ppermute | solution.py:465
  139.4 2.7 %collective-permute-start.11 = (f32[88,128]{1,0:T(8,128)S(1)}, f32[88,128]{1,0:T(8,128)S(1)}, u32[]{:S(2)}, u32[]{:S(2)}) collective-permute-start(f32[88,128]{1,0:T(8,128)S(1)} %add.51), channel_id=1, source_target_pairs={{0,16},{4,20},{8,24},{12,28},{16,0},{20,4},{24,8},{28,12},{32,48},... | collective-permute-start | bytes 135176 | tf_op jit(solution)/shard_map/ppermute | solution.py:465
  142.1 3.0 %collective-permute-done.11 = f32[88,128]{1,0:T(8,128)S(1)} collective-permute-done((f32[88,128]{1,0:T(8,128)S(1)}, f32[88,128]{1,0:T(8,128)S(1)}, u32[]{:S(2)}, u32[]{:S(2)}) %collective-permute-start.11) | collective-permute-done | bytes 45088 | tf_op jit(solution)/shard_map/ppermute | solution.py:465
  145.1 1.5 collective-permute-start.12
  146.5 2.6 %collective-permute-done.12 = f32[88,128]{1,0:T(8,128)S(1)} collective-permute-done((f32[88,128]{1,0:T(8,128)S(1)}, f32[88,128]{1,0:T(8,128)S(1)}, u32[]{:S(2)}, u32[]{:S(2)}) %collective-permute-start.12) | collective-permute-done | bytes 45088 | tf_op jit(solution)/shard_map/ppermute | solution.py:465
  149.2 3.2 %collective-permute-start.13 = (f32[88,128]{1,0:T(8,128)S(1)}, f32[88,128]{1,0:T(8,128)S(1)}, u32[]{:S(2)}, u32[]{:S(2)}) collective-permute-start(f32[88,128]{1,0:T(8,128)S(1)} %add.53), channel_id=1, source_target_pairs={{0,64},{4,68},{8,72},{12,76},{16,80},{20,84},{24,88},{28,92},{32,9... | collective-permute-start | bytes 135176 | tf_op jit(solution)/shard_map/ppermute | solution.py:465
  152.3 2.5 %collective-permute-done.13 = f32[88,128]{1,0:T(8,128)S(1)} collective-permute-done((f32[88,128]{1,0:T(8,128)S(1)}, f32[88,128]{1,0:T(8,128)S(1)}, u32[]{:S(2)}, u32[]{:S(2)}) %collective-permute-start.13) | collective-permute-done | bytes 45088 | tf_op jit(solution)/shard_map/ppermute | solution.py:465
  154.8 2.0 %collective-permute-start.14 = (f32[88,128]{1,0:T(8,128)S(1)}, f32[88,128]{1,0:T(8,128)S(1)}, u32[]{:S(2)}, u32[]{:S(2)}) collective-permute-start(f32[88,128]{1,0:T(8,128)S(1)} %add.54), channel_id=1, source_target_pairs={{1,0},{2,1},{3,2},{0,3},{5,4},{6,5},{7,6},{4,7},{9,8},{10,9},{11,1... | collective-permute-start | bytes 135176 | tf_op jit(solution)/shard_map/ppermute | solution.py:373
  156.8 0.7 collective-permute-start.15
  157.5 0.4 collective-permute-start.16
  157.9 1.1 collective-permute-done.14
  158.9 3.5 %collective-permute-done.15 = f32[88,128]{1,0:T(8,128)S(1)} collective-permute-done((f32[88,128]{1,0:T(8,128)S(1)}, f32[88,128]{1,0:T(8,128)S(1)}, u32[]{:S(2)}, u32[]{:S(2)}) %collective-permute-start.15) | collective-permute-done | bytes 45088 | tf_op jit(solution)/shard_map/ppermute | solution.py:373
  162.4 0.5 collective-permute-done.16
  162.9 0.8 fusion.3
  163.7 1.1 copy-done
  164.8 10.3 %unpack.1 = (bf16[84,2048]{1,0:T(8,128)(2,1)}, f32[84,2048]{1,0:T(8,128)}) custom-call(bf16[32,176,128]{2,1,0:T(8,128)(2,1)} %copy-done, f32[32,2048]{1,0:T(8,128)} %get-tuple-element.45.own_rank, f32[32,2048]{1,0:T(8,128)} %get-tuple-element.46.dec_rank), custom_call_target="tpu_custom_call" | custom-call | flops 2952790016 | bytes 1048576 | tf_op jit(solution)/shard_map/unpack/pallas_call | solution.py:37
  (38 shorter events, 0.2 us)
Async XLA Ops:
  16.0 8.6 %copy-start.8 = (bf16[84,512]{1,0:T(8,128)(2,1)S(1)}, bf16[84,512]{1,0:T(8,128)(2,1)}, u32[]{:S(2)}) copy-start(bf16[84,512]{1,0:T(8,128)(2,1)} %param.16) | copy-start | bytes 258052
  16.0 8.8 %copy-start.9 = (s32[4,16]{1,0:T(4,128)S(1)}, s32[4,16]{1,0:T(4,128)}, u32[]{:S(2)}) copy-start(s32[4,16]{1,0:T(4,128)} %param.25) | copy-start | bytes 772
  16.0 8.8 %copy-start.6 = (bf16[512,84]{0,1:T(8,128)(2,1)S(1)}, bf16[512,84]{0,1:T(8,128)(2,1)}, u32[]{:S(2)}) copy-start(bf16[512,84]{0,1:T(8,128)(2,1)} %param.22) | copy-start | bytes 258052
  16.0 30.9 %all-to-all-start = ((bf16[32,176,128]{2,1,0:T(8,128)(2,1)}), bf16[32,176,128]{2,1,0:T(8,128)(2,1)S(1)}, u32[]{:S(2)}, u32[]{:S(2)}) async-start(bf16[32,176,128]{2,1,0:T(8,128)(2,1)} %get-tuple-element.27), calls=%async_computation | async-start | bytes 2883584 | tf_op jit(solution)/shard_map/all_to_all | solution.py:348
  26.2 34.2 %copy-start.10 = (bf16[512]{0:T(512)(128)(2,1)S(1)}, bf16[512]{0:T(512)(128)(2,1)}, u32[]{:S(2)}) copy-start(bf16[512]{0:T(512)(128)(2,1)} %param.17) | copy-start | bytes 3076
  26.2 35.0 %copy-start.3 = (bf16[512,512]{1,0:T(8,128)(2,1)S(1)}, bf16[512,512]{1,0:T(8,128)(2,1)}, u32[]{:S(2)}) copy-start(bf16[512,512]{1,0:T(8,128)(2,1)} %query_w.1) | copy-start | bytes 1572868
  46.9 1.1 copy-start.1
  55.0 8.6 %copy-start.4 = (bf16[512,512]{1,0:T(8,128)(2,1)S(1)}, bf16[512,512]{1,0:T(8,128)(2,1)}, u32[]{:S(2)}) copy-start(bf16[512,512]{1,0:T(8,128)(2,1)} %key_w.1) | copy-start | bytes 1572868
  55.0 16.1 %collective-permute-start = (bf16[88,512]{1,0:T(8,128)(2,1)}, bf16[88,512]{1,0:T(8,128)(2,1)S(1)}, u32[]{:S(2)}, u32[]{:S(2)}) collective-permute-start(bf16[88,512]{1,0:T(8,128)(2,1)} %get-tuple-element.30.s0_ref), channel_id=1, source_target_pairs={{1,0},{2,1},{3,2},{0,3},{5,4},{6,5},{7,6},{4,7},{9,8},{10,9},{11,1... | collective-permute-start | bytes 270344 | tf_op jit(solution)/shard_map/ppermute | solution.py:373
  57.8 13.4 %collective-permute-start.1 = (bf16[88,512]{1,0:T(8,128)(2,1)}, bf16[88,512]{1,0:T(8,128)(2,1)S(1)}, u32[]{:S(2)}, u32[]{:S(2)}) collective-permute-start(bf16[88,512]{1,0:T(8,128)(2,1)} %get-tuple-element.30.s0_ref), channel_id=1, source_target_pairs={{2,0},{3,1},{0,2},{1,3},{6,4},{7,5},{4,6},{5,7},{10,8},{11,9},{8,1... | collective-permute-start | bytes 270344 | tf_op jit(solution)/shard_map/ppermute | solution.py:373
  58.6 12.6 %collective-permute-start.2 = (bf16[88,512]{1,0:T(8,128)(2,1)}, bf16[88,512]{1,0:T(8,128)(2,1)S(1)}, u32[]{:S(2)}, u32[]{:S(2)}) collective-permute-start(bf16[88,512]{1,0:T(8,128)(2,1)} %get-tuple-element.30.s0_ref), channel_id=1, source_target_pairs={{3,0},{0,1},{1,2},{2,3},{7,4},{4,5},{5,6},{6,7},{11,8},{8,9},{9,10... | collective-permute-start | bytes 270344 | tf_op jit(solution)/shard_map/ppermute | solution.py:373
  60.4 4.2 %copy-start.5 = (bf16[512,512]{1,0:T(8,128)(2,1)S(1)}, bf16[512,512]{1,0:T(8,128)(2,1)}, u32[]{:S(2)}) copy-start(bf16[512,512]{1,0:T(8,128)(2,1)} %value_w.1) | copy-start | bytes 1572868
  62.2 3.3 %copy-start.2 = (bf16[512,512]{1,0:T(8,128)(2,1)S(1)}, bf16[512,512]{1,0:T(8,128)(2,1)}, u32[]{:S(2)}) copy-start(bf16[512,512]{1,0:T(8,128)(2,1)} %output.1) | copy-start | bytes 1572868
  71.1 0.6 copy-start.11
  71.1 0.6 copy-start.12
  71.2 0.7 copy-start.13
  100.8 6.0 %collective-permute-start.3 = (bf16[88,512]{1,0:T(8,128)(2,1)}, bf16[88,512]{1,0:T(8,128)(2,1)S(1)}, u32[]{:S(2)}, u32[]{:S(2)}) collective-permute-start(bf16[88,512]{1,0:T(8,128)(2,1)} %get-tuple-element.42), channel_id=1, source_target_pairs={{0,1},{1,2},{2,3},{3,0},{4,5},{5,6},{6,7},{7,4},{8,9},{9,10},{10,1... | collective-permute-start | bytes 270344 | tf_op jit(solution)/shard_map/ppermute | solution.py:376
  102.7 6.2 %collective-permute-start.4 = (bf16[88,512]{1,0:T(8,128)(2,1)}, bf16[88,512]{1,0:T(8,128)(2,1)S(1)}, u32[]{:S(2)}, u32[]{:S(2)}) collective-permute-start(bf16[88,512]{1,0:T(8,128)(2,1)} %get-tuple-element.43), channel_id=1, source_target_pairs={{0,2},{1,3},{2,0},{3,1},{4,6},{5,7},{6,4},{7,5},{8,10},{9,11},{10,... | collective-permute-start | bytes 270344 | tf_op jit(solution)/shard_map/ppermute | solution.py:376
  104.7 4.7 %collective-permute-start.5 = (bf16[88,512]{1,0:T(8,128)(2,1)}, bf16[88,512]{1,0:T(8,128)(2,1)S(1)}, u32[]{:S(2)}, u32[]{:S(2)}) collective-permute-start(bf16[88,512]{1,0:T(8,128)(2,1)} %get-tuple-element.44), channel_id=1, source_target_pairs={{0,3},{1,0},{2,1},{3,2},{4,7},{5,4},{6,5},{7,6},{8,11},{9,8},{10,9... | collective-permute-start | bytes 270344 | tf_op jit(solution)/shard_map/ppermute | solution.py:376
  106.8 2.6 %copy-start.14 = (bf16[88,512]{1,0:T(8,128)(2,1)}, bf16[88,512]{1,0:T(8,128)(2,1)S(1)}, u32[]{:S(2)}) copy-start(bf16[88,512]{1,0:T(8,128)(2,1)S(1)} %collective-permute-done.3.i1_ref) | copy-start | bytes 270340
  108.9 0.6 copy-start.15
  109.4 0.6 copy-start.16
  116.0 4.1 %copy-start.7 = (f32[88,512]{1,0:T(8,128)S(1)}, f32[88,512]{1,0:T(8,128)}, u32[]{:S(2)}) copy-start(f32[88,512]{1,0:T(8,128)} %get-tuple-element.49) | copy-start | bytes 540676
  116.0 47.7 %all-to-all-start.1 = ((bf16[32,176,128]{2,1,0:T(8,128)(2,1)}), bf16[32,176,128]{2,1,0:T(8,128)(2,1)S(1)}, u32[]{:S(2)}, u32[]{:S(2)}) async-start(bf16[32,176,128]{2,1,0:T(8,128)(2,1)} %slots.1), calls=%async_computation.1 | async-start | bytes 2883584 | tf_op jit(solution)/shard_map/all_to_all | solution.py:456
  120.2 4.5 %collective-permute-start.8 = (f32[88,128]{1,0:T(8,128)S(1)}, f32[88,128]{1,0:T(8,128)S(1)}, u32[]{:S(2)}, u32[]{:S(2)}) collective-permute-start(f32[88,128]{1,0:T(8,128)S(1)} %get-tuple-element.52), channel_id=1, source_target_pairs={{0,3},{1,0},{2,1},{3,2},{4,7},{5,4},{6,5},{7,6},{8,11},{9,8},{10,9... | collective-permute-start | bytes 135176 | tf_op jit(solution)/shard_map/ppermute | solution.py:376
  122.2 5.6 %collective-permute-start.7 = (f32[88,128]{1,0:T(8,128)S(1)}, f32[88,128]{1,0:T(8,128)S(1)}, u32[]{:S(2)}, u32[]{:S(2)}) collective-permute-start(f32[88,128]{1,0:T(8,128)S(1)} %get-tuple-element.51), channel_id=1, source_target_pairs={{0,2},{1,3},{2,0},{3,1},{4,6},{5,7},{6,4},{7,5},{8,10},{9,11},{10,... | collective-permute-start | bytes 135176 | tf_op jit(solution)/shard_map/ppermute | solution.py:376
  122.9 5.4 %collective-permute-start.6 = (f32[88,128]{1,0:T(8,128)S(1)}, f32[88,128]{1,0:T(8,128)S(1)}, u32[]{:S(2)}, u32[]{:S(2)}) collective-permute-start(f32[88,128]{1,0:T(8,128)S(1)} %get-tuple-element.50), channel_id=1, source_target_pairs={{0,1},{1,2},{2,3},{3,0},{4,5},{5,6},{6,7},{7,4},{8,9},{9,10},{10,1... | collective-permute-start | bytes 135176 | tf_op jit(solution)/shard_map/ppermute | solution.py:376
  128.3 1.3 collective-permute-start.9
  129.6 9.8 %collective-permute-start.10 = (f32[88,128]{1,0:T(8,128)S(1)}, f32[88,128]{1,0:T(8,128)S(1)}, u32[]{:S(2)}, u32[]{:S(2)}) collective-permute-start(f32[88,128]{1,0:T(8,128)S(1)} %add.50), channel_id=1, source_target_pairs={{0,8},{4,12},{8,0},{12,4},{16,24},{20,28},{24,16},{28,20},{32,40},... | collective-permute-start | bytes 135176 | tf_op jit(solution)/shard_map/ppermute | solution.py:465
  139.4 5.6 %collective-permute-start.11 = (f32[88,128]{1,0:T(8,128)S(1)}, f32[88,128]{1,0:T(8,128)S(1)}, u32[]{:S(2)}, u32[]{:S(2)}) collective-permute-start(f32[88,128]{1,0:T(8,128)S(1)} %add.51), channel_id=1, source_target_pairs={{0,16},{4,20},{8,24},{12,28},{16,0},{20,4},{24,8},{28,12},{32,48},... | collective-permute-start | bytes 135176 | tf_op jit(solution)/shard_map/ppermute | solution.py:465
  145.1 4.1 %collective-permute-start.12 = (f32[88,128]{1,0:T(8,128)S(1)}, f32[88,128]{1,0:T(8,128)S(1)}, u32[]{:S(2)}, u32[]{:S(2)}) collective-permute-start(f32[88,128]{1,0:T(8,128)S(1)} %add.52), channel_id=1, source_target_pairs={{0,32},{4,36},{8,40},{12,44},{16,48},{20,52},{24,56},{28,60},{32,0... | collective-permute-start | bytes 135176 | tf_op jit(solution)/shard_map/ppermute | solution.py:465
  149.2 5.6 %collective-permute-start.13 = (f32[88,128]{1,0:T(8,128)S(1)}, f32[88,128]{1,0:T(8,128)S(1)}, u32[]{:S(2)}, u32[]{:S(2)}) collective-permute-start(f32[88,128]{1,0:T(8,128)S(1)} %add.53), channel_id=1, source_target_pairs={{0,64},{4,68},{8,72},{12,76},{16,80},{20,84},{24,88},{28,92},{32,9... | collective-permute-start | bytes 135176 | tf_op jit(solution)/shard_map/ppermute | solution.py:465
  154.8 4.1 %collective-permute-start.14 = (f32[88,128]{1,0:T(8,128)S(1)}, f32[88,128]{1,0:T(8,128)S(1)}, u32[]{:S(2)}, u32[]{:S(2)}) collective-permute-start(f32[88,128]{1,0:T(8,128)S(1)} %add.54), channel_id=1, source_target_pairs={{1,0},{2,1},{3,2},{0,3},{5,4},{6,5},{7,6},{4,7},{9,8},{10,9},{11,1... | collective-permute-start | bytes 135176 | tf_op jit(solution)/shard_map/ppermute | solution.py:373
  156.8 5.6 %collective-permute-start.15 = (f32[88,128]{1,0:T(8,128)S(1)}, f32[88,128]{1,0:T(8,128)S(1)}, u32[]{:S(2)}, u32[]{:S(2)}) collective-permute-start(f32[88,128]{1,0:T(8,128)S(1)} %add.54), channel_id=1, source_target_pairs={{2,0},{3,1},{0,2},{1,3},{6,4},{7,5},{4,6},{5,7},{10,8},{11,9},{8,1... | collective-permute-start | bytes 135176 | tf_op jit(solution)/shard_map/ppermute | solution.py:373
  157.5 5.4 %collective-permute-start.16 = (f32[88,128]{1,0:T(8,128)S(1)}, f32[88,128]{1,0:T(8,128)S(1)}, u32[]{:S(2)}, u32[]{:S(2)}) collective-permute-start(f32[88,128]{1,0:T(8,128)S(1)} %add.54), channel_id=1, source_target_pairs={{3,0},{0,1},{1,2},{2,3},{7,4},{4,5},{5,6},{6,7},{11,8},{8,9},{9,10... | collective-permute-start | bytes 135176 | tf_op jit(solution)/shard_map/ppermute | solution.py:373
  163.7 1.1 copy-start

commit v2 on v1

v2 whole, which is shorter than its diff:
```python
import functools
import math

import jax
import jax.numpy as jnp
from jax import lax
from jax.experimental import pallas as pl
from jax.experimental.pallas import tpu as pltpu
from jax.sharding import PartitionSpec as P

HEADS = 4
HEAD = 128
TILE = 128
ROWS = 88
F32 = jnp.float32
BF16 = jnp.bfloat16
MIB = 1024 * 1024
ATTEND_LIMIT = 28
SHARE = 11


def dot(a, b):
    return jnp.dot(a, b, preferred_element_type=F32)


def dot_nt(a, b):
    return lax.dot_general(a, b, (((1,), (1,)), ((), ())), preferred_element_type=F32)


def split(x):
    high = x.astype(BF16)
    return high, (x - high.astype(F32)).astype(BF16)


def call(kernel, outs, scratch, name, flops, *args, smem=(), limit=12):
    specs = [
        pl.BlockSpec(memory_space=pltpu.SMEM if i in smem else pltpu.VMEM) for i in range(len(args))
    ]
    return pl.pallas_call(
        kernel,
        out_shape=[jax.ShapeDtypeStruct(s, d) for s, d in outs],
        in_specs=specs,
        out_specs=[pl.BlockSpec(memory_space=pltpu.VMEM) for _ in outs],
        scratch_shapes=scratch,
        compiler_params=pltpu.CompilerParams(vmem_limit_bytes=limit * MIB),
        cost_estimate=pl.CostEstimate(flops=flops, bytes_accessed=1 << 20, transcendentals=0),
        name=name,
    )(*args)


def slot_onehot(rank_ref, pair):
    grid_count = rank_ref.shape[1]
    level = lax.broadcasted_iota(jnp.int32, (TILE, grid_count), 0).astype(F32).astype(BF16)
    parts = []
    for k in range(2):
        row = rank_ref[pl.ds(2 * pair + k, 1), :].astype(BF16)
        parts.append(jnp.where(level == row, jnp.ones((), BF16), jnp.zeros((), BF16)))
    return jnp.concatenate(parts, axis=0)


def loop(count, unroll, step):
    def some(i, _):
        for k in range(unroll):
            step(i * unroll + k)
        return 0

    lax.fori_loop(0, count // unroll, some, 0)


def pack_kernel(shift, mask, x_ref, index, out_ref, rank, wide_s, pay):
    variables, grid_count = x_ref.shape
    peers = out_ref.shape[0]
    chunk = 256
    upper = jnp.where(
        lax.broadcasted_iota(jnp.int32, (chunk, chunk), 0)
        < lax.broadcasted_iota(jnp.int32, (chunk, chunk), 1),
        1.0,
        0.0,
    ).astype(BF16)
    carry = jnp.zeros((peers, 1), F32)
    for start in range(0, grid_count, chunk):
        span = pl.ds(start, chunk)
        nodes = index[:, span]
        hit = lax.broadcasted_iota(jnp.int32, (peers, chunk), 0) == (nodes >> shift)
        ones = jnp.where(hit, 1.0, 0.0)
        before = dot(ones.astype(BF16), upper) + carry
        rank[:, span] = jnp.where(hit, before, -1.0)
        carry = carry + jnp.sum(ones, axis=1, keepdims=True)
    local = index[...] & mask
    wide_s[0:variables, :] = x_ref[...].astype(F32)
    wide_s[variables : variables + 1, :] = (local >> 1).astype(F32)
    wide_s[variables + 1 : variables + 2, :] = (local & 1).astype(F32)
    wide_s[variables + 2 : ROWS, :] = jnp.zeros((ROWS - variables - 2, grid_count), F32)
    pay[...] = wide_s[...].astype(BF16)

    def step(pair):
        got = dot_nt(pay[...], slot_onehot(rank, pair)).astype(BF16)
        out_ref[2 * pair] = got[:, :TILE]
        out_ref[2 * pair + 1] = got[:, TILE:]

    loop(peers // 2, 4, step)


def sums_kernel(variables, recv_ref, high_ref, low_ref, index, total_ref):
    peers = recv_ref.shape[0]
    node_count = total_ref.shape[1]
    nodes = lax.broadcasted_iota(jnp.int32, (node_count, TILE), 0)
    total_ref[...] = jnp.zeros_like(total_ref)

    def step(pair):
        data, picks = [], []
        for one in range(2):
            block = recv_ref[2 * pair + one]
            wide = block[80:ROWS].astype(F32)
            at = variables - 80
            slots = (2.0 * wide[at : at + 1] + wide[at + 1 : at + 2]).astype(jnp.int32)
            index[pl.ds(2 * pair + one, 1), :] = slots
            picks.append(jnp.where(nodes == slots, 1.0, 0.0).astype(BF16))
            data.append(block)
        total_ref[...] += dot_nt(jnp.concatenate(data, axis=1), jnp.concatenate(picks, axis=1))

    loop(peers // 2, 4, step)
    keep = lax.broadcasted_iota(jnp.int32, total_ref.shape, 0) < variables
    high_ref[...], low_ref[...] = split(jnp.where(keep, total_ref[...], 0.0))


def padded(ref, rows_s):
    rows_s[...] = jnp.zeros_like(rows_s)
    rows_s[0 : ref.shape[0], :] = ref[...].astype(F32)
    return rows_s[0:ROWS, :].astype(BF16), rows_s[...].T[:, :ROWS].astype(BF16)


def column(ref):
    return jnp.broadcast_to(ref[...].astype(F32), (TILE, ref.shape[1])).T[:, :1]


def norm_t(start, gain):
    inverse = lax.rsqrt(jnp.mean(start * start, axis=0, keepdims=True) + 1e-05)
    return inverse, (start * inverse * gain).astype(BF16)


def query_kernel(high, low, enc, gain_ref, query_w, start_ref, inverse_ref, q_ref, qt_ref, rows_s):
    _, encoder_t = padded(enc, rows_s)
    start = dot(encoder_t, high[...]) + dot(encoder_t, low[...])
    start_ref[...] = start
    inverse, normed = norm_t(start, column(gain_ref))
    inverse_ref[...] = inverse
    queries = dot(query_w[...].T, normed).astype(BF16)
    qt_ref[...] = queries
    q_ref[...] = queries.T


def top_kernel(high, low, dec, output, top_ref, g_ref, gt_ref, rows_s):
    _, decoder = padded(dec, rows_s)
    top = dot(decoder, high[...]) + dot(decoder, low[...])
    top_ref[...] = top
    grad = dot(output[...], top.astype(BF16)).astype(BF16)
    gt_ref[...] = grad
    g_ref[...] = grad.T


def attend_kernel(
    place,
    pattern,
    s0_ref,
    s1_ref,
    s2_ref,
    s3_ref,
    start_ref,
    inverse_ref,
    top_ref,
    q_ref,
    qt_ref,
    g_ref,
    gt_ref,
    enc,
    gain_ref,
    query_w,
    key_w,
    value_w,
    output_w,
    dec,
    decoded_ref,
    own_ref,
    o1_ref,
    o2_ref,
    o3_ref,
    enc_ref,
    start_s,
    inverse_s,
    keys_s,
    values_s,
    weight_s,
    prob_s,
    score_s,
    mixed_s,
    query_s,
    keyg_s,
    valueg_s,
    rows_s,
):
    node_count = s0_ref.shape[1]
    pieces = (s0_ref, s1_ref, s2_ref, s3_ref)
    key_tiles = len(pieces) * node_count // TILE
    gain = column(gain_ref)
    _, encoder_t = padded(enc, rows_s)
    key_t = key_w[...].T
    value_t = value_w[...].T
    scale = 1.0 / math.sqrt(HEAD)
    for r, piece in enumerate(pieces):
        span = pl.ds(r * node_count, node_count)
        start = dot(encoder_t, piece[...])
        start_s[:, span] = start
        inverse, normed = norm_t(start, gain)
        inverse_s[:, span] = inverse
        keys_s[:, span] = dot(key_t, normed).astype(BF16)
        values_s[:, span] = dot(value_t, normed).astype(BF16)
    first = place[0] * (node_count // TILE)

    def head(h, _):
        rows = pl.ds(pl.multiple_of(h * HEAD, HEAD), HEAD)
        g = g_ref[:, rows]
        kt = keys_s[rows, :]
        vt = values_s[rows, :]
        scores = dot(q_ref[:, rows], kt)
        for qt in range(node_count // TILE):
            for kb in range(key_tiles):
                seen = pattern[qt, lax.rem(first + kb, key_tiles)] > 0
                bias = jnp.where(seen, 0.0, -1e30).astype(F32)
                at = (slice(qt * TILE, (qt + 1) * TILE), slice(kb * TILE, (kb + 1) * TILE))
                weight_s[at] = scores[at] * (scale / math.log(2.0)) + bias
        biased = weight_s[...]
        weights = jnp.exp2(biased - jnp.max(biased, axis=1, keepdims=True))
        probs = weights * (1.0 / jnp.sum(weights, axis=1, keepdims=True))
        weight_s[...] = probs
        prob_s[...] = probs.astype(BF16)
        mixed = dot_nt(prob_s[...], vt)
        mixed_s[rows, :] = mixed.astype(BF16).T
        delta = jnp.sum(mixed * g.astype(F32), axis=1, keepdims=True)
        prob_grad = dot(g, vt)
        score_s[...] = (weight_s[...] * ((prob_grad - delta) * scale)).astype(BF16)
        query_s[rows, :] = dot_nt(score_s[...], kt).astype(BF16).T
        keyg_s[rows, :] = dot(qt_ref[rows, :], score_s[...]).astype(BF16)
        valueg_s[rows, :] = dot(gt_ref[rows, :], prob_s[...]).astype(BF16)
        return 0

    lax.fori_loop(0, HEADS, head, 0)
    final = start_ref[...] + dot(output_w[...].T, mixed_s[...])
    decoder_t, _ = padded(dec, rows_s)
    decoded_ref[...] = dot(decoder_t, final.astype(BF16)).astype(BF16)
    encoder, _ = padded(enc, rows_s)
    total_enc = jnp.zeros(enc_ref.shape, F32)
    for r, (piece, out) in enumerate(zip(pieces, (own_ref, o1_ref, o2_ref, o3_ref))):
        span = pl.ds(r * node_count, node_count)
        grad = dot(key_w[...], keyg_s[:, span]) + dot(value_w[...], valueg_s[:, span])
        if r == 0:
            grad = grad + dot(query_w[...], query_s[...])
            start, inverse = start_ref[...], inverse_ref[...]
        else:
            start, inverse = start_s[:, span], inverse_s[:, span]
        scaled = grad * gain
        mean = jnp.mean(start * scaled, axis=0, keepdims=True)
        total = inverse * scaled - start * (inverse * inverse * inverse * mean)
        if r == 0:
            total = total + top_ref[...]
        total = total.astype(BF16)
        out[...] = dot(encoder, total).astype(out.dtype)
        total_enc = total_enc + dot_nt(piece[...], total)
    enc_ref[...] = total_enc


def picks_of(index, pair, nodes):
    return jnp.concatenate(
        [
            jnp.where(nodes == index[pl.ds(2 * pair + one, 1), :], 1.0, 0.0).astype(BF16)
            for one in range(2)
        ],
        axis=1,
    )


def decoded_slots_kernel(index, decoded_ref, enc_ref, out_ref, whole, extra):
    peers = out_ref.shape[0]
    height = enc_ref.shape[0]
    for t in range(enc_ref.shape[1] // TILE):
        whole[t * height : (t + 1) * height, :] = enc_ref[:, t * TILE : (t + 1) * TILE]
    extra[...] = jnp.zeros_like(extra)
    for j in range(SHARE):
        rows = whole[j * peers : (j + 1) * peers, :]
        high = rows.astype(BF16).astype(F32)
        extra[pl.ds(j, peers, stride=24), :] = high
        extra[pl.ds(SHARE + j, peers, stride=24), :] = rows - high
    nodes = lax.broadcasted_iota(jnp.int32, (decoded_ref.shape[1], TILE), 0)

    def step(pair):
        got = dot(decoded_ref[...], picks_of(index, pair, nodes))
        for one in range(2):
            tail = extra[pl.ds(pl.multiple_of((2 * pair + one) * 24, 8), 24), :]
            rows = jnp.concatenate([got[:, one * TILE : (one + 1) * TILE], tail], axis=0)
            out_ref[2 * pair + one] = rows.astype(BF16)

    loop(peers // 2, 4, step)


def grad_slots_kernel(index, own_ref, i1_ref, i2_ref, i3_ref, out_ref, grad_s):
    total = own_ref[...]
    for piece in (i1_ref, i2_ref, i3_ref):
        total = total + piece[...].astype(F32)
    grad_s[...] = total.astype(BF16)
    nodes = lax.broadcasted_iota(jnp.int32, (own_ref.shape[1], TILE), 0)
    blank = jnp.zeros((out_ref.shape[1] - ROWS, TILE), F32)

    def step(pair):
        got = dot(grad_s[...], picks_of(index, pair, nodes))
        for one in range(2):
            rows = jnp.concatenate([got[:, one * TILE : (one + 1) * TILE], blank], axis=0)
            out_ref[2 * pair + one] = rows.astype(BF16)

    loop(out_ref.shape[0] // 2, 4, step)


def unpack_kernel(back_ref, rank, out_ref, acc):
    peers = back_ref.shape[0]
    acc[...] = jnp.zeros_like(acc)

    def step(pair):
        data = jnp.concatenate([back_ref[2 * pair], back_ref[2 * pair + 1]], axis=1)
        acc[...] += dot(data[:ROWS], slot_onehot(rank, pair))

    loop(peers // 2, 4, step)
    out_ref[...] = acc[0 : out_ref.shape[0], :].astype(out_ref.dtype)


def body(
    grid_state,
    cotangent,
    encoder_weight,
    norm_gain,
    query_weight,
    key_weight,
    value_weight,
    output_weight,
    decoder_weight,
    grid_owner,
    decode_node,
    tile_pattern,
):
    peers = lax.axis_size("wide")
    group = lax.axis_size("patch")
    variables, grid_count = grid_state.shape
    width = query_weight.shape[0]
    nodes = tile_pattern.shape[0] * TILE
    keys = group * nodes
    capacity = 2 * grid_count // peers
    shift = (nodes * group).bit_length() - 1
    vm = pltpu.VMEM

    route = 2 * ROWS * grid_count * peers * capacity
    spread = 2 * ROWS * nodes * peers * capacity

    def exchange(x):
        return lax.all_to_all(x, "wide", split_axis=0, concat_axis=0, tiled=True)

    def pack(x, index):
        return call(
            functools.partial(pack_kernel, shift, nodes - 1),
            [((peers, ROWS, capacity), BF16), ((peers, grid_count), F32)],
            [vm((ROWS, grid_count), F32), vm((ROWS, grid_count), BF16)],
            "pack",
            route,
            x,
            index.reshape(1, grid_count),
        )

    def sums(recv):
        return call(
            functools.partial(sums_kernel, variables),
            [((ROWS, nodes), BF16), ((ROWS, nodes), BF16), ((peers, capacity), jnp.int32)],
            [vm((ROWS, nodes), F32)],
            "sums",
            spread,
            recv,
        )

    def unpack(x, rank, dtype):
        return call(
            unpack_kernel,
            [((variables, grid_count), dtype)],
            [vm((ROWS, grid_count), F32)],
            "unpack",
            route,
            x,
            rank,
        )[0]

    def from_ahead(x, r):
        return lax.ppermute(x, "patch", [((i + r) % group, i) for i in range(group)])

    def to_ahead(x, r):
        return lax.ppermute(x, "patch", [(i, (i + r) % group) for i in range(group)])

    place = lax.axis_index("patch").reshape(1).astype(jnp.int32)
    gain = norm_gain.reshape(1, width)
    decoder_rows = decoder_weight.T

    state_send, own_rank = pack(grid_state, grid_owner)
    cotangent, state_send = lax.optimization_barrier((cotangent, state_send))
    state_recv = exchange(state_send)
    cot_send, dec_rank = pack(cotangent, decode_node)
    cot_recv = exchange(cot_send)

    state, state_low, own_idx = sums(state_recv)
    pieces = [state] + [from_ahead(state, r) for r in range(1, group)]
    square = ((width, nodes), BF16)
    start, inverse, q, qt = call(
        query_kernel,
        [((width, nodes), F32), ((1, nodes), F32), square, square],
        [vm((TILE, width), F32)],
        "query",
        3 * width * width * nodes,
        state,
        state_low,
        encoder_weight,
        gain,
        query_weight,
    )
    cot, cot_low, dec_idx = sums(cot_recv)
    top, g, gt = call(
        top_kernel,
        [((width, nodes), F32), square, square],
        [vm((TILE, width), F32)],
        "top",
        3 * width * width * nodes,
        cot,
        cot_low,
        decoder_rows,
        output_weight,
    )
    decoded, own, o1, o2, o3, enc = call(
        attend_kernel,
        [((ROWS, nodes), BF16), ((ROWS, nodes), F32)]
        + [((ROWS, nodes), BF16)] * 3
        + [((ROWS, width), F32)],
        [
            vm((width, keys), F32),
            vm((1, keys), F32),
            vm((width, keys), BF16),
            vm((width, keys), BF16),
            vm((nodes, keys), F32),
            vm((nodes, keys), BF16),
            vm((nodes, keys), BF16),
            vm((width, nodes), BF16),
            vm((width, nodes), BF16),
            vm((width, keys), BF16),
            vm((width, keys), BF16),
            vm((TILE, width), F32),
        ],
        "attend",
        20 * nodes * keys * width,
        place,
        tile_pattern,
        *pieces,
        start,
        inverse,
        top,
        q,
        qt,
        g,
        gt,
        encoder_weight,
        gain,
        query_weight,
        key_weight,
        value_weight,
        output_weight,
        decoder_rows,
        smem=(0, 1),
        limit=ATTEND_LIMIT,
    )
    back = [to_ahead(o, r) for r, o in ((1, o1), (2, o2), (3, o3))]
    (decoded_send,) = call(
        decoded_slots_kernel,
        [((peers, ROWS + 24, capacity), BF16)],
        [vm((peers * SHARE, TILE), F32), vm((peers * 24, TILE), F32)],
        "decoded_slots",
        spread,
        dec_idx,
        decoded,
        enc,
    )
    decoded_back = exchange(decoded_send)
    (grad_send,) = call(
        grad_slots_kernel,
        [((peers, ROWS + 8, capacity), BF16)],
        [vm((ROWS, nodes), BF16)],
        "grad_slots",
        spread,
        own_idx,
        own,
        *back,
    )
    chunk = jnp.sum(decoded_back[:, ROWS : ROWS + 2 * SHARE].astype(F32), axis=0)
    chunk = (chunk[:SHARE] + chunk[SHARE:]).astype(BF16)
    span = slice(variables, variables + SHARE)
    grad_send = grad_send.at[:, span].set(jnp.broadcast_to(chunk, (peers,) + chunk.shape))
    grad_back = exchange(grad_send)
    denoised = unpack(decoded_back, dec_rank, BF16)
    grad_back, denoised = lax.optimization_barrier((grad_back, denoised))
    mine = jnp.swapaxes(grad_back[:, span], 0, 1).reshape(peers * SHARE, TILE)
    parts = [mine] + [from_ahead(mine, r) for r in range(1, group)]
    state_grad = unpack(grad_back, own_rank, F32)
    whole = sum(p.astype(F32) for p in parts).reshape(width // TILE, ROWS, TILE)
    encoder_grad = jnp.swapaxes(whole, 0, 1).reshape(ROWS, width)[:variables]
    return (denoised, state_grad, encoder_grad)


def solution(mesh):
    in_specs = (
        P(None, ("wide", "patch")),
        P(None, ("wide", "patch")),
        P(),
        P(),
        P(),
        P(),
        P(),
        P(),
        P(),
        P(("wide", "patch")),
        P(("wide", "patch")),
        P(("wide", "patch"), None),
    )
    out_specs = (P(None, ("wide", "patch")), P(None, ("wide", "patch")), P())
    return jax.shard_map(body, mesh=mesh, in_specs=in_specs, out_specs=out_specs, check_vma=False)
```

time: 176 us -> 134 us (0.76)
  waiting for transfers between devices: 52.1 us -> 31.8 us
  Pallas kernels: 72.1 us -> 57.6 us
  local copies, waits for them, and re-layouts: 12.1 us -> 5.67 us
    ppermute x5 -> x0, waiting for transfers between devices: 17.3 us -> none  [body(): lax.ppermute(mine, 'wide', [(i, i ^ step) for i in range(peers)])]
    pallas_call x6 -> x11, Pallas kernels: 72.1 us -> 57.6 us  [call(): pl.pallas_call(kernel, out_shape=[jax.ShapeDtypeStruct(s, d) for s, d in...]
    ppermute x5 -> x0, starting transfers between devices: 9.15 us -> none  [body(): lax.ppermute(mine, 'wide', [(i, i ^ step) for i in range(peers)])]
    all_to_all x2 -> x4, starting transfers between devices: 12.7 us -> 20.3 us  [exchange(): return lax.all_to_all(x, 'wide', split_axis=0, concat_axis=0, tiled=True)]
    all_to_all x2 -> x4, waiting for transfers between devices: 20.8 us -> 28 us  [exchange(): return lax.all_to_all(x, 'wide', split_axis=0, concat_axis=0, tiled=True)]
    ppermute x6 -> x3, waiting for transfers between devices: 9 us -> 3.16 us  [to_ahead(): lax.ppermute(x, 'patch', [(i, (i + r) % group) for i in range(group)])]
    ppermute x6, waiting for transfers between devices: 5.03 us -> 0.67 us  [from_ahead(): lax.ppermute(x, 'patch', [((i + r) % group, i) for i in range(group)])]
    unnamed x41 -> x26, local copies, waits for them, and re-layouts: 7.97 us -> 3.84 us
  transfers between devices with their start and end apart: 19 -> 13, of which waited for: 15 -> 7; matrix products, arithmetic and copies ran while one was open for 5% -> 0% of each run, Pallas kernels for 3% -> 17%
where the time goes in v2:
time: 134 us; the launch traced here: 133 us
  Pallas kernels  57.6 us (43%)
  starting transfers between devices  36.9 us (28%)
  waiting for transfers between devices  31.8 us (24%)
  local copies, waits for them, and re-layouts  5.67 us (4%)
    pallas_call x11, Pallas kernels, call(): pl.pallas_call(kernel, out_shape=[jax.ShapeDtypeStruct(s, d) for s, d in...  57.6 us
    all_to_all x4, waiting for transfers between devices, exchange(): return lax.all_to_all(x, 'wide', split_axis=0, concat_axis=0, tiled=True)  28 us
    all_to_all x4, starting transfers between devices, exchange(): return lax.all_to_all(x, 'wide', split_axis=0, concat_axis=0, tiled=True)  20.3 us
    ppermute x6, starting transfers between devices, from_ahead(): lax.ppermute(x, 'patch', [((i + r) % group, i) for i in range(group)])  10.9 us
    ppermute x3, starting transfers between devices, to_ahead(): lax.ppermute(x, 'patch', [(i, (i + r) % group) for i in range(group)])  5.73 us
    unnamed x26, local copies, waits for them, and re-layouts  3.84 us
    ppermute x3, waiting for transfers between devices, to_ahead(): lax.ppermute(x, 'patch', [(i, (i + r) % group) for i in range(group)])  3.16 us
  transfers between devices with their start and end apart: 13, of which 7 were waited for; matrix products, arithmetic and copies ran while one was open for 0% of the time, Pallas kernels for 17%

profile of v2, /device:TPU:0, one launch (start us, length us, event | category | flops | bytes accessed | tf_op | source)
XLA Modules:
  0.0 133.0 jit_solution(13854886947489514483)
XLA Ops:
  0.6 0.0 copy-start.4
  0.6 1.0 copy-done.4
  1.6 0.0 copy-start.8
  1.6 0.7 copy-done.8
  2.3 6.8 %pack.2 = (bf16[32,88,128]{2,1,0:T(8,128)(2,1)}, f32[32,2048]{1,0:T(8,128)S(1)}) custom-call(bf16[84,2048]{1,0:T(8,128)(2,1)S(1)} %copy-done.4, s32[1,2048]{1,0:T(1,128)S(1)} %bitcast.17), custom_call_target="tpu_custom_call" | custom-call | flops 1476395008 | bytes 1048576 | tf_op jit(solution)/shard_map/pack/pallas_call | solution.py:39
  9.1 0.0 copy-start.5
  9.1 0.0 copy-start.9
  9.1 8.6 %all-to-all-start = ((bf16[32,88,128]{2,1,0:T(8,128)(2,1)}), bf16[32,88,128]{2,1,0:T(8,128)(2,1)S(1)}, u32[]{:S(2)}, u32[]{:S(2)}) async-start(bf16[32,88,128]{2,1,0:T(8,128)(2,1)} %get-tuple-element.43), calls=%async_computation | async-start | bytes 1441792 | tf_op jit(solution)/shard_map/all_to_all | solution.py:362
  17.7 0.0 copy-done.5
  17.7 0.0 copy-done.9
  17.7 6.8 %pack.3 = (bf16[32,88,128]{2,1,0:T(8,128)(2,1)}, f32[32,2048]{1,0:T(8,128)S(1)}) custom-call(bf16[84,2048]{1,0:T(8,128)(2,1)S(1)} %copy-done.5, s32[1,2048]{1,0:T(1,128)S(1)} %bitcast.18), custom_call_target="tpu_custom_call" | custom-call | flops 1476395008 | bytes 1048576 | tf_op jit(solution)/shard_map/pack/pallas_call | solution.py:39
  24.5 7.1 %all-to-all-done.recv_ref = bf16[32,88,128]{2,1,0:T(8,128)(2,1)S(1)} async-done(((bf16[32,88,128]{2,1,0:T(8,128)(2,1)}), bf16[32,88,128]{2,1,0:T(8,128)(2,1)S(1)}, u32[]{:S(2)}, u32[]{:S(2)}) %all-to-all-start) | async-done | bytes 720928 | tf_op jit(solution)/shard_map/all_to_all | solution.py:362
  31.6 3.9 %all-to-all-start.1 = ((bf16[32,88,128]{2,1,0:T(8,128)(2,1)}), bf16[32,88,128]{2,1,0:T(8,128)(2,1)S(1)}, u32[]{:S(2)}, u32[]{:S(2)}) async-start(bf16[32,88,128]{2,1,0:T(8,128)(2,1)} %get-tuple-element.50), calls=%async_computation.1 | async-start | bytes 1441792 | tf_op jit(solution)/shard_map/all_to_all | solution.py:362
  35.5 0.0 copy-start.11
  35.5 0.7 copy-done.11
  36.2 1.9 %sums.2 = (bf16[88,512]{1,0:T(8,128)(2,1)S(1)}, bf16[88,512]{1,0:T(8,128)(2,1)S(1)}, s32[32,128]{1,0:T(8,128)S(1)}) custom-call(bf16[32,88,128]{2,1,0:T(8,128)(2,1)S(1)} %all-to-all-done.recv_ref), custom_call_target="tpu_custom_call" | custom-call | flops 369098752 | bytes 1048576 | tf_op jit(solution)/shard_map/sums/pallas_call | solution.py:39
  38.1 0.0 copy-start.1
  38.1 0.0 copy-start.7
  38.1 1.6 %collective-permute-start.2 = (bf16[88,512]{1,0:T(8,128)(2,1)S(1)}, bf16[88,512]{1,0:T(8,128)(2,1)S(1)}, u32[]{:S(2)}, u32[]{:S(2)}) collective-permute-start(bf16[88,512]{1,0:T(8,128)(2,1)S(1)} %get-tuple-element.45.high.s0_ref), channel_id=1, source_target_pairs={{3,0},{0,1},{1,2},{2,3},{7,4},{4,5},{5,6},{6,7},{11,8},{8,9},{9,10... | collective-permute-start | bytes 270344 | tf_op jit(solution)/shard_map/ppermute | solution.py:397
  39.7 2.7 %collective-permute-start.1 = (bf16[88,512]{1,0:T(8,128)(2,1)S(1)}, bf16[88,512]{1,0:T(8,128)(2,1)S(1)}, u32[]{:S(2)}, u32[]{:S(2)}) collective-permute-start(bf16[88,512]{1,0:T(8,128)(2,1)S(1)} %get-tuple-element.45.high.s0_ref), channel_id=1, source_target_pairs={{2,0},{3,1},{0,2},{1,3},{6,4},{7,5},{4,6},{5,7},{10,8},{11,9},{8,1... | collective-permute-start | bytes 270344 | tf_op jit(solution)/shard_map/ppermute | solution.py:397
  42.4 1.4 %collective-permute-start = (bf16[88,512]{1,0:T(8,128)(2,1)S(1)}, bf16[88,512]{1,0:T(8,128)(2,1)S(1)}, u32[]{:S(2)}, u32[]{:S(2)}) collective-permute-start(bf16[88,512]{1,0:T(8,128)(2,1)S(1)} %get-tuple-element.45.high.s0_ref), channel_id=1, source_target_pairs={{1,0},{2,1},{3,2},{0,3},{5,4},{6,5},{7,6},{4,7},{9,8},{10,9},{11,1... | collective-permute-start | bytes 270344 | tf_op jit(solution)/shard_map/ppermute | solution.py:397
  43.8 5.6 %all-to-all-done.1.recv_ref = bf16[32,88,128]{2,1,0:T(8,128)(2,1)S(1)} async-done(((bf16[32,88,128]{2,1,0:T(8,128)(2,1)}), bf16[32,88,128]{2,1,0:T(8,128)(2,1)S(1)}, u32[]{:S(2)}, u32[]{:S(2)}) %all-to-all-start.1) | async-done | bytes 720928 | tf_op jit(solution)/shard_map/all_to_all | solution.py:362
  49.4 1.9 %sums.3 = (bf16[88,512]{1,0:T(8,128)(2,1)S(1)}, bf16[88,512]{1,0:T(8,128)(2,1)S(1)}, s32[32,128]{1,0:T(8,128)S(1)}) custom-call(bf16[32,88,128]{2,1,0:T(8,128)(2,1)S(1)} %all-to-all-done.1.recv_ref), custom_call_target="tpu_custom_call" | custom-call | flops 369098752 | bytes 1048576 | tf_op jit(solution)/shard_map/sums/pallas_call | solution.py:39
  51.3 0.0 copy-done.1
  51.3 0.0 copy-done.7
  51.3 0.0 copy-start
  51.3 0.0 copy-start.6
  51.3 0.9 top.1
  52.3 0.1 copy-done
  52.3 0.0 copy-done.6
  52.3 0.0 copy-start.2
  52.3 0.0 copy-start.3
  52.4 1.2 query.1
  53.6 0.0 collective-permute-done.2.s3_ref
  53.6 0.0 collective-permute-done.1.s2_ref
  53.6 0.0 collective-permute-done.s1_ref
  53.6 0.0 copy-start.10
  53.6 0.0 copy-done.2
  53.6 0.0 copy-done.3
  53.6 0.7 copy-done.10
  54.3 25.4 %attend.1 = (bf16[88,512]{1,0:T(8,128)(2,1)S(1)}, f32[88,512]{1,0:T(8,128)S(1)}, bf16[88,512]{1,0:T(8,128)(2,1)S(1)}, bf16[88,512]{1,0:T(8,128)(2,1)S(1)}, bf16[...) custom-call(s32[1]{0:T(128)} %bitcast.1.place, s32[4,16]{1,0:T(4,128)S(1)} %copy-done.10, ...), custom_call_target="tpu_custom_call" | custom-call | flops 10737418240 | bytes 1048576 | tf_op jit(solution)/shard_map/attend/pallas_call | solution.py:39
  79.7 2.3 %decoded_slots.1 = bf16[32,112,128]{2,1,0:T(8,128)(2,1)} custom-call(s32[32,128]{1,0:T(8,128)S(1)} %get-tuple-element.62.index, bf16[88,512]{1,0:T(8,128)(2,1)S(1)} %get-tuple-element.63.decoded_ref, f32[88,512]{1,0:T(8,128)S(1)} %get-tuple-element.64.enc_ref), custom_call_target="tpu_custom_call" | custom-call | flops 369098752 | bytes 1048576 | tf_op jit(solution)/shard_map/decoded_slots/pallas_call | solution.py:39
  82.0 3.9 %all-to-all-start.2 = ((bf16[32,112,128]{2,1,0:T(8,128)(2,1)}), bf16[32,112,128]{2,1,0:T(8,128)(2,1)S(1)}, u32[]{:S(2)}, u32[]{:S(2)}) async-start(bf16[32,112,128]{2,1,0:T(8,128)(2,1)} %decoded_slots.1), calls=%async_computation.2 | async-start | bytes 1835008 | tf_op jit(solution)/shard_map/all_to_all | solution.py:362
  85.9 1.6 %collective-permute-start.3 = (bf16[88,512]{1,0:T(8,128)(2,1)S(1)}, bf16[88,512]{1,0:T(8,128)(2,1)S(1)}, u32[]{:S(2)}, u32[]{:S(2)}) collective-permute-start(bf16[88,512]{1,0:T(8,128)(2,1)S(1)} %get-tuple-element.59), channel_id=1, source_target_pairs={{0,1},{1,2},{2,3},{3,0},{4,5},{5,6},{6,7},{7,4},{8,9},{9,10},{10,1... | collective-permute-start | bytes 270344 | tf_op jit(solution)/shard_map/ppermute | solution.py:400
  87.5 2.7 %collective-permute-start.4 = (bf16[88,512]{1,0:T(8,128)(2,1)S(1)}, bf16[88,512]{1,0:T(8,128)(2,1)S(1)}, u32[]{:S(2)}, u32[]{:S(2)}) collective-permute-start(bf16[88,512]{1,0:T(8,128)(2,1)S(1)} %get-tuple-element.60), channel_id=1, source_target_pairs={{0,2},{1,3},{2,0},{3,1},{4,6},{5,7},{6,4},{7,5},{8,10},{9,11},{10,... | collective-permute-start | bytes 270344 | tf_op jit(solution)/shard_map/ppermute | solution.py:400
  90.2 1.4 %collective-permute-start.5 = (bf16[88,512]{1,0:T(8,128)(2,1)S(1)}, bf16[88,512]{1,0:T(8,128)(2,1)S(1)}, u32[]{:S(2)}, u32[]{:S(2)}) collective-permute-start(bf16[88,512]{1,0:T(8,128)(2,1)S(1)} %get-tuple-element.61), channel_id=1, source_target_pairs={{0,3},{1,0},{2,1},{3,2},{4,7},{5,4},{6,5},{7,6},{8,11},{9,8},{10,9... | collective-permute-start | bytes 270344 | tf_op jit(solution)/shard_map/ppermute | solution.py:400
  91.7 0.2 collective-permute-done.3.i1_ref
  91.9 2.9 %collective-permute-done.4.i2_ref = bf16[88,512]{1,0:T(8,128)(2,1)S(1)} collective-permute-done((bf16[88,512]{1,0:T(8,128)(2,1)S(1)}, bf16[88,512]{1,0:T(8,128)(2,1)S(1)}, u32[]{:S(2)}, u32[]{:S(2)}) %collective-permute-start.4) | collective-permute-done | bytes 90144 | tf_op jit(solution)/shard_map/ppermute | solution.py:400
  94.8 0.0 collective-permute-done.5.i3_ref
  94.8 2.2 %grad_slots.1 = bf16[32,96,128]{2,1,0:T(8,128)(2,1)} custom-call(s32[32,128]{1,0:T(8,128)S(1)} %get-tuple-element.44.index, f32[88,512]{1,0:T(8,128)S(1)} %get-tuple-element.58.own_ref, bf16[88,512]{1,0:T(8,128)(2,1)S(1)} %collective-permute-done.3.i1_ref, bf16[88,512]{1,0:T(8,128)(2,1)S(1)} %collective-permute-done.4.i2_ref, ...), custom_call_target="tpu_custom_call" | custom-call | flops 369098752 | bytes 1048576 | tf_op jit(solution)/shard_map/grad_slots/pallas_call | solution.py:39
  97.0 4.8 %all-to-all-done.2.back_ref = bf16[32,112,128]{2,1,0:T(8,128)(2,1)S(1)} async-done(((bf16[32,112,128]{2,1,0:T(8,128)(2,1)}), bf16[32,112,128]{2,1,0:T(8,128)(2,1)S(1)}, u32[]{:S(2)}, u32[]{:S(2)}) %all-to-all-start.2) | async-done | bytes 917536 | tf_op jit(solution)/shard_map/all_to_all | solution.py:362
  101.9 1.7 %scatter.4 = bf16[32,96,128]{2,1,0:T(8,128)(2,1)} dynamic-update-slice(bf16[32,96,128]{2,1,0:T(8,128)(2,1)} %grad_slots.1, bf16[32,11,128]{2,1,0:T(8,128)(2,1)S(1)} %broadcast.21, s32[]{:T(128)} %constant.33.clone.1, s32[]{:T(128)} %constant.34.clone.1, s32[]{:T(128)} %constant.33.clone.1) | dynamic-update-slice | bytes 180228 | tf_op jit(solution)/shard_map/scatter | solution.py:505
  103.6 3.9 %all-to-all-start.3 = ((bf16[32,96,128]{2,1,0:T(8,128)(2,1)}), bf16[32,96,128]{2,1,0:T(8,128)(2,1)S(1)}, u32[]{:S(2)}, u32[]{:S(2)}) async-start(bf16[32,96,128]{2,1,0:T(8,128)(2,1)} %scatter.4), calls=%async_computation.3 | async-start | bytes 1572864 | tf_op jit(solution)/shard_map/all_to_all | solution.py:362
  107.5 4.0 %unpack.2 = bf16[84,2048]{1,0:T(8,128)(2,1)} custom-call(bf16[32,112,128]{2,1,0:T(8,128)(2,1)S(1)} %all-to-all-done.2.back_ref, f32[32,2048]{1,0:T(8,128)S(1)} %get-tuple-element.65.rank), custom_call_target="tpu_custom_call" | custom-call | flops 1476395008 | bytes 1048576 | tf_op jit(solution)/shard_map/unpack/pallas_call | solution.py:39
  111.6 10.5 %all-to-all-done.3.back_ref = bf16[32,96,128]{2,1,0:T(8,128)(2,1)S(1)} async-done(((bf16[32,96,128]{2,1,0:T(8,128)(2,1)}), bf16[32,96,128]{2,1,0:T(8,128)(2,1)S(1)}, u32[]{:S(2)}, u32[]{:S(2)}) %all-to-all-start.3) | async-done | bytes 786464 | tf_op jit(solution)/shard_map/all_to_all | solution.py:362
  122.2 3.1 %collective-permute-start.7 = (bf16[352,128]{1,0:T(8,128)(2,1)S(1)}, bf16[352,128]{1,0:T(8,128)(2,1)S(1)}, u32[]{:S(2)}, u32[]{:S(2)}) collective-permute-start(bf16[352,128]{1,0:T(8,128)(2,1)S(1)} %bitcast.21), channel_id=1, source_target_pairs={{2,0},{3,1},{0,2},{1,3},{6,4},{7,5},{4,6},{5,7},{10,8},{11,9},{8,1... | collective-permute-start | bytes 270344 | tf_op jit(solution)/shard_map/ppermute | solution.py:397
  125.3 1.1 collective-permute-start.6
  126.4 0.9 collective-permute-start.8
  127.3 4.2 %unpack.3 = f32[84,2048]{1,0:T(8,128)} custom-call(bf16[32,96,128]{2,1,0:T(8,128)(2,1)S(1)} %all-to-all-done.3.back_ref, f32[32,2048]{1,0:T(8,128)S(1)} %get-tuple-element.68.rank), custom_call_target="tpu_custom_call" | custom-call | flops 1476395008 | bytes 1048576 | tf_op jit(solution)/shard_map/unpack/pallas_call | solution.py:39
  131.5 0.0 collective-permute-done.7
  131.5 0.0 collective-permute-done.6
  131.5 0.7 collective-permute-done.8
  132.2 0.1 convert_add_fusion
  132.3 0.7 copy.18
  (8 shorter events, 0.2 us)
Async XLA Ops:
  0.6 1.0 copy-start.4
  1.6 0.7 copy-start.8
  9.1 8.6 %copy-start.5 = (bf16[84,2048]{1,0:T(8,128)(2,1)S(1)}, bf16[84,2048]{1,0:T(8,128)(2,1)}, u32[]{:S(2)}) copy-start(bf16[84,2048]{1,0:T(8,128)(2,1)} %x_ref.2) | copy-start | bytes 1032196
  9.1 8.6 %copy-start.9 = (s32[2048]{0:T(1024)S(1)}, s32[2048]{0:T(1024)}, u32[]{:S(2)}) copy-start(s32[2048]{0:T(1024)} %param.24) | copy-start | bytes 24580
  9.1 22.5 %all-to-all-start = ((bf16[32,88,128]{2,1,0:T(8,128)(2,1)}), bf16[32,88,128]{2,1,0:T(8,128)(2,1)S(1)}, u32[]{:S(2)}, u32[]{:S(2)}) async-start(bf16[32,88,128]{2,1,0:T(8,128)(2,1)} %get-tuple-element.43), calls=%async_computation | async-start | bytes 1441792 | tf_op jit(solution)/shard_map/all_to_all | solution.py:362
  31.6 17.8 %all-to-all-start.1 = ((bf16[32,88,128]{2,1,0:T(8,128)(2,1)}), bf16[32,88,128]{2,1,0:T(8,128)(2,1)S(1)}, u32[]{:S(2)}, u32[]{:S(2)}) async-start(bf16[32,88,128]{2,1,0:T(8,128)(2,1)} %get-tuple-element.50), calls=%async_computation.1 | async-start | bytes 1441792 | tf_op jit(solution)/shard_map/all_to_all | solution.py:362
  35.5 0.7 copy-start.11
  38.1 13.2 %copy-start.1 = (bf16[512,512]{1,0:T(8,128)(2,1)S(1)}, bf16[512,512]{1,0:T(8,128)(2,1)}, u32[]{:S(2)}) copy-start(bf16[512,512]{1,0:T(8,128)(2,1)} %output_w.1) | copy-start | bytes 1572868
  38.1 13.2 %copy-start.7 = (bf16[512,84]{0,1:T(8,128)(2,1)S(1)}, bf16[512,84]{0,1:T(8,128)(2,1)}, u32[]{:S(2)}) copy-start(bf16[512,84]{0,1:T(8,128)(2,1)} %param.22) | copy-start | bytes 258052
  38.1 15.5 %collective-permute-start.2 = (bf16[88,512]{1,0:T(8,128)(2,1)S(1)}, bf16[88,512]{1,0:T(8,128)(2,1)S(1)}, u32[]{:S(2)}, u32[]{:S(2)}) collective-permute-start(bf16[88,512]{1,0:T(8,128)(2,1)S(1)} %get-tuple-element.45.high.s0_ref), channel_id=1, source_target_pairs={{3,0},{0,1},{1,2},{2,3},{7,4},{4,5},{5,6},{6,7},{11,8},{8,9},{9,10... | collective-permute-start | bytes 270344 | tf_op jit(solution)/shard_map/ppermute | solution.py:397
  39.7 13.9 %collective-permute-start.1 = (bf16[88,512]{1,0:T(8,128)(2,1)S(1)}, bf16[88,512]{1,0:T(8,128)(2,1)S(1)}, u32[]{:S(2)}, u32[]{:S(2)}) collective-permute-start(bf16[88,512]{1,0:T(8,128)(2,1)S(1)} %get-tuple-element.45.high.s0_ref), channel_id=1, source_target_pairs={{2,0},{3,1},{0,2},{1,3},{6,4},{7,5},{4,6},{5,7},{10,8},{11,9},{8,1... | collective-permute-start | bytes 270344 | tf_op jit(solution)/shard_map/ppermute | solution.py:397
  42.4 11.2 %collective-permute-start = (bf16[88,512]{1,0:T(8,128)(2,1)S(1)}, bf16[88,512]{1,0:T(8,128)(2,1)S(1)}, u32[]{:S(2)}, u32[]{:S(2)}) collective-permute-start(bf16[88,512]{1,0:T(8,128)(2,1)S(1)} %get-tuple-element.45.high.s0_ref), channel_id=1, source_target_pairs={{1,0},{2,1},{3,2},{0,3},{5,4},{6,5},{7,6},{4,7},{9,8},{10,9},{11,1... | collective-permute-start | bytes 270344 | tf_op jit(solution)/shard_map/ppermute | solution.py:397
  51.3 1.0 copy-start
  51.3 1.0 copy-start.6
  52.3 1.3 copy-start.2
  52.3 1.3 copy-start.3
  53.6 0.7 copy-start.10
  82.0 19.9 %all-to-all-start.2 = ((bf16[32,112,128]{2,1,0:T(8,128)(2,1)}), bf16[32,112,128]{2,1,0:T(8,128)(2,1)S(1)}, u32[]{:S(2)}, u32[]{:S(2)}) async-start(bf16[32,112,128]{2,1,0:T(8,128)(2,1)} %decoded_slots.1), calls=%async_computation.2 | async-start | bytes 1835008 | tf_op jit(solution)/shard_map/all_to_all | solution.py:362
  85.9 6.0 %collective-permute-start.3 = (bf16[88,512]{1,0:T(8,128)(2,1)S(1)}, bf16[88,512]{1,0:T(8,128)(2,1)S(1)}, u32[]{:S(2)}, u32[]{:S(2)}) collective-permute-start(bf16[88,512]{1,0:T(8,128)(2,1)S(1)} %get-tuple-element.59), channel_id=1, source_target_pairs={{0,1},{1,2},{2,3},{3,0},{4,5},{5,6},{6,7},{7,4},{8,9},{9,10},{10,1... | collective-permute-start | bytes 270344 | tf_op jit(solution)/shard_map/ppermute | solution.py:400
  87.5 7.3 %collective-permute-start.4 = (bf16[88,512]{1,0:T(8,128)(2,1)S(1)}, bf16[88,512]{1,0:T(8,128)(2,1)S(1)}, u32[]{:S(2)}, u32[]{:S(2)}) collective-permute-start(bf16[88,512]{1,0:T(8,128)(2,1)S(1)} %get-tuple-element.60), channel_id=1, source_target_pairs={{0,2},{1,3},{2,0},{3,1},{4,6},{5,7},{6,4},{7,5},{8,10},{9,11},{10,... | collective-permute-start | bytes 270344 | tf_op jit(solution)/shard_map/ppermute | solution.py:400
  90.2 4.6 %collective-permute-start.5 = (bf16[88,512]{1,0:T(8,128)(2,1)S(1)}, bf16[88,512]{1,0:T(8,128)(2,1)S(1)}, u32[]{:S(2)}, u32[]{:S(2)}) collective-permute-start(bf16[88,512]{1,0:T(8,128)(2,1)S(1)} %get-tuple-element.61), channel_id=1, source_target_pairs={{0,3},{1,0},{2,1},{3,2},{4,7},{5,4},{6,5},{7,6},{8,11},{9,8},{10,9... | collective-permute-start | bytes 270344 | tf_op jit(solution)/shard_map/ppermute | solution.py:400
  103.6 18.5 %all-to-all-start.3 = ((bf16[32,96,128]{2,1,0:T(8,128)(2,1)}), bf16[32,96,128]{2,1,0:T(8,128)(2,1)S(1)}, u32[]{:S(2)}, u32[]{:S(2)}) async-start(bf16[32,96,128]{2,1,0:T(8,128)(2,1)} %scatter.4), calls=%async_computation.3 | async-start | bytes 1572864 | tf_op jit(solution)/shard_map/all_to_all | solution.py:362
  122.2 9.3 %collective-permute-start.7 = (bf16[352,128]{1,0:T(8,128)(2,1)S(1)}, bf16[352,128]{1,0:T(8,128)(2,1)S(1)}, u32[]{:S(2)}, u32[]{:S(2)}) collective-permute-start(bf16[352,128]{1,0:T(8,128)(2,1)S(1)} %bitcast.21), channel_id=1, source_target_pairs={{2,0},{3,1},{0,2},{1,3},{6,4},{7,5},{4,6},{5,7},{10,8},{11,9},{8,1... | collective-permute-start | bytes 270344 | tf_op jit(solution)/shard_map/ppermute | solution.py:397
  125.3 6.2 %collective-permute-start.6 = (bf16[352,128]{1,0:T(8,128)(2,1)S(1)}, bf16[352,128]{1,0:T(8,128)(2,1)S(1)}, u32[]{:S(2)}, u32[]{:S(2)}) collective-permute-start(bf16[352,128]{1,0:T(8,128)(2,1)S(1)} %bitcast.22), channel_id=1, source_target_pairs={{1,0},{2,1},{3,2},{0,3},{5,4},{6,5},{7,6},{4,7},{9,8},{10,9},{11,1... | collective-permute-start | bytes 270344 | tf_op jit(solution)/shard_map/ppermute | solution.py:397
  126.4 5.7 %collective-permute-start.8 = (bf16[352,128]{1,0:T(8,128)(2,1)S(1)}, bf16[352,128]{1,0:T(8,128)(2,1)S(1)}, u32[]{:S(2)}, u32[]{:S(2)}) collective-permute-start(bf16[352,128]{1,0:T(8,128)(2,1)S(1)} %bitcast.23), channel_id=1, source_target_pairs={{3,0},{0,1},{1,2},{2,3},{7,4},{4,5},{5,6},{6,7},{11,8},{8,9},{9,10... | collective-permute-start | bytes 270344 | tf_op jit(solution)/shard_map/ppermute | solution.py:397

commit v3 on v2

--- a/solution.py
+++ b/solution.py
@@ -15,7 +15,7 @@
 F32 = jnp.float32
 BF16 = jnp.bfloat16
 MIB = 1024 * 1024
-ATTEND_LIMIT = 28
+ATTEND_LIMIT = 38
 SHARE = 11
 
 
@@ -48,14 +48,18 @@
     )(*args)
 
 
-def slot_onehot(rank_ref, pair):
-    grid_count = rank_ref.shape[1]
-    level = lax.broadcasted_iota(jnp.int32, (TILE, grid_count), 0).astype(F32).astype(BF16)
+def slot_targets(route):
+    level = lax.broadcasted_iota(jnp.int32, (TILE, route.shape[1]), 0).astype(F32).astype(BF16)
+    rank, target = route[0:1, :].astype(BF16), route[1:2, :].astype(BF16)
+    return jnp.where(level == rank, target, jnp.full((), -1.0, BF16))
+
+
+def slot_onehot(targets, pair, axis):
     parts = []
     for k in range(2):
-        row = rank_ref[pl.ds(2 * pair + k, 1), :].astype(BF16)
-        parts.append(jnp.where(level == row, jnp.ones((), BF16), jnp.zeros((), BF16)))
-    return jnp.concatenate(parts, axis=0)
+        peer = (jnp.zeros((1, targets.shape[1]), F32) + (2 * pair + k).astype(F32)).astype(BF16)
+        parts.append(jnp.where(targets[...] == peer, jnp.ones((), BF16), jnp.zeros((), BF16)))
+    return jnp.concatenate(parts, axis=axis)
 
 
 def loop(count, unroll, step):
@@ -67,7 +71,7 @@
     lax.fori_loop(0, count // unroll, some, 0)
 
 
-def pack_kernel(shift, mask, x_ref, index, out_ref, rank, wide_s, pay):
+def pack_kernel(shift, mask, x_ref, index, out_ref, route, wide_s, pay, targets):
     variables, grid_count = x_ref.shape
     peers = out_ref.shape[0]
     chunk = 256
@@ -84,7 +88,8 @@
         hit = lax.broadcasted_iota(jnp.int32, (peers, chunk), 0) == (nodes >> shift)
         ones = jnp.where(hit, 1.0, 0.0)
         before = dot(ones.astype(BF16), upper) + carry
-        rank[:, span] = jnp.where(hit, before, -1.0)
+        route[0:1, span] = jnp.sum(jnp.where(hit, before, 0.0), axis=0, keepdims=True)
+        route[1:2, span] = (nodes >> shift).astype(F32)
         carry = carry + jnp.sum(ones, axis=1, keepdims=True)
     local = index[...] & mask
     wide_s[0:variables, :] = x_ref[...].astype(F32)
@@ -92,9 +97,10 @@
     wide_s[variables + 1 : variables + 2, :] = (local & 1).astype(F32)
     wide_s[variables + 2 : ROWS, :] = jnp.zeros((ROWS - variables - 2, grid_count), F32)
     pay[...] = wide_s[...].astype(BF16)
+    targets[...] = slot_targets(route).T
 
     def step(pair):
-        got = dot_nt(pay[...], slot_onehot(rank, pair)).astype(BF16)
+        got = dot(pay[...], slot_onehot(targets, pair, 1)).astype(BF16)
         out_ref[2 * pair] = got[:, :TILE]
         out_ref[2 * pair + 1] = got[:, TILE:]
 
@@ -190,9 +196,12 @@
     inverse_s,
     keys_s,
     values_s,
-    weight_s,
-    prob_s,
-    score_s,
+    weight0_s,
+    weight1_s,
+    prob0_s,
+    prob1_s,
+    score0_s,
+    score1_s,
     mixed_s,
     query_s,
     keyg_s,
@@ -217,34 +226,44 @@
         values_s[:, span] = dot(value_t, normed).astype(BF16)
     first = place[0] * (node_count // TILE)
 
-    def head(h, _):
-        rows = pl.ds(pl.multiple_of(h * HEAD, HEAD), HEAD)
-        g = g_ref[:, rows]
-        kt = keys_s[rows, :]
-        vt = values_s[rows, :]
-        scores = dot(q_ref[:, rows], kt)
+    weight_s = (weight0_s, weight1_s)
+    prob_s = (prob0_s, prob1_s)
+    score_s = (score0_s, score1_s)
+
+    def soft(h):
+        rows = pl.ds(h * HEAD, HEAD)
+        weight, prob = weight_s[h % 2], prob_s[h % 2]
+        scores = dot(q_ref[:, rows], keys_s[rows, :])
         for qt in range(node_count // TILE):
             for kb in range(key_tiles):
                 seen = pattern[qt, lax.rem(first + kb, key_tiles)] > 0
                 bias = jnp.where(seen, 0.0, -1e30).astype(F32)
                 at = (slice(qt * TILE, (qt + 1) * TILE), slice(kb * TILE, (kb + 1) * TILE))
-                weight_s[at] = scores[at] * (scale / math.log(2.0)) + bias
-        biased = weight_s[...]
+                weight[at] = scores[at] * (scale / math.log(2.0)) + bias
+        biased = weight[...]
         weights = jnp.exp2(biased - jnp.max(biased, axis=1, keepdims=True))
         probs = weights * (1.0 / jnp.sum(weights, axis=1, keepdims=True))
-        weight_s[...] = probs
-        prob_s[...] = probs.astype(BF16)
-        mixed = dot_nt(prob_s[...], vt)
+        weight[...] = probs
+        prob[...] = probs.astype(BF16)
+
+    def rest(h):
+        rows = pl.ds(h * HEAD, HEAD)
+        weight, prob, score = weight_s[h % 2], prob_s[h % 2], score_s[h % 2]
+        g, kt, vt = g_ref[:, rows], keys_s[rows, :], values_s[rows, :]
+        mixed = dot_nt(prob[...], vt)
         mixed_s[rows, :] = mixed.astype(BF16).T
         delta = jnp.sum(mixed * g.astype(F32), axis=1, keepdims=True)
         prob_grad = dot(g, vt)
-        score_s[...] = (weight_s[...] * ((prob_grad - delta) * scale)).astype(BF16)
-        query_s[rows, :] = dot_nt(score_s[...], kt).astype(BF16).T
-        keyg_s[rows, :] = dot(qt_ref[rows, :], score_s[...]).astype(BF16)
-        valueg_s[rows, :] = dot(gt_ref[rows, :], prob_s[...]).astype(BF16)
-        return 0
-
-    lax.fori_loop(0, HEADS, head, 0)
+        score[...] = (weight[...] * ((prob_grad - delta) * scale)).astype(BF16)
+        query_s[rows, :] = dot_nt(score[...], kt).astype(BF16).T
+        keyg_s[rows, :] = dot(qt_ref[rows, :], score[...]).astype(BF16)
+        valueg_s[rows, :] = dot(gt_ref[rows, :], prob[...]).astype(BF16)
+
+    soft(0)
+    for h in range(HEADS):
+        if h + 1 < HEADS:
+            soft(h + 1)
+        rest(h)
     final = start_ref[...] + dot(output_w[...].T, mixed_s[...])
     decoder_t, _ = padded(dec, rows_s)
     decoded_ref[...] = dot(decoder_t, final.astype(BF16)).astype(BF16)
@@ -319,13 +338,14 @@
     loop(out_ref.shape[0] // 2, 4, step)
 
 
-def unpack_kernel(back_ref, rank, out_ref, acc):
+def unpack_kernel(back_ref, route, out_ref, acc, targets):
     peers = back_ref.shape[0]
+    targets[...] = slot_targets(route)
     acc[...] = jnp.zeros_like(acc)
 
     def step(pair):
         data = jnp.concatenate([back_ref[2 * pair], back_ref[2 * pair + 1]], axis=1)
-        acc[...] += dot(data[:ROWS], slot_onehot(rank, pair))
+        acc[...] += dot(data[:ROWS], slot_onehot(targets, pair, 0))
 
     loop(peers // 2, 4, step)
     out_ref[...] = acc[0 : out_ref.shape[0], :].astype(out_ref.dtype)
@@ -364,8 +384,12 @@
     def pack(x, index):
         return call(
             functools.partial(pack_kernel, shift, nodes - 1),
-            [((peers, ROWS, capacity), BF16), ((peers, grid_count), F32)],
-            [vm((ROWS, grid_count), F32), vm((ROWS, grid_count), BF16)],
+            [((peers, ROWS, capacity), BF16), ((2, grid_count), F32)],
+            [
+                vm((ROWS, grid_count), F32),
+                vm((ROWS, grid_count), BF16),
+                vm((grid_count, capacity), BF16),
+            ],
             "pack",
             route,
             x,
@@ -382,15 +406,15 @@
             recv,
         )
 
-    def unpack(x, rank, dtype):
+    def unpack(x, slots, dtype):
         return call(
             unpack_kernel,
             [((variables, grid_count), dtype)],
-            [vm((ROWS, grid_count), F32)],
+            [vm((ROWS, grid_count), F32), vm((capacity, grid_count), BF16)],
             "unpack",
             route,
             x,
-            rank,
+            slots,
         )[0]
 
     def from_ahead(x, r):
@@ -403,10 +427,10 @@
     gain = norm_gain.reshape(1, width)
     decoder_rows = decoder_weight.T
 
-    state_send, own_rank = pack(grid_state, grid_owner)
+    state_send, own_slots = pack(grid_state, grid_owner)
     cotangent, state_send = lax.optimization_barrier((cotangent, state_send))
     state_recv = exchange(state_send)
-    cot_send, dec_rank = pack(cotangent, decode_node)
+    cot_send, dec_slots = pack(cotangent, decode_node)
     cot_recv = exchange(cot_send)
 
     state, state_low, own_idx = sums(state_recv)
@@ -447,6 +471,9 @@
             vm((width, keys), BF16),
             vm((width, keys), BF16),
             vm((nodes, keys), F32),
+            vm((nodes, keys), F32),
+            vm((nodes, keys), BF16),
+            vm((nodes, keys), BF16),
             vm((nodes, keys), BF16),
             vm((nodes, keys), BF16),
             vm((width, nodes), BF16),
@@ -502,13 +529,14 @@
     chunk = jnp.sum(decoded_back[:, ROWS : ROWS + 2 * SHARE].astype(F32), axis=0)
     chunk = (chunk[:SHARE] + chunk[SHARE:]).astype(BF16)
     span = slice(variables, variables + SHARE)
-    grad_send = grad_send.at[:, span].set(jnp.broadcast_to(chunk, (peers,) + chunk.shape))
+    chunk = jnp.broadcast_to(chunk, (peers,) + chunk.shape)
+    grad_send = lax.dynamic_update_slice(grad_send, chunk, (0, variables, 0))
     grad_back = exchange(grad_send)
-    denoised = unpack(decoded_back, dec_rank, BF16)
+    denoised = unpack(decoded_back, dec_slots, BF16)
     grad_back, denoised = lax.optimization_barrier((grad_back, denoised))
     mine = jnp.swapaxes(grad_back[:, span], 0, 1).reshape(peers * SHARE, TILE)
     parts = [mine] + [from_ahead(mine, r) for r in range(1, group)]
-    state_grad = unpack(grad_back, own_rank, F32)
+    state_grad = unpack(grad_back, own_slots, F32)
     whole = sum(p.astype(F32) for p in parts).reshape(width // TILE, ROWS, TILE)
     encoder_grad = jnp.swapaxes(whole, 0, 1).reshape(ROWS, width)[:variables]
     return (denoised, state_grad, encoder_grad)

time: 134 us -> 130 us (0.970)
  Pallas kernels: 57.6 us -> 52.8 us
  waiting for transfers between devices: 31.8 us -> 33.4 us
    pallas_call x11, Pallas kernels: 57.6 us -> 52.8 us  [call(): pl.pallas_call(kernel, out_shape=[jax.ShapeDtypeStruct(s, d) for s, d in...]
    dynamic_update_slice x0 -> x1, local copies, waits for them, and re-layouts: none -> 1.7 us  [body(): grad_send = lax.dynamic_update_slice(grad_send, chunk, (0, variables, 0))]
    scatter x1 -> x0, local copies, waits for them, and re-layouts: 1.7 us -> none  [body(): grad_send.at[:, span].set(jnp.broadcast_to(chunk, (peers,) + chunk.shape))]
    all_to_all x4, waiting for transfers between devices: 28 us -> 29.6 us  [exchange(): return lax.all_to_all(x, 'wide', split_axis=0, concat_axis=0, tiled=True)]
where the time goes in v3:
time: 130 us
  Pallas kernels  52.8 us (41%)
  starting transfers between devices  36.9 us (28%)
  waiting for transfers between devices  33.4 us (26%)
  local copies, waits for them, and re-layouts  5.67 us (4%)
    pallas_call x11, Pallas kernels, call(): pl.pallas_call(kernel, out_shape=[jax.ShapeDtypeStruct(s, d) for s, d in...  52.8 us
    all_to_all x4, waiting for transfers between devices, exchange(): return lax.all_to_all(x, 'wide', split_axis=0, concat_axis=0, tiled=True)  29.6 us
    all_to_all x4, starting transfers between devices, exchange(): return lax.all_to_all(x, 'wide', split_axis=0, concat_axis=0, tiled=True)  20.3 us
    ppermute x6, starting transfers between devices, from_ahead(): lax.ppermute(x, 'patch', [((i + r) % group, i) for i in range(group)])  10.9 us
    ppermute x3, starting transfers between devices, to_ahead(): lax.ppermute(x, 'patch', [(i, (i + r) % group) for i in range(group)])  5.73 us
    unnamed x26, local copies, waits for them, and re-layouts  3.84 us
    ppermute x3, waiting for transfers between devices, to_ahead(): lax.ppermute(x, 'patch', [(i, (i + r) % group) for i in range(group)])  3.15 us
  transfers between devices with their start and end apart: 13, of which 7 were waited for; matrix products, arithmetic and copies ran while one was open for 0% of the time, Pallas kernels for 17%

profile of v3, /device:TPU:0, one launch (start us, length us, event | category | flops | bytes accessed | tf_op | source)
XLA Modules:
  0.0 129.7 jit_solution(9358797205138270835)
XLA Ops:
  0.6 0.0 copy-start.4
  0.6 1.0 copy-done.4
  1.6 0.0 copy-start.8
  1.6 0.7 copy-done.8
  2.3 5.2 %pack.2 = (bf16[32,88,128]{2,1,0:T(8,128)(2,1)}, f32[2,2048]{1,0:T(2,128)S(1)}) custom-call(bf16[84,2048]{1,0:T(8,128)(2,1)S(1)} %copy-done.4, s32[1,2048]{1,0:T(1,128)S(1)} %bitcast.17), custom_call_target="tpu_custom_call" | custom-call | flops 1476395008 | bytes 1048576 | tf_op jit(solution)/shard_map/pack/pallas_call | solution.py:39
  7.5 0.0 copy-start.5
  7.5 0.0 copy-start.9
  7.5 8.5 %all-to-all-start = ((bf16[32,88,128]{2,1,0:T(8,128)(2,1)}), bf16[32,88,128]{2,1,0:T(8,128)(2,1)S(1)}, u32[]{:S(2)}, u32[]{:S(2)}) async-start(bf16[32,88,128]{2,1,0:T(8,128)(2,1)} %get-tuple-element.31), calls=%async_computation | async-start | bytes 1441792 | tf_op jit(solution)/shard_map/all_to_all | solution.py:382
  16.0 0.0 copy-done.5
  16.0 0.0 copy-done.9
  16.1 5.2 %pack.3 = (bf16[32,88,128]{2,1,0:T(8,128)(2,1)}, f32[2,2048]{1,0:T(2,128)S(1)}) custom-call(bf16[84,2048]{1,0:T(8,128)(2,1)S(1)} %copy-done.5, s32[1,2048]{1,0:T(1,128)S(1)} %bitcast.18), custom_call_target="tpu_custom_call" | custom-call | flops 1476395008 | bytes 1048576 | tf_op jit(solution)/shard_map/pack/pallas_call | solution.py:39
  21.2 8.7 %all-to-all-done.recv_ref = bf16[32,88,128]{2,1,0:T(8,128)(2,1)S(1)} async-done(((bf16[32,88,128]{2,1,0:T(8,128)(2,1)}), bf16[32,88,128]{2,1,0:T(8,128)(2,1)S(1)}, u32[]{:S(2)}, u32[]{:S(2)}) %all-to-all-start) | async-done | bytes 720928 | tf_op jit(solution)/shard_map/all_to_all | solution.py:382
  29.9 3.9 %all-to-all-start.1 = ((bf16[32,88,128]{2,1,0:T(8,128)(2,1)}), bf16[32,88,128]{2,1,0:T(8,128)(2,1)S(1)}, u32[]{:S(2)}, u32[]{:S(2)}) async-start(bf16[32,88,128]{2,1,0:T(8,128)(2,1)} %get-tuple-element.38), calls=%async_computation.1 | async-start | bytes 1441792 | tf_op jit(solution)/shard_map/all_to_all | solution.py:382
  33.8 0.0 copy-start.11
  33.9 0.7 copy-done.11
  34.5 1.9 %sums.2 = (bf16[88,512]{1,0:T(8,128)(2,1)S(1)}, bf16[88,512]{1,0:T(8,128)(2,1)S(1)}, s32[32,128]{1,0:T(8,128)S(1)}) custom-call(bf16[32,88,128]{2,1,0:T(8,128)(2,1)S(1)} %all-to-all-done.recv_ref), custom_call_target="tpu_custom_call" | custom-call | flops 369098752 | bytes 1048576 | tf_op jit(solution)/shard_map/sums/pallas_call | solution.py:39
  36.4 0.0 copy-start.1
  36.4 0.0 copy-start.7
  36.4 1.6 %collective-permute-start.2 = (bf16[88,512]{1,0:T(8,128)(2,1)S(1)}, bf16[88,512]{1,0:T(8,128)(2,1)S(1)}, u32[]{:S(2)}, u32[]{:S(2)}) collective-permute-start(bf16[88,512]{1,0:T(8,128)(2,1)S(1)} %get-tuple-element.33.high.s0_ref), channel_id=1, source_target_pairs={{3,0},{0,1},{1,2},{2,3},{7,4},{4,5},{5,6},{6,7},{11,8},{8,9},{9,10... | collective-permute-start | bytes 270344 | tf_op jit(solution)/shard_map/ppermute | solution.py:421
  38.0 2.7 %collective-permute-start.1 = (bf16[88,512]{1,0:T(8,128)(2,1)S(1)}, bf16[88,512]{1,0:T(8,128)(2,1)S(1)}, u32[]{:S(2)}, u32[]{:S(2)}) collective-permute-start(bf16[88,512]{1,0:T(8,128)(2,1)S(1)} %get-tuple-element.33.high.s0_ref), channel_id=1, source_target_pairs={{2,0},{3,1},{0,2},{1,3},{6,4},{7,5},{4,6},{5,7},{10,8},{11,9},{8,1... | collective-permute-start | bytes 270344 | tf_op jit(solution)/shard_map/ppermute | solution.py:421
  40.7 1.4 %collective-permute-start = (bf16[88,512]{1,0:T(8,128)(2,1)S(1)}, bf16[88,512]{1,0:T(8,128)(2,1)S(1)}, u32[]{:S(2)}, u32[]{:S(2)}) collective-permute-start(bf16[88,512]{1,0:T(8,128)(2,1)S(1)} %get-tuple-element.33.high.s0_ref), channel_id=1, source_target_pairs={{1,0},{2,1},{3,2},{0,3},{5,4},{6,5},{7,6},{4,7},{9,8},{10,9},{11,1... | collective-permute-start | bytes 270344 | tf_op jit(solution)/shard_map/ppermute | solution.py:421
  42.2 5.6 %all-to-all-done.1.recv_ref = bf16[32,88,128]{2,1,0:T(8,128)(2,1)S(1)} async-done(((bf16[32,88,128]{2,1,0:T(8,128)(2,1)}), bf16[32,88,128]{2,1,0:T(8,128)(2,1)S(1)}, u32[]{:S(2)}, u32[]{:S(2)}) %all-to-all-start.1) | async-done | bytes 720928 | tf_op jit(solution)/shard_map/all_to_all | solution.py:382
  47.7 2.0 %sums.3 = (bf16[88,512]{1,0:T(8,128)(2,1)S(1)}, bf16[88,512]{1,0:T(8,128)(2,1)S(1)}, s32[32,128]{1,0:T(8,128)S(1)}) custom-call(bf16[32,88,128]{2,1,0:T(8,128)(2,1)S(1)} %all-to-all-done.1.recv_ref), custom_call_target="tpu_custom_call" | custom-call | flops 369098752 | bytes 1048576 | tf_op jit(solution)/shard_map/sums/pallas_call | solution.py:39
  49.8 0.0 copy-done.1
  49.8 0.0 copy-done.7
  49.8 0.0 copy-start
  49.8 0.0 copy-start.6
  49.8 0.9 top.1
  50.8 0.1 copy-done
  50.9 0.0 copy-done.6
  50.9 0.0 copy-start.2
  50.9 0.0 copy-start.3
  50.9 1.2 query.1
  52.1 0.0 collective-permute-done.2.s3_ref
  52.1 0.0 collective-permute-done.1.s2_ref
  52.1 0.0 collective-permute-done.s1_ref
  52.1 0.0 copy-start.10
  52.1 0.0 copy-done.2
  52.1 0.0 copy-done.3
  52.1 0.7 copy-done.10
  52.8 23.7 %attend.1 = (bf16[88,512]{1,0:T(8,128)(2,1)S(1)}, f32[88,512]{1,0:T(8,128)S(1)}, bf16[88,512]{1,0:T(8,128)(2,1)S(1)}, bf16[88,512]{1,0:T(8,128)(2,1)S(1)}, bf16[...) custom-call(s32[1]{0:T(128)} %bitcast.1.place, s32[4,16]{1,0:T(4,128)S(1)} %copy-done.10, ...), custom_call_target="tpu_custom_call" | custom-call | flops 10737418240 | bytes 1048576 | tf_op jit(solution)/shard_map/attend/pallas_call | solution.py:39
  76.5 2.3 %decoded_slots.1 = bf16[32,112,128]{2,1,0:T(8,128)(2,1)} custom-call(s32[32,128]{1,0:T(8,128)S(1)} %get-tuple-element.50.index, bf16[88,512]{1,0:T(8,128)(2,1)S(1)} %get-tuple-element.51.decoded_ref, f32[88,512]{1,0:T(8,128)S(1)} %get-tuple-element.52.enc_ref), custom_call_target="tpu_custom_call" | custom-call | flops 369098752 | bytes 1048576 | tf_op jit(solution)/shard_map/decoded_slots/pallas_call | solution.py:39
  78.7 3.9 %all-to-all-start.2 = ((bf16[32,112,128]{2,1,0:T(8,128)(2,1)}), bf16[32,112,128]{2,1,0:T(8,128)(2,1)S(1)}, u32[]{:S(2)}, u32[]{:S(2)}) async-start(bf16[32,112,128]{2,1,0:T(8,128)(2,1)} %decoded_slots.1), calls=%async_computation.2 | async-start | bytes 1835008 | tf_op jit(solution)/shard_map/all_to_all | solution.py:382
  82.7 1.6 %collective-permute-start.3 = (bf16[88,512]{1,0:T(8,128)(2,1)S(1)}, bf16[88,512]{1,0:T(8,128)(2,1)S(1)}, u32[]{:S(2)}, u32[]{:S(2)}) collective-permute-start(bf16[88,512]{1,0:T(8,128)(2,1)S(1)} %get-tuple-element.47), channel_id=1, source_target_pairs={{0,1},{1,2},{2,3},{3,0},{4,5},{5,6},{6,7},{7,4},{8,9},{9,10},{10,1... | collective-permute-start | bytes 270344 | tf_op jit(solution)/shard_map/ppermute | solution.py:424
  84.2 2.7 %collective-permute-start.4 = (bf16[88,512]{1,0:T(8,128)(2,1)S(1)}, bf16[88,512]{1,0:T(8,128)(2,1)S(1)}, u32[]{:S(2)}, u32[]{:S(2)}) collective-permute-start(bf16[88,512]{1,0:T(8,128)(2,1)S(1)} %get-tuple-element.48), channel_id=1, source_target_pairs={{0,2},{1,3},{2,0},{3,1},{4,6},{5,7},{6,4},{7,5},{8,10},{9,11},{10,... | collective-permute-start | bytes 270344 | tf_op jit(solution)/shard_map/ppermute | solution.py:424
  87.0 1.4 %collective-permute-start.5 = (bf16[88,512]{1,0:T(8,128)(2,1)S(1)}, bf16[88,512]{1,0:T(8,128)(2,1)S(1)}, u32[]{:S(2)}, u32[]{:S(2)}) collective-permute-start(bf16[88,512]{1,0:T(8,128)(2,1)S(1)} %get-tuple-element.49), channel_id=1, source_target_pairs={{0,3},{1,0},{2,1},{3,2},{4,7},{5,4},{6,5},{7,6},{8,11},{9,8},{10,9... | collective-permute-start | bytes 270344 | tf_op jit(solution)/shard_map/ppermute | solution.py:424
  88.4 0.2 collective-permute-done.3.i1_ref
  88.6 2.9 %collective-permute-done.4.i2_ref = bf16[88,512]{1,0:T(8,128)(2,1)S(1)} collective-permute-done((bf16[88,512]{1,0:T(8,128)(2,1)S(1)}, bf16[88,512]{1,0:T(8,128)(2,1)S(1)}, u32[]{:S(2)}, u32[]{:S(2)}) %collective-permute-start.4) | collective-permute-done | bytes 90144 | tf_op jit(solution)/shard_map/ppermute | solution.py:424
  91.6 0.0 collective-permute-done.5.i3_ref
  91.6 2.2 %grad_slots.1 = bf16[32,96,128]{2,1,0:T(8,128)(2,1)} custom-call(s32[32,128]{1,0:T(8,128)S(1)} %get-tuple-element.32.index, f32[88,512]{1,0:T(8,128)S(1)} %get-tuple-element.46.own_ref, bf16[88,512]{1,0:T(8,128)(2,1)S(1)} %collective-permute-done.3.i1_ref, bf16[88,512]{1,0:T(8,128)(2,1)S(1)} %collective-permute-done.4.i2_ref, ...), custom_call_target="tpu_custom_call" | custom-call | flops 369098752 | bytes 1048576 | tf_op jit(solution)/shard_map/grad_slots/pallas_call | solution.py:39
  93.8 4.8 %all-to-all-done.2.back_ref = bf16[32,112,128]{2,1,0:T(8,128)(2,1)S(1)} async-done(((bf16[32,112,128]{2,1,0:T(8,128)(2,1)}), bf16[32,112,128]{2,1,0:T(8,128)(2,1)S(1)}, u32[]{:S(2)}, u32[]{:S(2)}) %all-to-all-start.2) | async-done | bytes 917536 | tf_op jit(solution)/shard_map/all_to_all | solution.py:382
  98.7 1.7 %dynamic_update_slice.3 = bf16[32,96,128]{2,1,0:T(8,128)(2,1)} dynamic-update-slice(bf16[32,96,128]{2,1,0:T(8,128)(2,1)} %grad_slots.1, bf16[32,11,128]{2,1,0:T(8,128)(2,1)S(1)} %broadcast_in_dim.3, s32[]{:T(128)} %constant.2.clone.1, s32[]{:T(128)} %constant.3.clone.1, s32[]{:T(128)} %constant.2.clone.1) | dynamic-update-slice | bytes 180228 | tf_op jit(solution)/shard_map/dynamic_update_slice | solution.py:533
  100.4 3.9 %all-to-all-start.3 = ((bf16[32,96,128]{2,1,0:T(8,128)(2,1)}), bf16[32,96,128]{2,1,0:T(8,128)(2,1)S(1)}, u32[]{:S(2)}, u32[]{:S(2)}) async-start(bf16[32,96,128]{2,1,0:T(8,128)(2,1)} %dynamic_update_slice.3), calls=%async_computation.3 | async-start | bytes 1572864 | tf_op jit(solution)/shard_map/all_to_all | solution.py:382
  104.3 4.1 %unpack.2 = bf16[84,2048]{1,0:T(8,128)(2,1)} custom-call(bf16[32,112,128]{2,1,0:T(8,128)(2,1)S(1)} %all-to-all-done.2.back_ref, f32[2,2048]{1,0:T(2,128)S(1)} %get-tuple-element.53.route), custom_call_target="tpu_custom_call" | custom-call | flops 1476395008 | bytes 1048576 | tf_op jit(solution)/shard_map/unpack/pallas_call | solution.py:39
  108.4 10.5 %all-to-all-done.3.back_ref = bf16[32,96,128]{2,1,0:T(8,128)(2,1)S(1)} async-done(((bf16[32,96,128]{2,1,0:T(8,128)(2,1)}), bf16[32,96,128]{2,1,0:T(8,128)(2,1)S(1)}, u32[]{:S(2)}, u32[]{:S(2)}) %all-to-all-start.3) | async-done | bytes 786464 | tf_op jit(solution)/shard_map/all_to_all | solution.py:382
  118.9 3.1 %collective-permute-start.7 = (bf16[352,128]{1,0:T(8,128)(2,1)S(1)}, bf16[352,128]{1,0:T(8,128)(2,1)S(1)}, u32[]{:S(2)}, u32[]{:S(2)}) collective-permute-start(bf16[352,128]{1,0:T(8,128)(2,1)S(1)} %bitcast.21), channel_id=1, source_target_pairs={{2,0},{3,1},{0,2},{1,3},{6,4},{7,5},{4,6},{5,7},{10,8},{11,9},{8,1... | collective-permute-start | bytes 270344 | tf_op jit(solution)/shard_map/ppermute | solution.py:421
  122.0 1.1 collective-permute-start.6
  123.2 0.9 collective-permute-start.8
  124.1 4.2 %unpack.3 = f32[84,2048]{1,0:T(8,128)} custom-call(bf16[32,96,128]{2,1,0:T(8,128)(2,1)S(1)} %all-to-all-done.3.back_ref, f32[2,2048]{1,0:T(2,128)S(1)} %get-tuple-element.56.route), custom_call_target="tpu_custom_call" | custom-call | flops 1476395008 | bytes 1048576 | tf_op jit(solution)/shard_map/unpack/pallas_call | solution.py:39
  128.3 0.0 collective-permute-done.7
  128.3 0.0 collective-permute-done.6
  128.3 0.6 collective-permute-done.8
  128.9 0.1 convert_add_fusion
  129.1 0.7 copy.18
  (8 shorter events, 0.2 us)
Async XLA Ops:
  0.6 1.0 copy-start.4
  1.6 0.7 copy-start.8
  7.5 8.6 %copy-start.5 = (bf16[84,2048]{1,0:T(8,128)(2,1)S(1)}, bf16[84,2048]{1,0:T(8,128)(2,1)}, u32[]{:S(2)}) copy-start(bf16[84,2048]{1,0:T(8,128)(2,1)} %x_ref.2) | copy-start | bytes 1032196
  7.5 8.6 %copy-start.9 = (s32[2048]{0:T(1024)S(1)}, s32[2048]{0:T(1024)}, u32[]{:S(2)}) copy-start(s32[2048]{0:T(1024)} %param.22) | copy-start | bytes 24580
  7.5 22.4 %all-to-all-start = ((bf16[32,88,128]{2,1,0:T(8,128)(2,1)}), bf16[32,88,128]{2,1,0:T(8,128)(2,1)S(1)}, u32[]{:S(2)}, u32[]{:S(2)}) async-start(bf16[32,88,128]{2,1,0:T(8,128)(2,1)} %get-tuple-element.31), calls=%async_computation | async-start | bytes 1441792 | tf_op jit(solution)/shard_map/all_to_all | solution.py:382
  29.9 17.8 %all-to-all-start.1 = ((bf16[32,88,128]{2,1,0:T(8,128)(2,1)}), bf16[32,88,128]{2,1,0:T(8,128)(2,1)S(1)}, u32[]{:S(2)}, u32[]{:S(2)}) async-start(bf16[32,88,128]{2,1,0:T(8,128)(2,1)} %get-tuple-element.38), calls=%async_computation.1 | async-start | bytes 1441792 | tf_op jit(solution)/shard_map/all_to_all | solution.py:382
  33.8 0.7 copy-start.11
  36.4 13.4 %copy-start.1 = (bf16[512,512]{1,0:T(8,128)(2,1)S(1)}, bf16[512,512]{1,0:T(8,128)(2,1)}, u32[]{:S(2)}) copy-start(bf16[512,512]{1,0:T(8,128)(2,1)} %output_w.1) | copy-start | bytes 1572868
  36.4 13.4 %copy-start.7 = (bf16[512,84]{0,1:T(8,128)(2,1)S(1)}, bf16[512,84]{0,1:T(8,128)(2,1)}, u32[]{:S(2)}) copy-start(bf16[512,84]{0,1:T(8,128)(2,1)} %param.20) | copy-start | bytes 258052
  36.4 15.7 %collective-permute-start.2 = (bf16[88,512]{1,0:T(8,128)(2,1)S(1)}, bf16[88,512]{1,0:T(8,128)(2,1)S(1)}, u32[]{:S(2)}, u32[]{:S(2)}) collective-permute-start(bf16[88,512]{1,0:T(8,128)(2,1)S(1)} %get-tuple-element.33.high.s0_ref), channel_id=1, source_target_pairs={{3,0},{0,1},{1,2},{2,3},{7,4},{4,5},{5,6},{6,7},{11,8},{8,9},{9,10... | collective-permute-start | bytes 270344 | tf_op jit(solution)/shard_map/ppermute | solution.py:421
  38.0 14.1 %collective-permute-start.1 = (bf16[88,512]{1,0:T(8,128)(2,1)S(1)}, bf16[88,512]{1,0:T(8,128)(2,1)S(1)}, u32[]{:S(2)}, u32[]{:S(2)}) collective-permute-start(bf16[88,512]{1,0:T(8,128)(2,1)S(1)} %get-tuple-element.33.high.s0_ref), channel_id=1, source_target_pairs={{2,0},{3,1},{0,2},{1,3},{6,4},{7,5},{4,6},{5,7},{10,8},{11,9},{8,1... | collective-permute-start | bytes 270344 | tf_op jit(solution)/shard_map/ppermute | solution.py:421
  40.7 11.4 %collective-permute-start = (bf16[88,512]{1,0:T(8,128)(2,1)S(1)}, bf16[88,512]{1,0:T(8,128)(2,1)S(1)}, u32[]{:S(2)}, u32[]{:S(2)}) collective-permute-start(bf16[88,512]{1,0:T(8,128)(2,1)S(1)} %get-tuple-element.33.high.s0_ref), channel_id=1, source_target_pairs={{1,0},{2,1},{3,2},{0,3},{5,4},{6,5},{7,6},{4,7},{9,8},{10,9},{11,1... | collective-permute-start | bytes 270344 | tf_op jit(solution)/shard_map/ppermute | solution.py:421
  49.8 1.0 copy-start
  49.8 1.0 copy-start.6
  50.9 1.3 copy-start.2
  50.9 1.3 copy-start.3
  52.1 0.7 copy-start.10
  78.7 19.9 %all-to-all-start.2 = ((bf16[32,112,128]{2,1,0:T(8,128)(2,1)}), bf16[32,112,128]{2,1,0:T(8,128)(2,1)S(1)}, u32[]{:S(2)}, u32[]{:S(2)}) async-start(bf16[32,112,128]{2,1,0:T(8,128)(2,1)} %decoded_slots.1), calls=%async_computation.2 | async-start | bytes 1835008 | tf_op jit(solution)/shard_map/all_to_all | solution.py:382
  82.7 6.0 %collective-permute-start.3 = (bf16[88,512]{1,0:T(8,128)(2,1)S(1)}, bf16[88,512]{1,0:T(8,128)(2,1)S(1)}, u32[]{:S(2)}, u32[]{:S(2)}) collective-permute-start(bf16[88,512]{1,0:T(8,128)(2,1)S(1)} %get-tuple-element.47), channel_id=1, source_target_pairs={{0,1},{1,2},{2,3},{3,0},{4,5},{5,6},{6,7},{7,4},{8,9},{9,10},{10,1... | collective-permute-start | bytes 270344 | tf_op jit(solution)/shard_map/ppermute | solution.py:424
  84.2 7.3 %collective-permute-start.4 = (bf16[88,512]{1,0:T(8,128)(2,1)S(1)}, bf16[88,512]{1,0:T(8,128)(2,1)S(1)}, u32[]{:S(2)}, u32[]{:S(2)}) collective-permute-start(bf16[88,512]{1,0:T(8,128)(2,1)S(1)} %get-tuple-element.48), channel_id=1, source_target_pairs={{0,2},{1,3},{2,0},{3,1},{4,6},{5,7},{6,4},{7,5},{8,10},{9,11},{10,... | collective-permute-start | bytes 270344 | tf_op jit(solution)/shard_map/ppermute | solution.py:424
  87.0 4.6 %collective-permute-start.5 = (bf16[88,512]{1,0:T(8,128)(2,1)S(1)}, bf16[88,512]{1,0:T(8,128)(2,1)S(1)}, u32[]{:S(2)}, u32[]{:S(2)}) collective-permute-start(bf16[88,512]{1,0:T(8,128)(2,1)S(1)} %get-tuple-element.49), channel_id=1, source_target_pairs={{0,3},{1,0},{2,1},{3,2},{4,7},{5,4},{6,5},{7,6},{8,11},{9,8},{10,9... | collective-permute-start | bytes 270344 | tf_op jit(solution)/shard_map/ppermute | solution.py:424
  100.4 18.5 %all-to-all-start.3 = ((bf16[32,96,128]{2,1,0:T(8,128)(2,1)}), bf16[32,96,128]{2,1,0:T(8,128)(2,1)S(1)}, u32[]{:S(2)}, u32[]{:S(2)}) async-start(bf16[32,96,128]{2,1,0:T(8,128)(2,1)} %dynamic_update_slice.3), calls=%async_computation.3 | async-start | bytes 1572864 | tf_op jit(solution)/shard_map/all_to_all | solution.py:382
  118.9 9.4 %collective-permute-start.7 = (bf16[352,128]{1,0:T(8,128)(2,1)S(1)}, bf16[352,128]{1,0:T(8,128)(2,1)S(1)}, u32[]{:S(2)}, u32[]{:S(2)}) collective-permute-start(bf16[352,128]{1,0:T(8,128)(2,1)S(1)} %bitcast.21), channel_id=1, source_target_pairs={{2,0},{3,1},{0,2},{1,3},{6,4},{7,5},{4,6},{5,7},{10,8},{11,9},{8,1... | collective-permute-start | bytes 270344 | tf_op jit(solution)/shard_map/ppermute | solution.py:421
  122.0 6.3 %collective-permute-start.6 = (bf16[352,128]{1,0:T(8,128)(2,1)S(1)}, bf16[352,128]{1,0:T(8,128)(2,1)S(1)}, u32[]{:S(2)}, u32[]{:S(2)}) collective-permute-start(bf16[352,128]{1,0:T(8,128)(2,1)S(1)} %bitcast.22), channel_id=1, source_target_pairs={{1,0},{2,1},{3,2},{0,3},{5,4},{6,5},{7,6},{4,7},{9,8},{10,9},{11,1... | collective-permute-start | bytes 270344 | tf_op jit(solution)/shard_map/ppermute | solution.py:421
  123.2 5.7 %collective-permute-start.8 = (bf16[352,128]{1,0:T(8,128)(2,1)S(1)}, bf16[352,128]{1,0:T(8,128)(2,1)S(1)}, u32[]{:S(2)}, u32[]{:S(2)}) collective-permute-start(bf16[352,128]{1,0:T(8,128)(2,1)S(1)} %bitcast.23), channel_id=1, source_target_pairs={{3,0},{0,1},{1,2},{2,3},{7,4},{4,5},{5,6},{6,7},{11,8},{8,9},{9,10... | collective-permute-start | bytes 270344 | tf_op jit(solution)/shard_map/ppermute | solution.py:421

commit v4 on v3

--- a/solution.py
+++ b/solution.py
@@ -305,17 +305,15 @@
         whole[t * height : (t + 1) * height, :] = enc_ref[:, t * TILE : (t + 1) * TILE]
     extra[...] = jnp.zeros_like(extra)
     for j in range(SHARE):
-        rows = whole[j * peers : (j + 1) * peers, :]
-        high = rows.astype(BF16).astype(F32)
-        extra[pl.ds(j, peers, stride=24), :] = high
-        extra[pl.ds(SHARE + j, peers, stride=24), :] = rows - high
+        extra[pl.ds(4 + j, peers, stride=16), :] = whole[j * peers : (j + 1) * peers, :]
     nodes = lax.broadcasted_iota(jnp.int32, (decoded_ref.shape[1], TILE), 0)
 
     def step(pair):
         got = dot(decoded_ref[...], picks_of(index, pair, nodes))
         for one in range(2):
-            tail = extra[pl.ds(pl.multiple_of((2 * pair + one) * 24, 8), 24), :]
-            rows = jnp.concatenate([got[:, one * TILE : (one + 1) * TILE], tail], axis=0)
+            tail = extra[pl.ds(pl.multiple_of((2 * pair + one) * 16, 16), 16), :]
+            rows = got[:, one * TILE : (one + 1) * TILE]
+            rows = jnp.concatenate([rows[:80], rows[80:] + tail[:8], tail[8:]], axis=0)
             out_ref[2 * pair + one] = rows.astype(BF16)
 
     loop(peers // 2, 4, step)
@@ -349,6 +347,15 @@
 
     loop(peers // 2, 4, step)
     out_ref[...] = acc[0 : out_ref.shape[0], :].astype(out_ref.dtype)
+
+
+def assemble_kernel(p0_ref, p1_ref, p2_ref, p3_ref, out_ref):
+    total = p0_ref[...].astype(F32)
+    for part in (p1_ref, p2_ref, p3_ref):
+        total = total + part[...].astype(F32)
+    for t in range(out_ref.shape[1] // TILE):
+        rows = total[t * ROWS : (t + 1) * ROWS]
+        out_ref[:, t * TILE : (t + 1) * TILE] = rows[: out_ref.shape[0]]
 
 
 def body(
@@ -507,8 +514,8 @@
     back = [to_ahead(o, r) for r, o in ((1, o1), (2, o2), (3, o3))]
     (decoded_send,) = call(
         decoded_slots_kernel,
-        [((peers, ROWS + 24, capacity), BF16)],
-        [vm((peers * SHARE, TILE), F32), vm((peers * 24, TILE), F32)],
+        [((peers, ROWS + 8, capacity), BF16)],
+        [vm((peers * SHARE, TILE), F32), vm((peers * 16, TILE), F32)],
         "decoded_slots",
         spread,
         dec_idx,
@@ -526,9 +533,8 @@
         own,
         *back,
     )
-    chunk = jnp.sum(decoded_back[:, ROWS : ROWS + 2 * SHARE].astype(F32), axis=0)
-    chunk = (chunk[:SHARE] + chunk[SHARE:]).astype(BF16)
     span = slice(variables, variables + SHARE)
+    chunk = jnp.sum(decoded_back[:, span].astype(F32), axis=0).astype(BF16)
     chunk = jnp.broadcast_to(chunk, (peers,) + chunk.shape)
     grad_send = lax.dynamic_update_slice(grad_send, chunk, (0, variables, 0))
     grad_back = exchange(grad_send)
@@ -537,8 +543,9 @@
     mine = jnp.swapaxes(grad_back[:, span], 0, 1).reshape(peers * SHARE, TILE)
     parts = [mine] + [from_ahead(mine, r) for r in range(1, group)]
     state_grad = unpack(grad_back, own_slots, F32)
-    whole = sum(p.astype(F32) for p in parts).reshape(width // TILE, ROWS, TILE)
-    encoder_grad = jnp.swapaxes(whole, 0, 1).reshape(ROWS, width)[:variables]
+    (encoder_grad,) = call(
+        assemble_kernel, [((variables, width), F32)], [], "assemble", 8 * ROWS * width, *parts
+    )
     return (denoised, state_grad, encoder_grad)
 
 

time: 130 us -> 129 us (level)
  waiting for transfers between devices: 33.4 us -> 31.4 us
    all_to_all x4, waiting for transfers between devices: 29.6 us -> 28.2 us  [exchange(): return lax.all_to_all(x, 'wide', split_axis=0, concat_axis=0, tiled=True)]
    pallas_call x11 -> x12, Pallas kernels: 52.8 us -> 53.6 us  [call(): pl.pallas_call(kernel, out_shape=[jax.ShapeDtypeStruct(s, d) for s, d in...]
    unnamed x26 -> x24, local copies, waits for them, and re-layouts: 3.84 us -> 3.13 us
  transfers between devices with their start and end apart: 13 -> 13, of which waited for: 7 -> 6; matrix products, arithmetic and copies ran while one was open for 0% -> 0% of each run, Pallas kernels for 17% -> 17%
where the time goes in v4:
time: 129 us; the launch traced here: 128 us
  Pallas kernels  53.6 us (42%)
  starting transfers between devices  37.5 us (29%)
  waiting for transfers between devices  31.4 us (24%)
  local copies, waits for them, and re-layouts  4.93 us (4%)
    pallas_call x12, Pallas kernels, call(): pl.pallas_call(kernel, out_shape=[jax.ShapeDtypeStruct(s, d) for s, d in...  53.6 us
    all_to_all x4, waiting for transfers between devices, exchange(): return lax.all_to_all(x, 'wide', split_axis=0, concat_axis=0, tiled=True)  28.2 us
    all_to_all x4, starting transfers between devices, exchange(): return lax.all_to_all(x, 'wide', split_axis=0, concat_axis=0, tiled=True)  20.3 us
    ppermute x6, starting transfers between devices, from_ahead(): lax.ppermute(x, 'patch', [((i + r) % group, i) for i in range(group)])  11.5 us
    ppermute x3, starting transfers between devices, to_ahead(): lax.ppermute(x, 'patch', [(i, (i + r) % group) for i in range(group)])  5.73 us
    ppermute x3, waiting for transfers between devices, to_ahead(): lax.ppermute(x, 'patch', [(i, (i + r) % group) for i in range(group)])  3.15 us
    unnamed x24, local copies, waits for them, and re-layouts  3.13 us
  transfers between devices with their start and end apart: 13, of which 6 were waited for; matrix products, arithmetic and copies ran while one was open for 0% of the time, Pallas kernels for 17%

profile of v4, /device:TPU:0, one launch (start us, length us, event | category | flops | bytes accessed | tf_op | source)
XLA Modules:
  0.0 128.3 jit_solution(7588762036538481602)
XLA Ops:
  0.6 0.0 copy-start.4
  0.6 1.0 copy-done.4
  1.6 0.0 copy-start.8
  1.6 0.7 copy-done.8
  2.3 5.2 %pack.2 = (bf16[32,88,128]{2,1,0:T(8,128)(2,1)}, f32[2,2048]{1,0:T(2,128)S(1)}) custom-call(bf16[84,2048]{1,0:T(8,128)(2,1)S(1)} %copy-done.4, s32[1,2048]{1,0:T(1,128)S(1)} %bitcast.13), custom_call_target="tpu_custom_call" | custom-call | flops 1476395008 | bytes 1048576 | tf_op jit(solution)/shard_map/pack/pallas_call | solution.py:39
  7.5 0.0 copy-start.5
  7.5 0.0 copy-start.9
  7.5 8.5 %all-to-all-start = ((bf16[32,88,128]{2,1,0:T(8,128)(2,1)}), bf16[32,88,128]{2,1,0:T(8,128)(2,1)S(1)}, u32[]{:S(2)}, u32[]{:S(2)}) async-start(bf16[32,88,128]{2,1,0:T(8,128)(2,1)} %get-tuple-element.31), calls=%async_computation | async-start | bytes 1441792 | tf_op jit(solution)/shard_map/all_to_all | solution.py:389
  16.0 0.0 copy-done.5
  16.0 0.0 copy-done.9
  16.1 5.2 %pack.3 = (bf16[32,88,128]{2,1,0:T(8,128)(2,1)}, f32[2,2048]{1,0:T(2,128)S(1)}) custom-call(bf16[84,2048]{1,0:T(8,128)(2,1)S(1)} %copy-done.5, s32[1,2048]{1,0:T(1,128)S(1)} %bitcast.14), custom_call_target="tpu_custom_call" | custom-call | flops 1476395008 | bytes 1048576 | tf_op jit(solution)/shard_map/pack/pallas_call | solution.py:39
  21.2 8.7 %all-to-all-done.recv_ref = bf16[32,88,128]{2,1,0:T(8,128)(2,1)S(1)} async-done(((bf16[32,88,128]{2,1,0:T(8,128)(2,1)}), bf16[32,88,128]{2,1,0:T(8,128)(2,1)S(1)}, u32[]{:S(2)}, u32[]{:S(2)}) %all-to-all-start) | async-done | bytes 720928 | tf_op jit(solution)/shard_map/all_to_all | solution.py:389
  29.9 3.9 %all-to-all-start.1 = ((bf16[32,88,128]{2,1,0:T(8,128)(2,1)}), bf16[32,88,128]{2,1,0:T(8,128)(2,1)S(1)}, u32[]{:S(2)}, u32[]{:S(2)}) async-start(bf16[32,88,128]{2,1,0:T(8,128)(2,1)} %get-tuple-element.38), calls=%async_computation.1 | async-start | bytes 1441792 | tf_op jit(solution)/shard_map/all_to_all | solution.py:389
  33.8 0.0 copy-start.11
  33.9 0.7 copy-done.11
  34.5 1.9 %sums.2 = (bf16[88,512]{1,0:T(8,128)(2,1)S(1)}, bf16[88,512]{1,0:T(8,128)(2,1)S(1)}, s32[32,128]{1,0:T(8,128)S(1)}) custom-call(bf16[32,88,128]{2,1,0:T(8,128)(2,1)S(1)} %all-to-all-done.recv_ref), custom_call_target="tpu_custom_call" | custom-call | flops 369098752 | bytes 1048576 | tf_op jit(solution)/shard_map/sums/pallas_call | solution.py:39
  36.4 0.0 copy-start.1
  36.4 0.0 copy-start.7
  36.4 1.6 %collective-permute-start.2 = (bf16[88,512]{1,0:T(8,128)(2,1)S(1)}, bf16[88,512]{1,0:T(8,128)(2,1)S(1)}, u32[]{:S(2)}, u32[]{:S(2)}) collective-permute-start(bf16[88,512]{1,0:T(8,128)(2,1)S(1)} %get-tuple-element.33.high.s0_ref), channel_id=1, source_target_pairs={{3,0},{0,1},{1,2},{2,3},{7,4},{4,5},{5,6},{6,7},{11,8},{8,9},{9,10... | collective-permute-start | bytes 270344 | tf_op jit(solution)/shard_map/ppermute | solution.py:428
  38.0 2.7 %collective-permute-start.1 = (bf16[88,512]{1,0:T(8,128)(2,1)S(1)}, bf16[88,512]{1,0:T(8,128)(2,1)S(1)}, u32[]{:S(2)}, u32[]{:S(2)}) collective-permute-start(bf16[88,512]{1,0:T(8,128)(2,1)S(1)} %get-tuple-element.33.high.s0_ref), channel_id=1, source_target_pairs={{2,0},{3,1},{0,2},{1,3},{6,4},{7,5},{4,6},{5,7},{10,8},{11,9},{8,1... | collective-permute-start | bytes 270344 | tf_op jit(solution)/shard_map/ppermute | solution.py:428
  40.7 1.4 %collective-permute-start = (bf16[88,512]{1,0:T(8,128)(2,1)S(1)}, bf16[88,512]{1,0:T(8,128)(2,1)S(1)}, u32[]{:S(2)}, u32[]{:S(2)}) collective-permute-start(bf16[88,512]{1,0:T(8,128)(2,1)S(1)} %get-tuple-element.33.high.s0_ref), channel_id=1, source_target_pairs={{1,0},{2,1},{3,2},{0,3},{5,4},{6,5},{7,6},{4,7},{9,8},{10,9},{11,1... | collective-permute-start | bytes 270344 | tf_op jit(solution)/shard_map/ppermute | solution.py:428
  42.2 5.6 %all-to-all-done.1.recv_ref = bf16[32,88,128]{2,1,0:T(8,128)(2,1)S(1)} async-done(((bf16[32,88,128]{2,1,0:T(8,128)(2,1)}), bf16[32,88,128]{2,1,0:T(8,128)(2,1)S(1)}, u32[]{:S(2)}, u32[]{:S(2)}) %all-to-all-start.1) | async-done | bytes 720928 | tf_op jit(solution)/shard_map/all_to_all | solution.py:389
  47.7 2.0 %sums.3 = (bf16[88,512]{1,0:T(8,128)(2,1)S(1)}, bf16[88,512]{1,0:T(8,128)(2,1)S(1)}, s32[32,128]{1,0:T(8,128)S(1)}) custom-call(bf16[32,88,128]{2,1,0:T(8,128)(2,1)S(1)} %all-to-all-done.1.recv_ref), custom_call_target="tpu_custom_call" | custom-call | flops 369098752 | bytes 1048576 | tf_op jit(solution)/shard_map/sums/pallas_call | solution.py:39
  49.8 0.0 copy-done.1
  49.8 0.0 copy-done.7
  49.8 0.0 copy-start
  49.8 0.0 copy-start.6
  49.8 0.9 top.1
  50.8 0.1 copy-done
  50.9 0.0 copy-done.6
  50.9 0.0 copy-start.2
  50.9 0.0 copy-start.3
  50.9 1.2 query.1
  52.1 0.0 collective-permute-done.2.s3_ref
  52.1 0.0 collective-permute-done.1.s2_ref
  52.1 0.0 collective-permute-done.s1_ref
  52.1 0.0 copy-start.10
  52.1 0.0 copy-done.2
  52.1 0.0 copy-done.3
  52.1 0.7 copy-done.10
  52.8 23.7 %attend.1 = (bf16[88,512]{1,0:T(8,128)(2,1)S(1)}, f32[88,512]{1,0:T(8,128)S(1)}, bf16[88,512]{1,0:T(8,128)(2,1)S(1)}, bf16[88,512]{1,0:T(8,128)(2,1)S(1)}, bf16[...) custom-call(s32[1]{0:T(128)} %bitcast.1.place, s32[4,16]{1,0:T(4,128)S(1)} %copy-done.10, ...), custom_call_target="tpu_custom_call" | custom-call | flops 10737418240 | bytes 1048576 | tf_op jit(solution)/shard_map/attend/pallas_call | solution.py:39
  76.5 2.3 %decoded_slots.1 = bf16[32,96,128]{2,1,0:T(8,128)(2,1)} custom-call(s32[32,128]{1,0:T(8,128)S(1)} %get-tuple-element.50.index, bf16[88,512]{1,0:T(8,128)(2,1)S(1)} %get-tuple-element.51.decoded_ref, f32[88,512]{1,0:T(8,128)S(1)} %get-tuple-element.52.enc_ref), custom_call_target="tpu_custom_call" | custom-call | flops 369098752 | bytes 1048576 | tf_op jit(solution)/shard_map/decoded_slots/pallas_call | solution.py:39
  78.8 3.9 %all-to-all-start.2 = ((bf16[32,96,128]{2,1,0:T(8,128)(2,1)}), bf16[32,96,128]{2,1,0:T(8,128)(2,1)S(1)}, u32[]{:S(2)}, u32[]{:S(2)}) async-start(bf16[32,96,128]{2,1,0:T(8,128)(2,1)} %decoded_slots.1), calls=%async_computation.2 | async-start | bytes 1572864 | tf_op jit(solution)/shard_map/all_to_all | solution.py:389
  82.7 1.6 %collective-permute-start.3 = (bf16[88,512]{1,0:T(8,128)(2,1)S(1)}, bf16[88,512]{1,0:T(8,128)(2,1)S(1)}, u32[]{:S(2)}, u32[]{:S(2)}) collective-permute-start(bf16[88,512]{1,0:T(8,128)(2,1)S(1)} %get-tuple-element.47), channel_id=1, source_target_pairs={{0,1},{1,2},{2,3},{3,0},{4,5},{5,6},{6,7},{7,4},{8,9},{9,10},{10,1... | collective-permute-start | bytes 270344 | tf_op jit(solution)/shard_map/ppermute | solution.py:431
  84.2 2.7 %collective-permute-start.4 = (bf16[88,512]{1,0:T(8,128)(2,1)S(1)}, bf16[88,512]{1,0:T(8,128)(2,1)S(1)}, u32[]{:S(2)}, u32[]{:S(2)}) collective-permute-start(bf16[88,512]{1,0:T(8,128)(2,1)S(1)} %get-tuple-element.48), channel_id=1, source_target_pairs={{0,2},{1,3},{2,0},{3,1},{4,6},{5,7},{6,4},{7,5},{8,10},{9,11},{10,... | collective-permute-start | bytes 270344 | tf_op jit(solution)/shard_map/ppermute | solution.py:431
  87.0 1.4 %collective-permute-start.5 = (bf16[88,512]{1,0:T(8,128)(2,1)S(1)}, bf16[88,512]{1,0:T(8,128)(2,1)S(1)}, u32[]{:S(2)}, u32[]{:S(2)}) collective-permute-start(bf16[88,512]{1,0:T(8,128)(2,1)S(1)} %get-tuple-element.49), channel_id=1, source_target_pairs={{0,3},{1,0},{2,1},{3,2},{4,7},{5,4},{6,5},{7,6},{8,11},{9,8},{10,9... | collective-permute-start | bytes 270344 | tf_op jit(solution)/shard_map/ppermute | solution.py:431
  88.4 0.2 collective-permute-done.3.i1_ref
  88.6 2.9 %collective-permute-done.4.i2_ref = bf16[88,512]{1,0:T(8,128)(2,1)S(1)} collective-permute-done((bf16[88,512]{1,0:T(8,128)(2,1)S(1)}, bf16[88,512]{1,0:T(8,128)(2,1)S(1)}, u32[]{:S(2)}, u32[]{:S(2)}) %collective-permute-start.4) | collective-permute-done | bytes 90144 | tf_op jit(solution)/shard_map/ppermute | solution.py:431
  91.6 0.0 collective-permute-done.5.i3_ref
  91.6 2.2 %grad_slots.1 = bf16[32,96,128]{2,1,0:T(8,128)(2,1)} custom-call(s32[32,128]{1,0:T(8,128)S(1)} %get-tuple-element.32.index, f32[88,512]{1,0:T(8,128)S(1)} %get-tuple-element.46.own_ref, bf16[88,512]{1,0:T(8,128)(2,1)S(1)} %collective-permute-done.3.i1_ref, bf16[88,512]{1,0:T(8,128)(2,1)S(1)} %collective-permute-done.4.i2_ref, ...), custom_call_target="tpu_custom_call" | custom-call | flops 369098752 | bytes 1048576 | tf_op jit(solution)/shard_map/grad_slots/pallas_call | solution.py:39
  93.8 3.5 %all-to-all-done.2.back_ref = bf16[32,96,128]{2,1,0:T(8,128)(2,1)S(1)} async-done(((bf16[32,96,128]{2,1,0:T(8,128)(2,1)}), bf16[32,96,128]{2,1,0:T(8,128)(2,1)S(1)}, u32[]{:S(2)}, u32[]{:S(2)}) %all-to-all-start.2) | async-done | bytes 786464 | tf_op jit(solution)/shard_map/all_to_all | solution.py:389
  97.2 0.1 slice_reduce_fusion
  97.3 1.7 %dynamic_update_slice.3 = bf16[32,96,128]{2,1,0:T(8,128)(2,1)} dynamic-update-slice(bf16[32,96,128]{2,1,0:T(8,128)(2,1)} %grad_slots.1, bf16[32,11,128]{2,1,0:T(8,128)(2,1)S(1)} %broadcast_in_dim.3, s32[]{:T(128)} %constant.3.clone.1, s32[]{:T(128)} %constant.10.clone.1, s32[]{:T(128)} %constant.3.clone.1) | dynamic-update-slice | bytes 180228 | tf_op jit(solution)/shard_map/dynamic_update_slice | solution.py:539
  99.0 3.9 %all-to-all-start.3 = ((bf16[32,96,128]{2,1,0:T(8,128)(2,1)}), bf16[32,96,128]{2,1,0:T(8,128)(2,1)S(1)}, u32[]{:S(2)}, u32[]{:S(2)}) async-start(bf16[32,96,128]{2,1,0:T(8,128)(2,1)} %dynamic_update_slice.3), calls=%async_computation.3 | async-start | bytes 1572864 | tf_op jit(solution)/shard_map/all_to_all | solution.py:389
  102.9 4.1 %unpack.2 = bf16[84,2048]{1,0:T(8,128)(2,1)} custom-call(bf16[32,96,128]{2,1,0:T(8,128)(2,1)S(1)} %all-to-all-done.2.back_ref, f32[2,2048]{1,0:T(2,128)S(1)} %get-tuple-element.53.route), custom_call_target="tpu_custom_call" | custom-call | flops 1476395008 | bytes 1048576 | tf_op jit(solution)/shard_map/unpack/pallas_call | solution.py:39
  107.0 10.5 %all-to-all-done.3.back_ref = bf16[32,96,128]{2,1,0:T(8,128)(2,1)S(1)} async-done(((bf16[32,96,128]{2,1,0:T(8,128)(2,1)}), bf16[32,96,128]{2,1,0:T(8,128)(2,1)S(1)}, u32[]{:S(2)}, u32[]{:S(2)}) %all-to-all-start.3) | async-done | bytes 786464 | tf_op jit(solution)/shard_map/all_to_all | solution.py:389
  117.6 1.6 %collective-permute-start.8 = (bf16[352,128]{1,0:T(8,128)(2,1)S(1)}, bf16[352,128]{1,0:T(8,128)(2,1)S(1)}, u32[]{:S(2)}, u32[]{:S(2)}) collective-permute-start(bf16[352,128]{1,0:T(8,128)(2,1)S(1)} %bitcast.7), channel_id=1, source_target_pairs={{3,0},{0,1},{1,2},{2,3},{7,4},{4,5},{5,6},{6,7},{11,8},{8,9},{9,10... | collective-permute-start | bytes 270344 | tf_op jit(solution)/shard_map/ppermute | solution.py:428
  119.1 2.7 %collective-permute-start.7 = (bf16[352,128]{1,0:T(8,128)(2,1)S(1)}, bf16[352,128]{1,0:T(8,128)(2,1)S(1)}, u32[]{:S(2)}, u32[]{:S(2)}) collective-permute-start(bf16[352,128]{1,0:T(8,128)(2,1)S(1)} %bitcast.8), channel_id=1, source_target_pairs={{2,0},{3,1},{0,2},{1,3},{6,4},{7,5},{4,6},{5,7},{10,8},{11,9},{8,1... | collective-permute-start | bytes 270344 | tf_op jit(solution)/shard_map/ppermute | solution.py:428
  121.9 1.4 %collective-permute-start.6 = (bf16[352,128]{1,0:T(8,128)(2,1)S(1)}, bf16[352,128]{1,0:T(8,128)(2,1)S(1)}, u32[]{:S(2)}, u32[]{:S(2)}) collective-permute-start(bf16[352,128]{1,0:T(8,128)(2,1)S(1)} %bitcast.9), channel_id=1, source_target_pairs={{1,0},{2,1},{3,2},{0,3},{5,4},{6,5},{7,6},{4,7},{9,8},{10,9},{11,1... | collective-permute-start | bytes 270344 | tf_op jit(solution)/shard_map/ppermute | solution.py:428
  123.3 4.2 %unpack.3 = f32[84,2048]{1,0:T(8,128)} custom-call(bf16[32,96,128]{2,1,0:T(8,128)(2,1)S(1)} %all-to-all-done.3.back_ref, f32[2,2048]{1,0:T(2,128)S(1)} %get-tuple-element.56.route), custom_call_target="tpu_custom_call" | custom-call | flops 1476395008 | bytes 1048576 | tf_op jit(solution)/shard_map/unpack/pallas_call | solution.py:39
  127.5 0.0 collective-permute-done.8.p3_ref
  127.5 0.0 collective-permute-done.7.p2_ref
  127.5 0.0 collective-permute-done.6.p1_ref
  127.5 0.7 assemble.1
  (4 shorter events, 0.1 us)
Async XLA Ops:
  0.6 1.0 copy-start.4
  1.6 0.7 copy-start.8
  7.5 8.6 %copy-start.5 = (bf16[84,2048]{1,0:T(8,128)(2,1)S(1)}, bf16[84,2048]{1,0:T(8,128)(2,1)}, u32[]{:S(2)}) copy-start(bf16[84,2048]{1,0:T(8,128)(2,1)} %x_ref.2) | copy-start | bytes 1032196
  7.5 8.6 %copy-start.9 = (s32[2048]{0:T(1024)S(1)}, s32[2048]{0:T(1024)}, u32[]{:S(2)}) copy-start(s32[2048]{0:T(1024)} %param.22) | copy-start | bytes 24580
  7.5 22.4 %all-to-all-start = ((bf16[32,88,128]{2,1,0:T(8,128)(2,1)}), bf16[32,88,128]{2,1,0:T(8,128)(2,1)S(1)}, u32[]{:S(2)}, u32[]{:S(2)}) async-start(bf16[32,88,128]{2,1,0:T(8,128)(2,1)} %get-tuple-element.31), calls=%async_computation | async-start | bytes 1441792 | tf_op jit(solution)/shard_map/all_to_all | solution.py:389
  29.9 17.8 %all-to-all-start.1 = ((bf16[32,88,128]{2,1,0:T(8,128)(2,1)}), bf16[32,88,128]{2,1,0:T(8,128)(2,1)S(1)}, u32[]{:S(2)}, u32[]{:S(2)}) async-start(bf16[32,88,128]{2,1,0:T(8,128)(2,1)} %get-tuple-element.38), calls=%async_computation.1 | async-start | bytes 1441792 | tf_op jit(solution)/shard_map/all_to_all | solution.py:389
  33.8 0.7 copy-start.11
  36.4 13.4 %copy-start.1 = (bf16[512,512]{1,0:T(8,128)(2,1)S(1)}, bf16[512,512]{1,0:T(8,128)(2,1)}, u32[]{:S(2)}) copy-start(bf16[512,512]{1,0:T(8,128)(2,1)} %output_w.1) | copy-start | bytes 1572868
  36.4 13.4 %copy-start.7 = (bf16[512,84]{0,1:T(8,128)(2,1)S(1)}, bf16[512,84]{0,1:T(8,128)(2,1)}, u32[]{:S(2)}) copy-start(bf16[512,84]{0,1:T(8,128)(2,1)} %param.20) | copy-start | bytes 258052
  36.4 15.7 %collective-permute-start.2 = (bf16[88,512]{1,0:T(8,128)(2,1)S(1)}, bf16[88,512]{1,0:T(8,128)(2,1)S(1)}, u32[]{:S(2)}, u32[]{:S(2)}) collective-permute-start(bf16[88,512]{1,0:T(8,128)(2,1)S(1)} %get-tuple-element.33.high.s0_ref), channel_id=1, source_target_pairs={{3,0},{0,1},{1,2},{2,3},{7,4},{4,5},{5,6},{6,7},{11,8},{8,9},{9,10... | collective-permute-start | bytes 270344 | tf_op jit(solution)/shard_map/ppermute | solution.py:428
  38.0 14.1 %collective-permute-start.1 = (bf16[88,512]{1,0:T(8,128)(2,1)S(1)}, bf16[88,512]{1,0:T(8,128)(2,1)S(1)}, u32[]{:S(2)}, u32[]{:S(2)}) collective-permute-start(bf16[88,512]{1,0:T(8,128)(2,1)S(1)} %get-tuple-element.33.high.s0_ref), channel_id=1, source_target_pairs={{2,0},{3,1},{0,2},{1,3},{6,4},{7,5},{4,6},{5,7},{10,8},{11,9},{8,1... | collective-permute-start | bytes 270344 | tf_op jit(solution)/shard_map/ppermute | solution.py:428
  40.7 11.4 %collective-permute-start = (bf16[88,512]{1,0:T(8,128)(2,1)S(1)}, bf16[88,512]{1,0:T(8,128)(2,1)S(1)}, u32[]{:S(2)}, u32[]{:S(2)}) collective-permute-start(bf16[88,512]{1,0:T(8,128)(2,1)S(1)} %get-tuple-element.33.high.s0_ref), channel_id=1, source_target_pairs={{1,0},{2,1},{3,2},{0,3},{5,4},{6,5},{7,6},{4,7},{9,8},{10,9},{11,1... | collective-permute-start | bytes 270344 | tf_op jit(solution)/shard_map/ppermute | solution.py:428
  49.8 1.0 copy-start
  49.8 1.0 copy-start.6
  50.9 1.3 copy-start.2
  50.9 1.3 copy-start.3
  52.1 0.7 copy-start.10
  78.8 18.5 %all-to-all-start.2 = ((bf16[32,96,128]{2,1,0:T(8,128)(2,1)}), bf16[32,96,128]{2,1,0:T(8,128)(2,1)S(1)}, u32[]{:S(2)}, u32[]{:S(2)}) async-start(bf16[32,96,128]{2,1,0:T(8,128)(2,1)} %decoded_slots.1), calls=%async_computation.2 | async-start | bytes 1572864 | tf_op jit(solution)/shard_map/all_to_all | solution.py:389
  82.7 6.0 %collective-permute-start.3 = (bf16[88,512]{1,0:T(8,128)(2,1)S(1)}, bf16[88,512]{1,0:T(8,128)(2,1)S(1)}, u32[]{:S(2)}, u32[]{:S(2)}) collective-permute-start(bf16[88,512]{1,0:T(8,128)(2,1)S(1)} %get-tuple-element.47), channel_id=1, source_target_pairs={{0,1},{1,2},{2,3},{3,0},{4,5},{5,6},{6,7},{7,4},{8,9},{9,10},{10,1... | collective-permute-start | bytes 270344 | tf_op jit(solution)/shard_map/ppermute | solution.py:431
  84.2 7.3 %collective-permute-start.4 = (bf16[88,512]{1,0:T(8,128)(2,1)S(1)}, bf16[88,512]{1,0:T(8,128)(2,1)S(1)}, u32[]{:S(2)}, u32[]{:S(2)}) collective-permute-start(bf16[88,512]{1,0:T(8,128)(2,1)S(1)} %get-tuple-element.48), channel_id=1, source_target_pairs={{0,2},{1,3},{2,0},{3,1},{4,6},{5,7},{6,4},{7,5},{8,10},{9,11},{10,... | collective-permute-start | bytes 270344 | tf_op jit(solution)/shard_map/ppermute | solution.py:431
  87.0 4.6 %collective-permute-start.5 = (bf16[88,512]{1,0:T(8,128)(2,1)S(1)}, bf16[88,512]{1,0:T(8,128)(2,1)S(1)}, u32[]{:S(2)}, u32[]{:S(2)}) collective-permute-start(bf16[88,512]{1,0:T(8,128)(2,1)S(1)} %get-tuple-element.49), channel_id=1, source_target_pairs={{0,3},{1,0},{2,1},{3,2},{4,7},{5,4},{6,5},{7,6},{8,11},{9,8},{10,9... | collective-permute-start | bytes 270344 | tf_op jit(solution)/shard_map/ppermute | solution.py:431
  99.0 18.5 %all-to-all-start.3 = ((bf16[32,96,128]{2,1,0:T(8,128)(2,1)}), bf16[32,96,128]{2,1,0:T(8,128)(2,1)S(1)}, u32[]{:S(2)}, u32[]{:S(2)}) async-start(bf16[32,96,128]{2,1,0:T(8,128)(2,1)} %dynamic_update_slice.3), calls=%async_computation.3 | async-start | bytes 1572864 | tf_op jit(solution)/shard_map/all_to_all | solution.py:389
  117.6 10.0 %collective-permute-start.8 = (bf16[352,128]{1,0:T(8,128)(2,1)S(1)}, bf16[352,128]{1,0:T(8,128)(2,1)S(1)}, u32[]{:S(2)}, u32[]{:S(2)}) collective-permute-start(bf16[352,128]{1,0:T(8,128)(2,1)S(1)} %bitcast.7), channel_id=1, source_target_pairs={{3,0},{0,1},{1,2},{2,3},{7,4},{4,5},{5,6},{6,7},{11,8},{8,9},{9,10... | collective-permute-start | bytes 270344 | tf_op jit(solution)/shard_map/ppermute | solution.py:428
  119.1 8.4 %collective-permute-start.7 = (bf16[352,128]{1,0:T(8,128)(2,1)S(1)}, bf16[352,128]{1,0:T(8,128)(2,1)S(1)}, u32[]{:S(2)}, u32[]{:S(2)}) collective-permute-start(bf16[352,128]{1,0:T(8,128)(2,1)S(1)} %bitcast.8), channel_id=1, source_target_pairs={{2,0},{3,1},{0,2},{1,3},{6,4},{7,5},{4,6},{5,7},{10,8},{11,9},{8,1... | collective-permute-start | bytes 270344 | tf_op jit(solution)/shard_map/ppermute | solution.py:428
  121.9 5.7 %collective-permute-start.6 = (bf16[352,128]{1,0:T(8,128)(2,1)S(1)}, bf16[352,128]{1,0:T(8,128)(2,1)S(1)}, u32[]{:S(2)}, u32[]{:S(2)}) collective-permute-start(bf16[352,128]{1,0:T(8,128)(2,1)S(1)} %bitcast.9), channel_id=1, source_target_pairs={{1,0},{2,1},{3,2},{0,3},{5,4},{6,5},{7,6},{4,7},{9,8},{10,9},{11,1... | collective-permute-start | bytes 270344 | tf_op jit(solution)/shard_map/ppermute | solution.py:428
